TPU v7x, 256 devices: a whole 4x4x8 slice. The times are simulated.
256 devices in a mesh: dp: 8 (over z_hi, core), tensor: 32 (over x, z_lo, y).
Axes of the slice: x: 4, y: 4, z: 8 (z_hi: 4, z_lo: 2; z = z_hi * 2 + z_lo), core: 2. Of those that a mesh axis runs over, the one named last changes fastest.
Arguments:
- d_out: bfloat16 [1024, 8192], P('dp', 'tensor'), may hold values from -6 to 6
- gate_act: bfloat16 [1024, 14336], P('dp', 'tensor'), may hold values from -6 to 6
- up_act: bfloat16 [1024, 14336], P('dp', 'tensor'), may hold values from -6 to 6
- gate_weight: bfloat16 [8192, 14336], P('dp', 'tensor'), may hold values from -0.0625 to 0.0625
- up_weight: bfloat16 [8192, 14336], P('dp', 'tensor'), may hold values from -0.0625 to 0.0625
- down_weight: bfloat16 [8192, 14336], P('dp', 'tensor'), may hold values from -0.046875 to 0.046875
- momentum: float32 [8192, 14336], P('dp', 'tensor'), may hold values from -12 to 12
Outputs:
- d_in: bfloat16 [1024, 8192], P('tensor', 'dp')
- direction: bfloat16 [8192, 14336], P('dp', 'tensor')
- new_momentum: float32 [8192, 14336], P('dp', 'tensor')
All inputs are finite; a program needn't handle non-finite values.
Results may differ from a plain program's by a relative error of at most 0.0049.
Values may be sent and summed in bfloat16 or wider, within the bound.
No kernel may reach another device: no remote copies, remote signals or barrier semaphores. Data moves between devices by JAX's collectives and lax.ppermute only.
A program may use at most 128 MiB of HBM per device.

v0:
```python
import jax
import jax.numpy as jnp
from jax import lax
from jax.sharding import PartitionSpec as P


def owned_blocks(full_out):
    return lax.all_to_all(full_out, "dp", split_axis=1, concat_axis=0, tiled=True)


def body(d_out, gate_act, up_act, gate_weight, up_weight, down_weight, momentum):
    groups = lax.axis_size("dp")
    full_out = lax.all_gather(d_out, "tensor", axis=1, tiled=True)
    gate_full = gate_act.astype(jnp.float32)
    up_full = up_act.astype(jnp.float32)
    sigma = jax.nn.sigmoid(gate_full)
    swish = gate_full * sigma
    hidden = (swish * up_full).astype(jnp.bfloat16)
    grad_sum = lax.psum_scatter(
        lax.dot_general(
            full_out, hidden, (((0,), (0,)), ((), ())), preferred_element_type=jnp.float32
        ),
        "dp",
        scatter_dimension=0,
        tiled=True,
    )
    grad_mean = grad_sum / groups
    direction = (0.9 * momentum + 0.1 * grad_mean).astype(jnp.bfloat16)
    new_momentum = 0.99 * momentum + 0.01 * grad_mean
    exchanged = owned_blocks(full_out)
    d_hidden = lax.psum_scatter(
        jnp.dot(exchanged, down_weight, preferred_element_type=jnp.float32),
        "dp",
        scatter_dimension=0,
        tiled=True,
    )
    d_up = (d_hidden * swish).astype(jnp.bfloat16)
    d_gate = (d_hidden * up_full * sigma * (1.0 + gate_full * (1.0 - sigma))).astype(jnp.bfloat16)
    all_gate, all_up = (
        lax.all_gather(d_gate, "dp", axis=0, tiled=True),
        lax.all_gather(d_up, "dp", axis=0, tiled=True),
    )
    first = lax.dot_general(
        all_gate, gate_weight, (((1,), (1,)), ((), ())), preferred_element_type=jnp.float32
    )
    second = lax.dot_general(
        all_up, up_weight, (((1,), (1,)), ((), ())), preferred_element_type=jnp.float32
    )
    d_in = lax.psum_scatter(first + second, "tensor", scatter_dimension=0, tiled=True).astype(
        jnp.bfloat16
    )
    return (d_in, direction, new_momentum)


def solution(mesh):
    return jax.shard_map(
        body,
        mesh=mesh,
        in_specs=(
            P("dp", "tensor"),
            P("dp", "tensor"),
            P("dp", "tensor"),
            P("dp", "tensor"),
            P("dp", "tensor"),
            P("dp", "tensor"),
            P("dp", "tensor"),
        ),
        out_specs=(P("tensor", "dp"), P("dp", "tensor"), P("dp", "tensor")),
        check_vma=False,
    )
```

profile of v0, /device:TPU:3, one launch (start us, length us, event | category | flops | bytes accessed | tf_op | source)
XLA Modules:
  0.0 648.3 jit_solution(8924635378281521359)
XLA Ops:
  7.2 0.0 all-gather.2.cloned.1.call-start
  7.2 1.6 copy.10
  8.9 0.0 all-gather.2.cloned.1.call-update
  8.9 0.0 reduce-scatter.4.cloned.1.call-start
  8.9 130.9 %all-gather.2.cloned.1.call-done = bf16[128,8192]{0,1:T(8,128)(2,1)} async-done(((bf16[128,256]{0,1:T(8,128)(2,1)}), bf16[128,8192]{0,1:T(8,128)(2,1)}) %all-gather.2.cloned.1.call-update) | async-done | bytes 2097168 | tf_op jit(solution)/shard_map/all_gather | solution.py:13
  139.9 71.9 %all_to_all.19 = bf16[128,8,1024]{0,2,1:T(8,128)(2,1)S(1)} all-to-all(bf16[128,8,1024]{0,2,1:T(8,128)(2,1)} %bitcast.12), channel_id=1, replica_groups=mesh['dp'=8,'tensor'=32] {'dp'}, dimensions={1} | all-to-all | bytes 4194304 | tf_op jit(solution)/shard_map/all_to_all | solution.py:8
  211.7 2.6 copy.11
  214.3 4.2 fusion.10
  218.6 0.0 reduce-scatter.4.cloned.1.call-update
  218.6 0.0 reduce-scatter.6.cloned.1.call-start
  218.6 48.1 %reduce-scatter.4.cloned.1.call-done = f32[128,448]{0,1:T(8,128)} async-done(((f32[1024,448]{0,1:T(8,128)}), f32[128,448]{0,1:T(8,128)}) %reduce-scatter.4.cloned.1.call-update) | async-done | bytes 229392 | tf_op jit(solution)/shard_map/reduce_scatter | solution.py:31
  266.7 1.1 multiply_convert_fusion
  267.8 22.6 %all_gather.11 = bf16[1024,448]{0,1:T(8,128)(2,1)S(1)} all-gather(bf16[128,448]{0,1:T(8,128)(2,1)S(1)} %get-tuple-element.5), channel_id=1, replica_groups=mesh['dp'=8,'tensor'=32] {'dp'}, dimensions={0}, use_global_device_ids=true | all-gather | bytes 1032192 | tf_op jit(solution)/shard_map/all_gather | solution.py:41
  290.4 21.4 %all_gather.10 = bf16[1024,448]{0,1:T(8,128)(2,1)S(1)} all-gather(bf16[128,448]{0,1:T(8,128)(2,1)S(1)} %get-tuple-element.6), channel_id=1, replica_groups=mesh['dp'=8,'tensor'=32] {'dp'}, dimensions={0}, use_global_device_ids=true | all-gather | bytes 1032192 | tf_op jit(solution)/shard_map/all_gather | solution.py:40
  311.8 1.3 fusion.11
  313.1 3.3 convolution_add_fusion
  316.4 0.0 reduce-scatter.6.cloned.1.call-update
  316.4 0.0 reduce-scatter.8.cloned.1.call-start
  316.5 1.5 copy-done.1
  318.0 7.3 %convolution_bitcast_fusion = f32[8192,448]{0,1:T(8,128)} fusion(bf16[128,8192]{0,1:T(8,128)(2,1)S(1)} %copy-done.1, bf16[128,448]{0,1:T(8,128)(2,1)S(1)} %copy-done.5, bf16[128,448]{0,1:T(8,128)(2,1)S(1)} %copy-done.4), kind=kOutput, calls=%fused_computation | convolution fusion | flops 939982848 | bytes 17006592 | tf_op jit(solution)/shard_map/dot_general | solution.py:20
  325.3 123.3 %reduce-scatter.6.cloned.1.call-done = f32[32,1024]{1,0:T(8,128)} async-done(((f32[1024,1024]{1,0:T(8,128)}), f32[32,1024]{1,0:T(8,128)}) %reduce-scatter.6.cloned.1.call-update) | async-done | bytes 131088 | tf_op jit(solution)/shard_map/reduce_scatter | solution.py:49
  448.6 1.5 convert_element_type.25
  450.1 188.1 %reduce-scatter.8.cloned.1.call-done = f32[1024,448]{0,1:T(8,128)} async-done(((f32[8192,448]{0,1:T(8,128)}), f32[1024,448]{0,1:T(8,128)}) %reduce-scatter.8.cloned.1.call-update) | async-done | bytes 1835024 | tf_op jit(solution)/shard_map/reduce_scatter | solution.py:19
  638.3 3.5 multiply_add_fusion
  (12 shorter events, 0.0 us)
Async XLA Ops:
  7.2 304.6 %copy-start = (bf16[1024,448]{0,1:T(8,128)(2,1)S(1)}, bf16[1024,448]{0,1:T(8,128)(2,1)}, u32[]{:S(2)}) copy-start(bf16[1024,448]{0,1:T(8,128)(2,1)} %param.10) | copy-start | bytes 2752516
  7.2 132.7 %all-gather.2.cloned.1.call-start = ((), (), s32[]{:S(2)}) async-start(), calls=%async_computation.4 | async-start | bytes 2162688 | tf_op jit(solution)/shard_map/all_gather | solution.py:13
  8.9 257.8 %reduce-scatter.4.cloned.1.call-start = ((), (), s32[]{:S(2)}) async-start(), calls=%async_computation.5 | async-start | bytes 2064384 | tf_op jit(solution)/shard_map/reduce_scatter | solution.py:31
  214.3 52.4 %copy-start.4 = (bf16[128,448]{0,1:T(8,128)(2,1)S(1)}, bf16[128,448]{0,1:T(8,128)(2,1)}, u32[]{:S(2)}) copy-start(bf16[128,448]{0,1:T(8,128)(2,1)} %param.8) | copy-start | bytes 344068
  214.3 52.4 %copy-start.5 = (bf16[128,448]{0,1:T(8,128)(2,1)S(1)}, bf16[128,448]{0,1:T(8,128)(2,1)}, u32[]{:S(2)}) copy-start(bf16[128,448]{0,1:T(8,128)(2,1)} %param.9) | copy-start | bytes 344068
  218.6 230.0 %reduce-scatter.6.cloned.1.call-start = ((), (), s32[]{:S(2)}) async-start(), calls=%async_computation.6 | async-start | bytes 4325376 | tf_op jit(solution)/shard_map/reduce_scatter | solution.py:49
  311.8 1.3 copy-start.3
  316.4 1.6 copy-start.1
  316.4 321.8 %reduce-scatter.8.cloned.1.call-start = ((), (), s32[]{:S(2)}) async-start(), calls=%async_computation.7 | async-start | bytes 16515072 | tf_op jit(solution)/shard_map/reduce_scatter | solution.py:19
  325.3 313.0 %copy-start.2 = (f32[1024,448]{0,1:T(8,128)S(1)}, f32[1024,448]{0,1:T(8,128)}, u32[]{:S(2)}) copy-start(f32[1024,448]{0,1:T(8,128)} %param.13) | copy-start | bytes 5505028
Sparse Core Ops, SparseCore 0:
  10.4 129.4 all-gather.1
  218.7 47.9 reduce-scatter.3
  316.6 131.9 reduce-scatter.5
  451.0 187.2 reduce-scatter.7
where the time goes:
time: 651 us; the launch traced here: 648 us
  waiting for transfers between devices  490 us (75%)
  blocking collectives  116 us (18%)
  matrix products  16.1 us (2%)
  between operations  13.8 us (2%)
    reduce_scatter x1, waiting for transfers between devices, body(): lax.psum_scatter(lax.dot_general(full_out, hidden, (((0,), (0,)), ((), ()...  188 us
    all_gather x1, waiting for transfers between devices, body(): full_out = lax.all_gather(d_out, 'tensor', axis=1, tiled=True)  131 us
    reduce_scatter x1, waiting for transfers between devices, body(): lax.psum_scatter(first + second, 'tensor', scatter_dimension=0, tiled=True)  123 us
    all_to_all x1, blocking collectives, owned_blocks(): lax.all_to_all(full_out, 'dp', split_axis=1, concat_axis=0, tiled=True)  71.9 us
    reduce_scatter x1, waiting for transfers between devices, body(): lax.psum_scatter(jnp.dot(exchanged, down_weight, preferred_element_type=j...  48.1 us
    all_gather x1, blocking collectives, body(): lax.all_gather(d_up, 'dp', axis=0, tiled=True)  22.6 us
    all_gather x1, blocking collectives, body(): lax.all_gather(d_gate, 'dp', axis=0, tiled=True)  21.4 us
  transfers between devices with their start and end apart: 4, of which 4 were waited for; matrix products, arithmetic and copies ran while one was open for 1% of the time, Pallas kernels for 0%

commit v1 on v0

v1 whole, which is shorter than its diff:
```python
import jax
import jax.numpy as jnp
import numpy as np
from jax import lax
from jax.sharding import Mesh, PartitionSpec as P

AXES = ("zh", "co", "x", "zl", "y")
SIZES = (4, 2, 4, 2, 4)
DP = ("zh", "co")
TENSOR = ("x", "zl", "y")


def pairs(move):
    found = []
    for source in range(256):
        place = [int(v) for v in np.unravel_index(source, SIZES)]
        found.append((source, int(np.ravel_multi_index(move(*place), SIZES))))
    return found


TRANSPOSE = pairs(lambda zh, co, x, zl, y: (x, zl, zh, co, y))


def body(d_out, gate_act, up_act, gate_weight, up_weight, down_weight, momentum):
    turned = lax.ppermute(d_out, AXES, TRANSPOSE)
    spread = jnp.broadcast_to(turned[None], (32, 128, 256))
    slots = lax.all_to_all(spread, TENSOR, split_axis=0, concat_axis=0, tiled=True)
    exchanged = slots.reshape(8, 4, 128, 256).transpose(0, 2, 1, 3).reshape(1024, 1024)
    all_gate = lax.all_gather(gate_act, DP, axis=0, tiled=True).astype(jnp.float32)
    all_up = lax.all_gather(up_act, DP, axis=0, tiled=True).astype(jnp.float32)
    sigma = jax.nn.sigmoid(all_gate)
    swish = all_gate * sigma
    hidden = (swish * all_up).astype(jnp.bfloat16)

    partial = jnp.dot(exchanged, down_weight, preferred_element_type=jnp.float32)
    parts = lax.all_to_all(
        partial.astype(jnp.bfloat16).reshape(8, 128, 448), DP, split_axis=0, concat_axis=0, tiled=True
    )
    mine = jnp.sum(parts.astype(jnp.float32), axis=0).astype(jnp.bfloat16)
    d_hidden = lax.all_gather(mine, DP, axis=0, tiled=True).astype(jnp.float32)
    d_up = (d_hidden * swish).astype(jnp.bfloat16)
    d_gate = (d_hidden * all_up * sigma * (1.0 + all_gate * (1.0 - sigma))).astype(jnp.bfloat16)
    first = lax.dot_general(
        d_gate, gate_weight, (((1,), (1,)), ((), ())), preferred_element_type=jnp.float32
    )
    second = lax.dot_general(
        d_up, up_weight, (((1,), (1,)), ((), ())), preferred_element_type=jnp.float32
    )
    slices = lax.all_to_all(
        (first + second).astype(jnp.bfloat16).reshape(32, 32, 1024),
        TENSOR,
        split_axis=0,
        concat_axis=0,
        tiled=True,
    )
    d_in = jnp.sum(slices.astype(jnp.float32), axis=0).astype(jnp.bfloat16)

    grad_sum = lax.dot_general(
        exchanged, hidden, (((0,), (0,)), ((), ())), preferred_element_type=jnp.float32
    )
    grad_mean = grad_sum / 8
    direction = (0.9 * momentum + 0.1 * grad_mean).astype(jnp.bfloat16)
    new_momentum = 0.99 * momentum + 0.01 * grad_mean
    return d_in, direction, new_momentum


def solution(mesh):
    fine = Mesh(mesh.devices.reshape(SIZES), AXES)
    both = P(DP, TENSOR)
    return jax.shard_map(
        body,
        mesh=fine,
        in_specs=(both,) * 7,
        out_specs=(P(TENSOR, DP), both, both),
        check_vma=False,
    )
```

time: 651 us -> 190 us (0.29)
  waiting for transfers between devices: 490 us -> 25.7 us
  starting transfers between devices: 0.16 us -> 23.8 us
  between operations: 13.8 us -> 0.71 us
    reduce_scatter x3 -> x0, waiting for transfers between devices: 359 us -> none  [the longest x1 188 us: body(): lax.psum_scatter(lax.dot_general(full_out, hidden, (((0,), (0,)), ((), ()...]
    all_gather x1 -> x0, waiting for transfers between devices: 131 us -> none  [body(): full_out = lax.all_gather(d_out, 'tensor', axis=1, tiled=True)]
    all_gather x2 -> x3, blocking collectives: 44 us -> 82.3 us  [the longest x1 40.5 us: body(): lax.all_gather(gate_act, DP, axis=0, tiled=True).astype(jnp.float32)]
    all_to_all x1, blocking collectives: 71.9 us -> 37.4 us  [body(): lax.all_to_all(spread, TENSOR, split_axis=0, concat_axis=0, tiled=True)]
    all_to_all x0 -> x2, waiting for transfers between devices: none -> 23.3 us  [the longest x1 23.3 us: body(): lax.all_to_all((first + second).astype(jnp.bfloat16).reshape(32, 32, 1024...]
    all_to_all x0 -> x2, starting transfers between devices: none -> 16.9 us  [the longest x1 10.5 us: body(): lax.all_to_all((first + second).astype(jnp.bfloat16).reshape(32, 32, 1024...]
    ppermute x0 -> x1, starting transfers between devices: none -> 6.92 us  [body(): turned = lax.ppermute(d_out, AXES, TRANSPOSE)]
  transfers between devices with their start and end apart: 4 -> 3, of which waited for: 4 -> 2; matrix products, arithmetic and copies ran while one was open for 1% -> 3% of each run, Pallas kernels for 0% -> 0%
where the time goes in v1:
time: 190 us
  blocking collectives  120 us (63%)
  waiting for transfers between devices  25.7 us (14%)
  starting transfers between devices  23.8 us (13%)
  matrix products  14.6 us (8%)
  local copies, waits for them, and re-layouts  3.9 us (2%)
    all_gather x1, blocking collectives, body(): lax.all_gather(gate_act, DP, axis=0, tiled=True).astype(jnp.float32)  40.5 us
    all_to_all x1, blocking collectives, body(): lax.all_to_all(spread, TENSOR, split_axis=0, concat_axis=0, tiled=True)  37.4 us
    all_to_all x1, waiting for transfers between devices, body(): lax.all_to_all((first + second).astype(jnp.bfloat16).reshape(32, 32, 1024...  23.3 us
    all_gather x1, blocking collectives, body(): all_up = lax.all_gather(up_act, DP, axis=0, tiled=True).astype(jnp.float32)  21.1 us
    all_gather x1, blocking collectives, body(): d_hidden = lax.all_gather(mine, DP, axis=0, tiled=True).astype(jnp.float32)  20.7 us
    all_to_all x1, starting transfers between devices, body(): lax.all_to_all((first + second).astype(jnp.bfloat16).reshape(32, 32, 1024...  10.5 us
    ppermute x1, starting transfers between devices, body(): turned = lax.ppermute(d_out, AXES, TRANSPOSE)  6.92 us
    all_to_all x1, starting transfers between devices, body(): lax.all_to_all(partial.astype(jnp.bfloat16).reshape(8, 128, 448), DP, spl...  6.37 us
  transfers between devices with their start and end apart: 3, of which 2 were waited for; matrix products, arithmetic and copies ran while one was open for 3% of the time, Pallas kernels for 0%

profile of v1, /device:TPU:3, one launch (start us, length us, event | category | flops | bytes accessed | tf_op | source)
XLA Modules:
  0.0 189.6 jit_solution(16493318641237550065)
XLA Ops:
  0.6 0.0 copy-start
  0.6 6.9 %collective-permute-start = (bf16[128,256]{1,0:T(8,128)(2,1)}, bf16[128,256]{1,0:T(8,128)(2,1)S(1)}, u32[]{:S(2)}, u32[]{:S(2)}) collective-permute-start(bf16[128,256]{1,0:T(8,128)(2,1)} %param.7), channel_id=1, source_target_pairs={{0,0},{1,1},{2,2},{3,3},{4,32},{5,33},{6,34},{7,35},{8,64},{9,65},... | collective-permute-start | bytes 196616 | tf_op jit(solution)/shard_map/ppermute | solution.py:25
  7.6 2.4 %collective-permute-done = bf16[128,256]{1,0:T(8,128)(2,1)S(1)} collective-permute-done((bf16[128,256]{1,0:T(8,128)(2,1)}, bf16[128,256]{1,0:T(8,128)(2,1)S(1)}, u32[]{:S(2)}, u32[]{:S(2)}) %collective-permute-start) | collective-permute-done | bytes 65568 | tf_op jit(solution)/shard_map/ppermute | solution.py:25
  10.0 0.2 broadcast_in_dim.2
  10.2 37.4 %all_to_all.15 = bf16[32,128,256]{2,1,0:T(8,128)(2,1)S(1)} all-to-all(bf16[32,128,256]{2,1,0:T(8,128)(2,1)S(1)} %broadcast_in_dim.2), channel_id=1, replica_groups=mesh['zh'=4,'co'=2,'x'=4,'zl'=2,'y'=4] {'x','zl','y'}, dimensions={0} | all-to-all | bytes 4194304 | tf_op jit(solution)/shard_map/all_to_all | solution.py:27
  47.6 2.6 %copy.11 = bf16[8,128,4,256]{1,0,3,2:T(8,128)(2,1)} copy(bf16[8,128,4,256]{3,1,2,0:T(8,128)(2,1)S(1)} %bitcast.33) | data formatting | bytes 4194304 | tf_op jit(solution)/shard_map/transpose | solution.py:28
  50.2 3.0 %fusion.19 = bf16[56,8,8,128]{3,2,1,0:T(8,128)(2,1)S(1)} fusion(bf16[1024,448]{0,1:T(8,128)(2,1)} %param.12, bf16[128,8,8,128]{3,2,1,0:T(8,128)(2,1)} %bitcast.34), kind=kOutput, calls=%fused_computation.26 | convolution fusion | flops 939982848 | bytes 3932160 | tf_op jit(solution)/shard_map/dot_general | solution.py:35
  53.2 0.0 copy-start.2
  53.2 1.1 copy.30
  54.3 6.4 %all-to-all-start.1 = ((bf16[8,128,448]{1,2,0:T(8,128)(2,1)}), bf16[8,128,448]{1,2,0:T(8,128)(2,1)S(1)}, u32[]{:S(2)}, u32[]{:S(2)}) async-start(bf16[8,128,448]{1,2,0:T(8,128)(2,1)} %bitcast.32), calls=%async_computation.1 | async-start | bytes 1835008 | tf_op jit(solution)/shard_map/all_to_all | solution.py:36
  60.7 0.0 copy-done.2
  60.7 40.5 %all_gather.11 = bf16[1024,448]{0,1:T(8,128)(2,1)S(1)} all-gather(bf16[128,448]{0,1:T(8,128)(2,1)S(1)} %copy-done.2), channel_id=1, replica_groups=mesh['zh'=4,'co'=2,'x'=4,'zl'=2,'y'=4] {'zh','co'}, dimensions={0}, use_global_device_ids=true | all-gather | bytes 1032192 | tf_op jit(solution)/shard_map/all_gather | solution.py:29
  101.2 0.0 copy-done.3
  101.2 21.1 %all_gather.10 = bf16[1024,448]{0,1:T(8,128)(2,1)} all-gather(bf16[128,448]{0,1:T(8,128)(2,1)S(1)} %copy-done.3), channel_id=1, replica_groups=mesh['zh'=4,'co'=2,'x'=4,'zl'=2,'y'=4] {'zh','co'}, dimensions={0}, use_global_device_ids=true | all-gather | bytes 1032192 | tf_op jit(solution)/shard_map/all_gather | solution.py:30
  122.3 0.0 all-to-all-done.1
  122.3 0.1 reduce_sum.24
  122.4 20.7 %all_gather.9 = bf16[1024,448]{0,1:T(8,128)(2,1)S(1)} all-gather(bf16[128,448]{0,1:T(8,128)(2,1)S(1)} %reduce_sum.24), channel_id=1, replica_groups=mesh['zh'=4,'co'=2,'x'=4,'zl'=2,'y'=4] {'zh','co'}, dimensions={0}, use_global_device_ids=true | all-gather | bytes 1032192 | tf_op jit(solution)/shard_map/all_gather | solution.py:40
  143.1 0.0 copy-done
  143.1 3.0 %fusion.22 = f32[1024,1024]{1,0:T(8,128)S(1)} fusion(bf16[1024,448]{0,1:T(8,128)(2,1)S(1)} %copy-done, bf16[1024,448]{0,1:T(8,128)(2,1)} %all_gather.10, bf16[1024,448]{0,1:T(8,128)(2,1)S(1)} %all_gather.9, bf16[1024,448]{0,1:T(8,128)(2,1)S(1)} %all_gather.11), kind=kOutput, calls=%fused_computation.27 | convolution fusion | flops 945487872 | bytes 7864320 | tf_op jit(solution)/shard_map/dot_general | solution.py:43
  146.1 2.8 %add_convert_fusion = bf16[1024,1024]{1,0:T(8,128)(2,1)} fusion(f32[1024,1024]{1,0:T(8,128)S(1)} %fusion.22, bf16[1024,448]{0,1:T(8,128)(2,1)S(1)} %copy-done.4, bf16[1024,448]{0,1:T(8,128)(2,1)S(1)} %all_gather.9, bf16[1024,448]{0,1:T(8,128)(2,1)S(1)} %all_gather.11), kind=kOutput, calls=%fused_computation | convolution fusion | flops 945291264 | bytes 9043968 | tf_op jit(solution)/shard_map/dot_general | solution.py:46
  148.9 10.5 %all-to-all-start.2 = ((bf16[32,32,1024]{2,1,0:T(8,128)(2,1)}), bf16[32,32,1024]{2,1,0:T(8,128)(2,1)S(1)}, u32[]{:S(2)}, u32[]{:S(2)}) async-start(bf16[32,32,1024]{2,1,0:T(8,128)(2,1)} %bitcast.36), calls=%async_computation.2 | async-start | bytes 4194304 | tf_op jit(solution)/shard_map/all_to_all | solution.py:49
  159.4 5.9 %bitcast_add_fusion = (f32[1024,448]{0,1:T(8,128)}, bf16[1024,448]{0,1:T(8,128)(2,1)}) fusion(f32[1024,448]{0,1:T(8,128)} %param.13, bf16[128,8,8,128]{3,2,1,0:T(8,128)(2,1)} %bitcast.35, bf16[1024,448]{0,1:T(8,128)(2,1)} %all_gather.10, bf16[1024,448]{0,1:T(8,128)(2,1)} %copy-done.1), kind=kOutput, calls=%fused_computation.22 | convolution fusion | flops 946405376 | bytes 8519680 | tf_op jit(solution)/shard_map/dot_general | solution.py:58
  165.3 23.3 %all-to-all-done.2 = bf16[32,32,1024]{2,1,0:T(8,128)(2,1)S(1)} async-done(((bf16[32,32,1024]{2,1,0:T(8,128)(2,1)}), bf16[32,32,1024]{2,1,0:T(8,128)(2,1)S(1)}, u32[]{:S(2)}, u32[]{:S(2)}) %all-to-all-start.2) | async-done | bytes 2097184 | tf_op jit(solution)/shard_map/all_to_all | solution.py:49
  188.6 1.0 reduce_sum.25
  (5 shorter events, 0.0 us)
Async XLA Ops:
  0.6 142.5 %copy-start = (bf16[1024,448]{0,1:T(8,128)(2,1)S(1)}, bf16[1024,448]{0,1:T(8,128)(2,1)}, u32[]{:S(2)}) copy-start(bf16[1024,448]{0,1:T(8,128)(2,1)} %param.10) | copy-start | bytes 2752516
  0.6 9.3 %collective-permute-start = (bf16[128,256]{1,0:T(8,128)(2,1)}, bf16[128,256]{1,0:T(8,128)(2,1)S(1)}, u32[]{:S(2)}, u32[]{:S(2)}) collective-permute-start(bf16[128,256]{1,0:T(8,128)(2,1)} %param.7), channel_id=1, source_target_pairs={{0,0},{1,1},{2,2},{3,3},{4,32},{5,33},{6,34},{7,35},{8,64},{9,65},... | collective-permute-start | bytes 196616 | tf_op jit(solution)/shard_map/ppermute | solution.py:25
  53.2 7.5 %copy-start.2 = (bf16[128,448]{0,1:T(8,128)(2,1)S(1)}, bf16[128,448]{0,1:T(8,128)(2,1)}, u32[]{:S(2)}) copy-start(bf16[128,448]{0,1:T(8,128)(2,1)} %param.8) | copy-start | bytes 344068
  54.3 46.9 %copy-start.3 = (bf16[128,448]{0,1:T(8,128)(2,1)S(1)}, bf16[128,448]{0,1:T(8,128)(2,1)}, u32[]{:S(2)}) copy-start(bf16[128,448]{0,1:T(8,128)(2,1)} %param.9) | copy-start | bytes 344068
  54.3 68.0 %all-to-all-start.1 = ((bf16[8,128,448]{1,2,0:T(8,128)(2,1)}), bf16[8,128,448]{1,2,0:T(8,128)(2,1)S(1)}, u32[]{:S(2)}, u32[]{:S(2)}) async-start(bf16[8,128,448]{1,2,0:T(8,128)(2,1)} %bitcast.32), calls=%async_computation.1 | async-start | bytes 1835008 | tf_op jit(solution)/shard_map/all_to_all | solution.py:36
  101.2 44.9 %copy-start.1 = (bf16[1024,448]{0,1:T(8,128)(2,1)}, bf16[1024,448]{0,1:T(8,128)(2,1)S(1)}, u32[]{:S(2)}) copy-start(bf16[1024,448]{0,1:T(8,128)(2,1)S(1)} %all_gather.11) | copy-start | bytes 2752516
  143.1 3.0 %copy-start.4 = (bf16[1024,448]{0,1:T(8,128)(2,1)S(1)}, bf16[1024,448]{0,1:T(8,128)(2,1)}, u32[]{:S(2)}) copy-start(bf16[1024,448]{0,1:T(8,128)(2,1)} %param.11) | copy-start | bytes 2752516
  148.9 39.7 %all-to-all-start.2 = ((bf16[32,32,1024]{2,1,0:T(8,128)(2,1)}), bf16[32,32,1024]{2,1,0:T(8,128)(2,1)S(1)}, u32[]{:S(2)}, u32[]{:S(2)}) async-start(bf16[32,32,1024]{2,1,0:T(8,128)(2,1)} %bitcast.36), calls=%async_computation.2 | async-start | bytes 4194304 | tf_op jit(solution)/shard_map/all_to_all | solution.py:49

commit v2 on v1

v2 whole, which is shorter than its diff:
```python
import jax
import jax.numpy as jnp
import numpy as np
from jax import lax
from jax.experimental import pallas as pl
from jax.experimental.pallas import tpu as pltpu
from jax.sharding import Mesh, PartitionSpec as P

AXES = ("zh", "co", "x", "zl", "y")
SIZES = (4, 2, 4, 2, 4)
DP = ("zh", "co")
TENSOR = ("x", "zl", "y")
CUTS = 1
PART = 128 // CUTS
ROWS = 32 // CUTS
HALF = 224
F32, BF16 = jnp.float32, jnp.bfloat16
PLACE = pl.BlockSpec(memory_space=pltpu.SMEM)
WHOLE = pl.BlockSpec(memory_space=pltpu.VMEM)
LIMIT = 16 * 1024 * 1024


def pairs(move):
    found = []
    for source in range(256):
        place = [int(v) for v in np.unravel_index(source, SIZES)]
        found.append((source, int(np.ravel_multi_index(move(*place), SIZES))))
    return found


TRANSPOSE = pairs(lambda zh, co, x, zl, y: (x, zl, zh, co, y))
OTHER_CORE = pairs(lambda zh, co, x, zl, y: (zh, 1 - co, x, zl, y))
NEXT_CHIP = pairs(lambda zh, co, x, zl, y: (zh, co, x, 1 - zl, y))
ALONG = [None] + [
    pairs(lambda zh, co, x, zl, y, k=k: ((zh + k) % 4, co, x, zl, y)) for k in (1, 2, 3)
]


def shape(*dims, kind=F32):
    return jax.ShapeDtypeStruct(dims, kind)


def call(kernel, out_shape, operands, scratch=(), cost=None):
    return pl.pallas_call(
        kernel,
        out_shape=out_shape,
        in_specs=[PLACE] + [WHOLE] * (len(operands) - 1),
        out_specs=jax.tree.map(lambda _: WHOLE, out_shape),
        scratch_shapes=list(scratch),
        compiler_params=pltpu.CompilerParams(vmem_limit_bytes=LIMIT),
        cost_estimate=cost,
    )(*operands)


def product_kernel(place, slots, weight, keep, give):
    core = place[1]
    right = jnp.concatenate([slots[0, y].reshape(2 * PART, 256) for y in range(4)], axis=1)
    for which, out in ((core, keep), (1 - core, give)):
        left = weight[pl.ds(pl.multiple_of(which * HALF, 32), HALF), :]
        out[0] = lax.dot_general(
            left, right, (((1,), (1,)), ((), ())), preferred_element_type=F32
        )


def first_product(place, slots, weight):
    part = pl.BlockSpec((1, HALF, 2 * PART), lambda zh: (zh, 0, 0))
    return pl.pallas_call(
        product_kernel,
        grid=(4,),
        out_shape=(shape(4, HALF, 2 * PART),) * 2,
        in_specs=[
            PLACE,
            pl.BlockSpec((1, 4, 2, PART, 256), lambda zh: (zh, 0, 0, 0, 0)),
            pl.BlockSpec((448, 1024), lambda zh: (0, 0)),
        ],
        out_specs=[part, part],
        compiler_params=pltpu.CompilerParams(vmem_limit_bytes=LIMIT),
    )(place, slots, weight)


def split_kernel(place, keep, got, own, one, two, three):
    zh = place[0]
    own[...] = keep[zh] + got[zh]
    for k, out in ((1, one), (2, two), (3, three)):
        to = lax.rem(zh + k, 4)
        out[...] = (keep[to] + got[to]).astype(BF16)


def factor_kernel(place, mine, other, hidden, by_gate, by_up):
    zh, core = place[0], place[1]
    for k in range(4):
        group = lax.rem(zh + 4 - k, 4)
        first = jnp.where(core == 0, mine[k], other[k])
        second = jnp.where(core == 0, other[k], mine[k])
        for cut in range(CUTS):
            lanes = slice(cut * PART, (cut + 1) * PART)
            both = jnp.concatenate([first[:, :, lanes], second[:, :, lanes]], axis=2)
            for half in range(2):
                units = slice(half * HALF, (half + 1) * HALF)
                gate, up = both[0, units].astype(F32), both[1, units].astype(F32)
                sigma = jax.nn.sigmoid(gate)
                swish = gate * sigma
                hidden[cut, group, units] = (swish * up).astype(BF16)

                @pl.when(core == half)
                def _():
                    by_up[cut, group] = swish
                    by_gate[cut, group] = up * sigma * (1.0 + gate * (1.0 - sigma))


def back_kernel(place, mine, by_gate, by_up, out):
    zh = place[0]
    for k in range(4):
        group = lax.rem(zh + 4 - k, 4)
        block = mine[k].astype(F32)
        both = jnp.concatenate([block * by_gate[group], block * by_up[group]], axis=0)
        out[group, :, :448] = both.astype(BF16).T


def input_kernel(place, mine, other, gate_weight, up_weight, out):
    core = place[1]
    total = None
    for held, which in ((mine, core), (other, 1 - core)):
        units = pl.ds(pl.multiple_of(which * HALF, 32), HALF)
        right = jnp.concatenate([gate_weight[units], up_weight[units]], axis=0)
        term = jnp.dot(held[:, :, :448].reshape(8 * PART, 448), right, preferred_element_type=F32)
        total = term if total is None else total + term
    out[...] = total.astype(BF16).reshape(4, 2, PART, 256)


def second_product(place, mine, other, gate_weight, up_weight):
    held = pl.BlockSpec((4, 2 * PART, 512), lambda n: (0, 0, 0))
    weight = pl.BlockSpec((448, 256), lambda n: (0, n))
    return pl.pallas_call(
        input_kernel,
        grid=(4,),
        out_shape=shape(4, 2, PART, 1024, kind=BF16),
        in_specs=[PLACE, held, held, weight, weight],
        out_specs=pl.BlockSpec((4, 2, PART, 256), lambda n: (0, 0, 0, n)),
        compiler_params=pltpu.CompilerParams(vmem_limit_bytes=LIMIT),
    )(place, mine, other, gate_weight, up_weight)


def momentum_kernel(*refs):
    slots, (hidden, momentum, direction, new_momentum) = refs[:CUTS], refs[CUTS:]
    total = None
    for cut in range(CUTS):
        left = jnp.concatenate([hidden[cut, zh] for zh in range(4)], axis=1)
        term = jnp.dot(left, slots[cut][:, 0].reshape(8 * PART, 256), preferred_element_type=F32)
        total = term if total is None else total + term
    mean = total * 0.125
    direction[...] = (0.9 * momentum[...] + 0.1 * mean).astype(BF16)
    new_momentum[...] = 0.99 * momentum[...] + 0.01 * mean


def sum_kernel(slices, out):
    total = slices[0].astype(F32)
    for i in range(1, 32):
        total = total + slices[i].astype(F32)
    out[...] = total.astype(BF16)


def exchange(slots, axes):
    return lax.all_to_all(slots, axes, split_axis=0, concat_axis=0, tiled=True)


def around(blocks):
    return [lax.ppermute(block, AXES, ALONG[k + 1]) for k, block in enumerate(blocks)]


def body(d_out, gate_act, up_act, gate_weight, up_weight, down_weight, momentum):
    place = jnp.stack([lax.axis_index("zh"), lax.axis_index("co")]).astype(jnp.int32)
    turned = lax.ppermute(d_out, AXES, TRANSPOSE)
    acts = jnp.stack([gate_act.T, up_act.T])
    if CUTS > 1:
        acts = acts.reshape(2, 448, 4, CUTS, ROWS).swapaxes(2, 3).reshape(2, 448, 128)
    acts, turned = lax.optimization_barrier((acts, turned))
    low = lax.axis_index("zl")
    beside = lax.ppermute(turned, AXES, NEXT_CHIP)
    pair = jnp.stack([jnp.where(low == 0, turned, beside), jnp.where(low == 0, beside, turned)])
    pair = pair.reshape(2, 4, CUTS, ROWS, 256)
    blocks = []
    for cut in range(CUTS):
        spread = jnp.broadcast_to(pair[:, :, cut].reshape(1, 2, PART, 256), (16, 2, PART, 256))
        blocks.append(exchange(spread, ("x", "y")).reshape(4, 4, 2, PART, 256))

    groups = around([acts] * 3)
    blocks[0], *groups = lax.optimization_barrier((blocks[0], *groups))
    mine = jnp.stack([acts] + groups)
    other = lax.ppermute(mine, AXES, OTHER_CORE)
    hidden, by_gate, by_up = call(
        factor_kernel,
        (
            shape(CUTS, 4, 448, 2 * PART, kind=BF16),
            shape(CUTS, 4, HALF, 2 * PART),
            shape(CUTS, 4, HALF, 2 * PART),
        ),
        (place, mine, other),
    )

    results = []
    for cut in range(CUTS):
        keep, give = first_product(place, blocks[cut], down_weight.T)
        got = lax.ppermute(give, AXES, OTHER_CORE)
        own, *away = call(
            split_kernel,
            (shape(HALF, 2 * PART),) + (shape(HALF, 2 * PART, kind=BF16),) * 3,
            (place, keep, got),
        )
        total = own
        for block in around(away):
            total = total + block.astype(F32)
        total = total.astype(BF16)
        mine = jnp.stack([total] + around([total] * 3))
        mine = call(
            back_kernel,
            shape(4, 2 * PART, 512, kind=BF16),
            (place, mine, by_gate[cut], by_up[cut]),
        )
        other = lax.ppermute(mine, AXES, OTHER_CORE)
        partial = second_product(place, mine, other, gate_weight.T, up_weight.T)
        slices = exchange(partial.reshape(32, ROWS, 1024), TENSOR)
        results.append(
            pl.pallas_call(
                sum_kernel,
                out_shape=shape(ROWS, 1024, kind=BF16),
            )(slices)
        )
    d_in = jnp.concatenate(results, axis=0)

    direction, new_momentum = pl.pallas_call(
        momentum_kernel,
        grid=(4,),
        out_shape=(shape(448, 1024, kind=BF16), shape(448, 1024)),
        in_specs=[pl.BlockSpec((4, 1, 2, PART, 256), lambda y: (0, y, 0, 0, 0))] * CUTS
        + [
            pl.BlockSpec((CUTS, 4, 448, 2 * PART), lambda y: (0, 0, 0, 0)),
            pl.BlockSpec((448, 256), lambda y: (0, y)),
        ],
        out_specs=[pl.BlockSpec((448, 256), lambda y: (0, y))] * 2,
        compiler_params=pltpu.CompilerParams(vmem_limit_bytes=LIMIT),
    )(*blocks, hidden, momentum.T)
    return d_in, direction.T, new_momentum.T


def solution(mesh):
    fine = Mesh(mesh.devices.reshape(SIZES), AXES)
    both = P(DP, TENSOR)
    return jax.shard_map(
        body,
        mesh=fine,
        in_specs=(both,) * 7,
        out_specs=(P(TENSOR, DP), both, both),
        check_vma=False,
    )
```

time: 190 us -> 140 us (0.74)
  blocking collectives: 120 us -> 0 us
  waiting for transfers between devices: 25.7 us -> 67.5 us
  starting transfers between devices: 23.8 us -> 49.6 us
  Pallas kernels: 0 us -> 15.2 us
  matrix products: 14.6 us -> 0 us
    all_gather x3 -> x0, blocking collectives: 82.3 us -> none  [the longest x1 40.5 us: body(): lax.all_gather(gate_act, DP, axis=0, tiled=True).astype(jnp.float32)]
    ppermute x0 -> x13, waiting for transfers between devices: none -> 41.4 us  [the longest x9 35.1 us: around(): lax.ppermute(block, AXES, ALONG[k + 1])]
    all_to_all x1 -> x0, blocking collectives: 37.4 us -> none  [body(): lax.all_to_all(spread, TENSOR, split_axis=0, concat_axis=0, tiled=True)]
    ppermute x0 -> x13, starting transfers between devices: none -> 21.7 us  [the longest x9 17.9 us: around(): lax.ppermute(block, AXES, ALONG[k + 1])]
    pallas_call x0 -> x7, Pallas kernels: none -> 15.2 us  [the longest x1 3.87 us: second_product(): pl.pallas_call(input_kernel, grid=(4,), out_shape=shape(4, 2, PART, 1024,...]
    dot_general x4 -> x0, matrix products: 14.6 us -> none  [the longest x1 5.85 us: body(): lax.dot_general(exchanged, hidden, (((0,), (0,)), ((), ())), preferred_el...]
    all_to_all x2, starting transfers between devices: 16.9 us -> 21.2 us  [exchange(): return lax.all_to_all(slots, axes, split_axis=0, concat_axis=0, tiled=True)]
    unnamed x10, local copies, waits for them, and re-layouts: 0.03 us -> 2.79 us
  transfers between devices with their start and end apart: 3 -> 16, of which waited for: 2 -> 10; matrix products, arithmetic and copies ran while one was open for 3% -> 2% of each run, Pallas kernels for 0% -> 4%
where the time goes in v2:
time: 140 us
  waiting for transfers between devices  67.5 us (48%)
  starting transfers between devices  49.6 us (35%)
  Pallas kernels  15.2 us (11%)
  local copies, waits for them, and re-layouts  4.36 us (3%)
  other arithmetic  2.36 us (2%)
    ppermute x9, waiting for transfers between devices, around(): lax.ppermute(block, AXES, ALONG[k + 1])  35.1 us
    all_to_all x2, waiting for transfers between devices, exchange(): return lax.all_to_all(slots, axes, split_axis=0, concat_axis=0, tiled=True)  24.6 us
    all_to_all x2, starting transfers between devices, exchange(): return lax.all_to_all(slots, axes, split_axis=0, concat_axis=0, tiled=True)  21.2 us
    ppermute x9, starting transfers between devices, around(): lax.ppermute(block, AXES, ALONG[k + 1])  17.9 us
    ppermute x1, starting transfers between devices, body(): turned = lax.ppermute(d_out, AXES, TRANSPOSE)  6.78 us
    pallas_call x1, Pallas kernels, second_product(): pl.pallas_call(input_kernel, grid=(4,), out_shape=shape(4, 2, PART, 1024,...  3.87 us
    pallas_call x1, Pallas kernels, body(): pl.pallas_call(momentum_kernel, grid=(4,), out_shape=(shape(448, 1024, ki...  3.23 us
    pallas_call x3, Pallas kernels, call(): pl.pallas_call(kernel, out_shape=out_shape, in_specs=[PLACE] + [WHOLE] *...  3.12 us
  transfers between devices with their start and end apart: 16, of which 10 were waited for; matrix products, arithmetic and copies ran while one was open for 2% of the time, Pallas kernels for 4%

profile of v2, /device:TPU:3, one launch (start us, length us, event | category | flops | bytes accessed | tf_op | source)
XLA Modules:
  0.0 139.8 jit_solution(9884969069439483634)
XLA Ops:
  0.6 6.8 %collective-permute-start = (bf16[128,256]{1,0:T(8,128)(2,1)}, bf16[128,256]{1,0:T(8,128)(2,1)S(1)}, u32[]{:S(2)}, u32[]{:S(2)}) collective-permute-start(bf16[128,256]{1,0:T(8,128)(2,1)} %param.7), channel_id=1, source_target_pairs={{0,0},{1,1},{2,2},{3,3},{4,32},{5,33},{6,34},{7,35},{8,64},{9,65},... | collective-permute-start | bytes 196616 | tf_op jit(solution)/shard_map/ppermute | solution.py:173
  8.4 1.5 %collective-permute-done = bf16[128,256]{1,0:T(8,128)(2,1)S(1)} collective-permute-done((bf16[128,256]{1,0:T(8,128)(2,1)}, bf16[128,256]{1,0:T(8,128)(2,1)S(1)}, u32[]{:S(2)}, u32[]{:S(2)}) %collective-permute-start) | collective-permute-done | bytes 65568 | tf_op jit(solution)/shard_map/ppermute | solution.py:173
  9.9 3.1 %collective-permute-done.1 = bf16[128,256]{1,0:T(8,128)(2,1)S(1)} collective-permute-done((bf16[128,256]{1,0:T(8,128)(2,1)S(1)}, bf16[128,256]{1,0:T(8,128)(2,1)S(1)}, u32[]{:S(2)}, u32[]{:S(2)}) %collective-permute-start.1) | collective-permute-done | bytes 65568 | tf_op jit(solution)/shard_map/ppermute | solution.py:179
  13.1 1.6 %broadcast_in_dim.2 = bf16[16,2,128,256]{3,2,1,0:T(8,128)(2,1)} broadcast(bf16[2,128,256]{2,1,0:T(8,128)(2,1)S(1)} %pad_maximum_fusion.3), dimensions={1,2,3} | broadcast | bytes 2228224 | tf_op jit(solution)/shard_map/broadcast_in_dim | solution.py:184
  14.6 10.9 %all-to-all-start = ((bf16[16,2,128,256]{3,2,1,0:T(8,128)(2,1)}), bf16[16,2,128,256]{3,2,1,0:T(8,128)(2,1)S(1)}, u32[]{:S(2)}, u32[]{:S(2)}) async-start(bf16[16,2,128,256]{3,2,1,0:T(8,128)(2,1)} %broadcast_in_dim.2), calls=%async_computation | async-start | bytes 4194304 | tf_op jit(solution)/shard_map/all_to_all | solution.py:164
  26.9 3.2 %collective-permute-start.3 = (bf16[2,448,128]{2,1,0:T(8,128)(2,1)S(1)}, bf16[2,448,128]{2,1,0:T(8,128)(2,1)}, u32[]{:S(2)}, u32[]{:S(2)}) collective-permute-start(bf16[2,448,128]{2,1,0:T(8,128)(2,1)S(1)} %pad_maximum_fusion.2), channel_id=1, source_target_pairs={{0,128},{1,129},{2,130},{3,131},{4,132},{5,133},{6,134},{7,135},{8... | collective-permute-start | bytes 688136 | tf_op jit(solution)/shard_map/ppermute | solution.py:168
  30.2 1.8 %collective-permute-start.4 = (bf16[2,448,128]{2,1,0:T(8,128)(2,1)S(1)}, bf16[2,448,128]{2,1,0:T(8,128)(2,1)}, u32[]{:S(2)}, u32[]{:S(2)}) collective-permute-start(bf16[2,448,128]{2,1,0:T(8,128)(2,1)S(1)} %pad_maximum_fusion.2), channel_id=1, source_target_pairs={{0,192},{1,193},{2,194},{3,195},{4,196},{5,197},{6,198},{7,199},{8... | collective-permute-start | bytes 688136 | tf_op jit(solution)/shard_map/ppermute | solution.py:168
  33.3 6.9 %collective-permute-done.3 = bf16[2,448,128]{2,1,0:T(8,128)(2,1)} collective-permute-done((bf16[2,448,128]{2,1,0:T(8,128)(2,1)S(1)}, bf16[2,448,128]{2,1,0:T(8,128)(2,1)}, u32[]{:S(2)}, u32[]{:S(2)}) %collective-permute-start.3) | collective-permute-done | bytes 229408 | tf_op jit(solution)/shard_map/ppermute | solution.py:168
  40.2 13.0 %collective-permute-done.4 = bf16[2,448,128]{2,1,0:T(8,128)(2,1)} collective-permute-done((bf16[2,448,128]{2,1,0:T(8,128)(2,1)S(1)}, bf16[2,448,128]{2,1,0:T(8,128)(2,1)}, u32[]{:S(2)}, u32[]{:S(2)}) %collective-permute-start.4) | collective-permute-done | bytes 229408 | tf_op jit(solution)/shard_map/ppermute | solution.py:168
  53.2 2.5 %shard_map.94 = (f32[4,224,256]{2,1,0:T(8,128)S(1)}, f32[4,224,256]{2,1,0:T(8,128)S(1)}) custom-call(s32[2]{0:T(128)S(1)} %pad_add_fusion.place, bf16[4,4,2,128,256]{4,3,2,1,0:T(8,128)(2,1)S(1)} %bitcast.30, bf16[448,1024]{1,0:T(8,128)(2,1)S(1)} %bitcast.36), custom_call_target="tpu_custom_call" | custom-call | tf_op jit(solution)/shard_map/pallas_call | solution.py:67
  59.4 2.9 %collective-permute-start.8 = (bf16[224,256]{1,0:T(8,128)(2,1)S(1)}, bf16[224,256]{1,0:T(8,128)(2,1)S(1)}, u32[]{:S(2)}, u32[]{:S(2)}) collective-permute-start(bf16[224,256]{1,0:T(8,128)(2,1)S(1)} %get-tuple-element.28), channel_id=1, source_target_pairs={{0,192},{1,193},{2,194},{3,195},{4,196},{5,197},{6,198},{7,199},{8... | collective-permute-start | bytes 344072 | tf_op jit(solution)/shard_map/ppermute | solution.py:168
  62.3 1.8 %collective-permute-start.7 = (bf16[224,256]{1,0:T(8,128)(2,1)S(1)}, bf16[224,256]{1,0:T(8,128)(2,1)S(1)}, u32[]{:S(2)}, u32[]{:S(2)}) collective-permute-start(bf16[224,256]{1,0:T(8,128)(2,1)S(1)} %get-tuple-element.27), channel_id=1, source_target_pairs={{0,128},{1,129},{2,130},{3,131},{4,132},{5,133},{6,134},{7,135},{8... | collective-permute-start | bytes 344072 | tf_op jit(solution)/shard_map/ppermute | solution.py:168
  65.1 7.9 %collective-permute-done.7 = bf16[224,256]{1,0:T(8,128)(2,1)S(1)} collective-permute-done((bf16[224,256]{1,0:T(8,128)(2,1)S(1)}, bf16[224,256]{1,0:T(8,128)(2,1)S(1)}, u32[]{:S(2)}, u32[]{:S(2)}) %collective-permute-start.7) | collective-permute-done | bytes 114720 | tf_op jit(solution)/shard_map/ppermute | solution.py:168
  73.1 3.0 %collective-permute-start.11 = (bf16[224,256]{1,0:T(8,128)(2,1)S(1)}, bf16[224,256]{1,0:T(8,128)(2,1)S(1)}, u32[]{:S(2)}, u32[]{:S(2)}) collective-permute-start(bf16[224,256]{1,0:T(8,128)(2,1)S(1)} %add_convert_fusion), channel_id=1, source_target_pairs={{0,192},{1,193},{2,194},{3,195},{4,196},{5,197},{6,198},{7,199},{8... | collective-permute-start | bytes 344072 | tf_op jit(solution)/shard_map/ppermute | solution.py:168
  76.1 1.6 %collective-permute-start.10 = (bf16[224,256]{1,0:T(8,128)(2,1)S(1)}, bf16[224,256]{1,0:T(8,128)(2,1)S(1)}, u32[]{:S(2)}, u32[]{:S(2)}) collective-permute-start(bf16[224,256]{1,0:T(8,128)(2,1)S(1)} %add_convert_fusion), channel_id=1, source_target_pairs={{0,128},{1,129},{2,130},{3,131},{4,132},{5,133},{6,134},{7,135},{8... | collective-permute-start | bytes 344072 | tf_op jit(solution)/shard_map/ppermute | solution.py:168
  78.8 1.6 %shard_map.96 = (bf16[1,4,448,256]{3,2,1,0:T(8,128)(2,1)S(1)}, f32[1,4,224,256]{3,2,1,0:T(8,128)S(1)}, f32[1,4,224,256]{3,2,1,0:T(8,128)S(1)}) custom-call(s32[2]{0:T(128)S(1)} %pad_add_fusion.place, bf16[4,2,448,128]{3,2,1,0:T(8,128)(2,1)S(1)} %pad_maximum_fusion.mine, bf16[4,2,448,128]{3,2,1,0:T(8,128)(2,1)S(1)} %collective-permute-done.12.other), custom_call_target="tpu_custom_call" | custom-call | tf_op jit(solution)/shard_map/pallas_call | solution.py:44
  80.4 6.1 %collective-permute-done.10 = bf16[224,256]{1,0:T(8,128)(2,1)S(1)} collective-permute-done((bf16[224,256]{1,0:T(8,128)(2,1)S(1)}, bf16[224,256]{1,0:T(8,128)(2,1)S(1)}, u32[]{:S(2)}, u32[]{:S(2)}) %collective-permute-start.10) | collective-permute-done | bytes 114720 | tf_op jit(solution)/shard_map/ppermute | solution.py:168
  87.5 2.8 %collective-permute-start.13 = (bf16[4,256,512]{2,1,0:T(8,128)(2,1)S(1)}, bf16[4,256,512]{2,1,0:T(8,128)(2,1)S(1)}, u32[]{:S(2)}, u32[]{:S(2)}) collective-permute-start(bf16[4,256,512]{2,1,0:T(8,128)(2,1)S(1)} %shard_map.97.mine), channel_id=1, source_target_pairs={{0,32},{1,33},{2,34},{3,35},{4,36},{5,37},{6,38},{7,39},{8,40},{9,... | collective-permute-start | bytes 3145736 | tf_op jit(solution)/shard_map/ppermute | solution.py:220
  90.3 2.3 %collective-permute-done.13.other = bf16[4,256,512]{2,1,0:T(8,128)(2,1)S(1)} collective-permute-done((bf16[4,256,512]{2,1,0:T(8,128)(2,1)S(1)}, bf16[4,256,512]{2,1,0:T(8,128)(2,1)S(1)}, u32[]{:S(2)}, u32[]{:S(2)}) %collective-permute-start.13) | collective-permute-done | bytes 1048608 | tf_op jit(solution)/shard_map/ppermute | solution.py:220
  92.6 3.9 %shard_map.98 = bf16[4,2,128,1024]{3,2,1,0:T(8,128)(2,1)S(1)} custom-call(s32[2]{0:T(128)S(1)} %pad_add_fusion.place, bf16[4,256,512]{2,1,0:T(8,128)(2,1)S(1)} %shard_map.97.mine, bf16[4,256,512]{2,1,0:T(8,128)(2,1)S(1)} %collective-permute-done.13.other, bf16[448,1024]{1,0:T(8,128)(2,1)S(1)} %bitcast.34, bf16[448,1024]{1,0:T(8,128)(2,1)S(1)} %bitcast.35), custom_call_target="tpu_custom_call" | custom-call | tf_op jit(solution)/shard_map/pallas_call | solution.py:134
  97.7 10.2 %all-to-all-start.1 = ((bf16[32,32,1024]{2,1,0:T(8,128)(2,1)}), bf16[32,32,1024]{2,1,0:T(8,128)(2,1)}, u32[]{:S(2)}, u32[]{:S(2)}) async-start(bf16[32,32,1024]{2,1,0:T(8,128)(2,1)} %bitcast.32), calls=%async_computation.1 | async-start | bytes 4194304 | tf_op jit(solution)/shard_map/all_to_all | solution.py:164
  109.5 3.2 %shard_map.100 = (bf16[448,1024]{1,0:T(8,128)(2,1)}, f32[448,1024]{1,0:T(8,128)}) custom-call(bf16[4,4,2,128,256]{4,3,2,1,0:T(8,128)(2,1)S(1)} %bitcast.31, bf16[1,4,448,256]{3,2,1,0:T(8,128)(2,1)S(1)} %get-tuple-element.34.refs_1_, f32[448,1024]{1,0:T(8,128)S(1)} %bitcast.33), custom_call_target="tpu_custom_call" | custom-call | tf_op jit(solution)/shard_map/pallas_call | solution.py:231
  112.7 24.6 %all-to-all-done.1.slices = bf16[32,32,1024]{2,1,0:T(8,128)(2,1)} async-done(((bf16[32,32,1024]{2,1,0:T(8,128)(2,1)}), bf16[32,32,1024]{2,1,0:T(8,128)(2,1)}, u32[]{:S(2)}, u32[]{:S(2)}) %all-to-all-start.1) | async-done | bytes 2097184 | tf_op jit(solution)/shard_map/all_to_all | solution.py:164
  137.3 2.5 %shard_map.99 = bf16[32,1024]{1,0:T(8,128)(2,1)} custom-call(bf16[32,32,1024]{2,1,0:T(8,128)(2,1)} %all-to-all-done.1.slices), custom_call_target="tpu_custom_call" | custom-call | tf_op jit(solution)/shard_map/pallas_call | solution.py:224
  (33 shorter events, 13.3 us)
Async XLA Ops:
  0.6 9.3 %collective-permute-start = (bf16[128,256]{1,0:T(8,128)(2,1)}, bf16[128,256]{1,0:T(8,128)(2,1)S(1)}, u32[]{:S(2)}, u32[]{:S(2)}) collective-permute-start(bf16[128,256]{1,0:T(8,128)(2,1)} %param.7), channel_id=1, source_target_pairs={{0,0},{1,1},{2,2},{3,3},{4,32},{5,33},{6,34},{7,35},{8,64},{9,65},... | collective-permute-start | bytes 196616 | tf_op jit(solution)/shard_map/ppermute | solution.py:173
  9.9 3.1 %collective-permute-start.1 = (bf16[128,256]{1,0:T(8,128)(2,1)S(1)}, bf16[128,256]{1,0:T(8,128)(2,1)S(1)}, u32[]{:S(2)}, u32[]{:S(2)}) collective-permute-start(bf16[128,256]{1,0:T(8,128)(2,1)S(1)} %collective-permute-done), channel_id=1, source_target_pairs={{0,4},{1,5},{2,6},{3,7},{4,0},{5,1},{6,2},{7,3},{8,12},{9,13},{10,... | collective-permute-start | bytes 196616 | tf_op jit(solution)/shard_map/ppermute | solution.py:179
  14.6 38.6 %copy-start.4 = (bf16[1024,448]{0,1:T(8,128)(2,1)S(1)}, bf16[1024,448]{0,1:T(8,128)(2,1)}, u32[]{:S(2)}) copy-start(bf16[1024,448]{0,1:T(8,128)(2,1)} %param.12) | copy-start | bytes 2752516
  14.6 38.6 %all-to-all-start = ((bf16[16,2,128,256]{3,2,1,0:T(8,128)(2,1)}), bf16[16,2,128,256]{3,2,1,0:T(8,128)(2,1)S(1)}, u32[]{:S(2)}, u32[]{:S(2)}) async-start(bf16[16,2,128,256]{3,2,1,0:T(8,128)(2,1)} %broadcast_in_dim.2), calls=%async_computation | async-start | bytes 4194304 | tf_op jit(solution)/shard_map/all_to_all | solution.py:164
  25.5 7.8 %collective-permute-start.2 = (bf16[2,448,128]{2,1,0:T(8,128)(2,1)S(1)}, bf16[2,448,128]{2,1,0:T(8,128)(2,1)S(1)}, u32[]{:S(2)}, u32[]{:S(2)}) collective-permute-start(bf16[2,448,128]{2,1,0:T(8,128)(2,1)S(1)} %pad_maximum_fusion.2), channel_id=1, source_target_pairs={{0,64},{1,65},{2,66},{3,67},{4,68},{5,69},{6,70},{7,71},{8,72},{9,... | collective-permute-start | bytes 688136 | tf_op jit(solution)/shard_map/ppermute | solution.py:168
  26.9 13.2 %collective-permute-start.3 = (bf16[2,448,128]{2,1,0:T(8,128)(2,1)S(1)}, bf16[2,448,128]{2,1,0:T(8,128)(2,1)}, u32[]{:S(2)}, u32[]{:S(2)}) collective-permute-start(bf16[2,448,128]{2,1,0:T(8,128)(2,1)S(1)} %pad_maximum_fusion.2), channel_id=1, source_target_pairs={{0,128},{1,129},{2,130},{3,131},{4,132},{5,133},{6,134},{7,135},{8... | collective-permute-start | bytes 688136 | tf_op jit(solution)/shard_map/ppermute | solution.py:168
  30.2 23.0 %collective-permute-start.4 = (bf16[2,448,128]{2,1,0:T(8,128)(2,1)S(1)}, bf16[2,448,128]{2,1,0:T(8,128)(2,1)}, u32[]{:S(2)}, u32[]{:S(2)}) collective-permute-start(bf16[2,448,128]{2,1,0:T(8,128)(2,1)S(1)} %pad_maximum_fusion.2), channel_id=1, source_target_pairs={{0,192},{1,193},{2,194},{3,195},{4,196},{5,197},{6,198},{7,199},{8... | collective-permute-start | bytes 688136 | tf_op jit(solution)/shard_map/ppermute | solution.py:168
  55.7 3.0 %collective-permute-start.5 = (f32[4,224,256]{2,1,0:T(8,128)S(1)}, f32[4,224,256]{2,1,0:T(8,128)S(1)}, u32[]{:S(2)}, u32[]{:S(2)}) collective-permute-start(f32[4,224,256]{2,1,0:T(8,128)S(1)} %get-tuple-element.24), channel_id=1, source_target_pairs={{0,32},{1,33},{2,34},{3,35},{4,36},{5,37},{6,38},{7,39},{8,40},{9,... | collective-permute-start | bytes 2752520 | tf_op jit(solution)/shard_map/ppermute | solution.py:204
  57.8 21.0 %collective-permute-start.12 = (bf16[4,2,448,128]{3,2,1,0:T(8,128)(2,1)S(1)}, bf16[4,2,448,128]{3,2,1,0:T(8,128)(2,1)S(1)}, u32[]{:S(2)}, u32[]{:S(2)}) collective-permute-start(bf16[4,2,448,128]{3,2,1,0:T(8,128)(2,1)S(1)} %pad_maximum_fusion.mine), channel_id=1, source_target_pairs={{0,32},{1,33},{2,34},{3,35},{4,36},{5,37},{6,38},{7,39},{8,40},{9,... | collective-permute-start | bytes 2752520 | tf_op jit(solution)/shard_map/ppermute | solution.py:190
  59.4 5.7 %collective-permute-start.8 = (bf16[224,256]{1,0:T(8,128)(2,1)S(1)}, bf16[224,256]{1,0:T(8,128)(2,1)S(1)}, u32[]{:S(2)}, u32[]{:S(2)}) collective-permute-start(bf16[224,256]{1,0:T(8,128)(2,1)S(1)} %get-tuple-element.28), channel_id=1, source_target_pairs={{0,192},{1,193},{2,194},{3,195},{4,196},{5,197},{6,198},{7,199},{8... | collective-permute-start | bytes 344072 | tf_op jit(solution)/shard_map/ppermute | solution.py:168
  62.3 10.8 %collective-permute-start.7 = (bf16[224,256]{1,0:T(8,128)(2,1)S(1)}, bf16[224,256]{1,0:T(8,128)(2,1)S(1)}, u32[]{:S(2)}, u32[]{:S(2)}) collective-permute-start(bf16[224,256]{1,0:T(8,128)(2,1)S(1)} %get-tuple-element.27), channel_id=1, source_target_pairs={{0,128},{1,129},{2,130},{3,131},{4,132},{5,133},{6,134},{7,135},{8... | collective-permute-start | bytes 344072 | tf_op jit(solution)/shard_map/ppermute | solution.py:168
  64.1 8.9 %collective-permute-start.6 = (bf16[224,256]{1,0:T(8,128)(2,1)S(1)}, bf16[224,256]{1,0:T(8,128)(2,1)S(1)}, u32[]{:S(2)}, u32[]{:S(2)}) collective-permute-start(bf16[224,256]{1,0:T(8,128)(2,1)S(1)} %get-tuple-element.26), channel_id=1, source_target_pairs={{0,64},{1,65},{2,66},{3,67},{4,68},{5,69},{6,70},{7,71},{8,72},{9,... | collective-permute-start | bytes 344072 | tf_op jit(solution)/shard_map/ppermute | solution.py:168
  73.1 7.3 %collective-permute-start.11 = (bf16[224,256]{1,0:T(8,128)(2,1)S(1)}, bf16[224,256]{1,0:T(8,128)(2,1)S(1)}, u32[]{:S(2)}, u32[]{:S(2)}) collective-permute-start(bf16[224,256]{1,0:T(8,128)(2,1)S(1)} %add_convert_fusion), channel_id=1, source_target_pairs={{0,192},{1,193},{2,194},{3,195},{4,196},{5,197},{6,198},{7,199},{8... | collective-permute-start | bytes 344072 | tf_op jit(solution)/shard_map/ppermute | solution.py:168
  76.1 10.4 %collective-permute-start.10 = (bf16[224,256]{1,0:T(8,128)(2,1)S(1)}, bf16[224,256]{1,0:T(8,128)(2,1)S(1)}, u32[]{:S(2)}, u32[]{:S(2)}) collective-permute-start(bf16[224,256]{1,0:T(8,128)(2,1)S(1)} %add_convert_fusion), channel_id=1, source_target_pairs={{0,128},{1,129},{2,130},{3,131},{4,132},{5,133},{6,134},{7,135},{8... | collective-permute-start | bytes 344072 | tf_op jit(solution)/shard_map/ppermute | solution.py:168
  77.8 8.7 %collective-permute-start.9 = (bf16[224,256]{1,0:T(8,128)(2,1)S(1)}, bf16[224,256]{1,0:T(8,128)(2,1)S(1)}, u32[]{:S(2)}, u32[]{:S(2)}) collective-permute-start(bf16[224,256]{1,0:T(8,128)(2,1)S(1)} %add_convert_fusion), channel_id=1, source_target_pairs={{0,64},{1,65},{2,66},{3,67},{4,68},{5,69},{6,70},{7,71},{8,72},{9,... | collective-permute-start | bytes 344072 | tf_op jit(solution)/shard_map/ppermute | solution.py:168
  86.5 6.1 %copy-start.2 = (bf16[1024,448]{0,1:T(8,128)(2,1)S(1)}, bf16[1024,448]{0,1:T(8,128)(2,1)}, u32[]{:S(2)}) copy-start(bf16[1024,448]{0,1:T(8,128)(2,1)} %param.10) | copy-start | bytes 2752516
  86.5 6.1 %copy-start.3 = (bf16[1024,448]{0,1:T(8,128)(2,1)S(1)}, bf16[1024,448]{0,1:T(8,128)(2,1)}, u32[]{:S(2)}) copy-start(bf16[1024,448]{0,1:T(8,128)(2,1)} %param.11) | copy-start | bytes 2752516
  87.5 5.1 %collective-permute-start.13 = (bf16[4,256,512]{2,1,0:T(8,128)(2,1)S(1)}, bf16[4,256,512]{2,1,0:T(8,128)(2,1)S(1)}, u32[]{:S(2)}, u32[]{:S(2)}) collective-permute-start(bf16[4,256,512]{2,1,0:T(8,128)(2,1)S(1)} %shard_map.97.mine), channel_id=1, source_target_pairs={{0,32},{1,33},{2,34},{3,35},{4,36},{5,37},{6,38},{7,39},{8,40},{9,... | collective-permute-start | bytes 3145736 | tf_op jit(solution)/shard_map/ppermute | solution.py:220
  96.4 1.3 copy-start
  97.7 39.6 %all-to-all-start.1 = ((bf16[32,32,1024]{2,1,0:T(8,128)(2,1)}), bf16[32,32,1024]{2,1,0:T(8,128)(2,1)}, u32[]{:S(2)}, u32[]{:S(2)}) async-start(bf16[32,32,1024]{2,1,0:T(8,128)(2,1)} %bitcast.32), calls=%async_computation.1 | async-start | bytes 4194304 | tf_op jit(solution)/shard_map/all_to_all | solution.py:164
  108.0 1.5 %copy-start.1 = (f32[1024,448]{0,1:T(8,128)S(1)}, f32[1024,448]{0,1:T(8,128)}, u32[]{:S(2)}) copy-start(f32[1024,448]{0,1:T(8,128)} %param.13) | copy-start | bytes 5505028

commit v3 on v2

--- a/solution.py
+++ b/solution.py
@@ -28,7 +28,7 @@
     return found
 
 
-TRANSPOSE = pairs(lambda zh, co, x, zl, y: (x, zl, zh, co, y))
+TRANSPOSE = pairs(lambda zh, co, x, zl, y: (x, zl, (zh + 2) % 4, co, y))
 OTHER_CORE = pairs(lambda zh, co, x, zl, y: (zh, 1 - co, x, zl, y))
 NEXT_CHIP = pairs(lambda zh, co, x, zl, y: (zh, co, x, 1 - zl, y))
 ALONG = [None] + [
@@ -52,28 +52,28 @@
     )(*operands)
 
 
-def product_kernel(place, slots, weight, keep, give):
+def product_kernel(place, slots, weight, keep, give, held, sems):
     core = place[1]
-    right = jnp.concatenate([slots[0, y].reshape(2 * PART, 256) for y in range(4)], axis=1)
-    for which, out in ((core, keep), (1 - core, give)):
-        left = weight[pl.ds(pl.multiple_of(which * HALF, 32), HALF), :]
-        out[0] = lax.dot_general(
-            left, right, (((1,), (1,)), ((), ())), preferred_element_type=F32
-        )
+    copies = [pltpu.make_async_copy(slots.at[zh ^ 2], held.at[zh], sems.at[zh]) for zh in range(4)]
+    for copy in copies:
+        copy.start()
+    for zh, copy in enumerate(copies):
+        copy.wait()
+        right = jnp.concatenate([held[zh, y].reshape(2 * PART, 256) for y in range(4)], axis=1)
+        for which, out in ((core, keep), (1 - core, give)):
+            left = weight[pl.ds(pl.multiple_of(which * HALF, 32), HALF), :]
+            out[zh] = lax.dot_general(
+                left, right, (((1,), (1,)), ((), ())), preferred_element_type=F32
+            )
 
 
 def first_product(place, slots, weight):
-    part = pl.BlockSpec((1, HALF, 2 * PART), lambda zh: (zh, 0, 0))
     return pl.pallas_call(
         product_kernel,
-        grid=(4,),
         out_shape=(shape(4, HALF, 2 * PART),) * 2,
-        in_specs=[
-            PLACE,
-            pl.BlockSpec((1, 4, 2, PART, 256), lambda zh: (zh, 0, 0, 0, 0)),
-            pl.BlockSpec((448, 1024), lambda zh: (0, 0)),
-        ],
-        out_specs=[part, part],
+        in_specs=[PLACE, pl.BlockSpec(memory_space=pl.ANY), WHOLE],
+        out_specs=[WHOLE] * 2,
+        scratch_shapes=[pltpu.VMEM((4, 4, 2, PART, 256), BF16), pltpu.SemaphoreType.DMA((4,))],
         compiler_params=pltpu.CompilerParams(vmem_limit_bytes=LIMIT),
     )(place, slots, weight)
 
@@ -119,33 +119,31 @@
 
 def input_kernel(place, mine, other, gate_weight, up_weight, out):
     core = place[1]
-    total = None
-    for held, which in ((mine, core), (other, 1 - core)):
-        units = pl.ds(pl.multiple_of(which * HALF, 32), HALF)
-        right = jnp.concatenate([gate_weight[units], up_weight[units]], axis=0)
-        term = jnp.dot(held[:, :, :448].reshape(8 * PART, 448), right, preferred_element_type=F32)
-        total = term if total is None else total + term
-    out[...] = total.astype(BF16).reshape(4, 2, PART, 256)
+    for n in range(4):
+        columns = slice(n * 256, (n + 1) * 256)
+        total = None
+        for held, which in ((mine, core), (other, 1 - core)):
+            units = pl.ds(pl.multiple_of(which * HALF, 32), HALF)
+            right = jnp.concatenate([gate_weight[units, columns], up_weight[units, columns]], axis=0)
+            left = held[:, :, :448].reshape(8 * PART, 448)
+            term = jnp.dot(left, right, preferred_element_type=F32)
+            total = term if total is None else total + term
+        out[:, :, :, columns] = total.astype(BF16).reshape(4, 2, PART, 256)
 
 
 def second_product(place, mine, other, gate_weight, up_weight):
-    held = pl.BlockSpec((4, 2 * PART, 512), lambda n: (0, 0, 0))
-    weight = pl.BlockSpec((448, 256), lambda n: (0, n))
-    return pl.pallas_call(
+    return call(
         input_kernel,
-        grid=(4,),
-        out_shape=shape(4, 2, PART, 1024, kind=BF16),
-        in_specs=[PLACE, held, held, weight, weight],
-        out_specs=pl.BlockSpec((4, 2, PART, 256), lambda n: (0, 0, 0, n)),
-        compiler_params=pltpu.CompilerParams(vmem_limit_bytes=LIMIT),
-    )(place, mine, other, gate_weight, up_weight)
+        shape(4, 2, PART, 1024, kind=BF16),
+        (place, mine, other, gate_weight, up_weight),
+    )
 
 
 def momentum_kernel(*refs):
     slots, (hidden, momentum, direction, new_momentum) = refs[:CUTS], refs[CUTS:]
     total = None
     for cut in range(CUTS):
-        left = jnp.concatenate([hidden[cut, zh] for zh in range(4)], axis=1)
+        left = jnp.concatenate([hidden[cut, zh ^ 2] for zh in range(4)], axis=1)
         term = jnp.dot(left, slots[cut][:, 0].reshape(8 * PART, 256), preferred_element_type=F32)
         total = term if total is None else total + term
     mean = total * 0.125
@@ -153,10 +151,19 @@
     new_momentum[...] = 0.99 * momentum[...] + 0.01 * mean
 
 
-def sum_kernel(slices, out):
-    total = slices[0].astype(F32)
-    for i in range(1, 32):
-        total = total + slices[i].astype(F32)
+def sum_kernel(slices, out, held, sems):
+    copies = [
+        pltpu.make_async_copy(slices.at[pl.ds(4 * i, 4)], held.at[pl.ds(4 * i, 4)], sems.at[i])
+        for i in range(8)
+    ]
+    for copy in copies:
+        copy.start()
+    total = None
+    for i, copy in enumerate(copies):
+        copy.wait()
+        for j in range(4 * i, 4 * i + 4):
+            term = held[j].astype(F32)
+            total = term if total is None else total + term
     out[...] = total.astype(BF16)
 
 
@@ -224,6 +231,12 @@
             pl.pallas_call(
                 sum_kernel,
                 out_shape=shape(ROWS, 1024, kind=BF16),
+                in_specs=[pl.BlockSpec(memory_space=pl.ANY)],
+                scratch_shapes=[
+                    pltpu.VMEM((32, ROWS, 1024), BF16),
+                    pltpu.SemaphoreType.DMA((8,)),
+                ],
+                compiler_params=pltpu.CompilerParams(vmem_limit_bytes=LIMIT),
             )(slices)
         )
     d_in = jnp.concatenate(results, axis=0)

time: 140 us -> 139 us (level)
    ppermute x9, starting transfers between devices: 17.9 us -> 25.9 us  [around(): lax.ppermute(block, AXES, ALONG[k + 1])]
    all_to_all x2, starting transfers between devices: 21.2 us -> 13.2 us  [exchange(): return lax.all_to_all(slots, axes, split_axis=0, concat_axis=0, tiled=True)]
    pallas_call x3 -> x2, Pallas kernels: 8.9 us -> 4.91 us  [the longest x1 2.68 us: first_product(): pl.pallas_call(product_kernel, out_shape=(shape(4, HALF, 2 * PART),) * 2,...]
    pallas_call x3 -> x4, Pallas kernels: 3.12 us -> 6.17 us  [call(): pl.pallas_call(kernel, out_shape=out_shape, in_specs=[PLACE] + [WHOLE] *...]
    ppermute x1, waiting for transfers between devices: 1.5 us -> 4.25 us  [body(): turned = lax.ppermute(d_out, AXES, TRANSPOSE)]
    ppermute x9, waiting for transfers between devices: 35.1 us -> 32.7 us  [around(): lax.ppermute(block, AXES, ALONG[k + 1])]
  transfers between devices with their start and end apart: 16 -> 16, of which waited for: 10 -> 12; matrix products, arithmetic and copies ran while one was open for 2% -> 2% of each run, Pallas kernels for 4% -> 4%
where the time goes in v3:
time: 139 us
  waiting for transfers between devices  68.3 us (49%)
  starting transfers between devices  48.3 us (35%)
  Pallas kernels  14.3 us (10%)
  local copies, waits for them, and re-layouts  4.36 us (3%)
  other arithmetic  2.36 us (2%)
    ppermute x9, waiting for transfers between devices, around(): lax.ppermute(block, AXES, ALONG[k + 1])  32.7 us
    ppermute x9, starting transfers between devices, around(): lax.ppermute(block, AXES, ALONG[k + 1])  25.9 us
    all_to_all x2, waiting for transfers between devices, exchange(): return lax.all_to_all(slots, axes, split_axis=0, concat_axis=0, tiled=True)  24.6 us
    all_to_all x2, starting transfers between devices, exchange(): return lax.all_to_all(slots, axes, split_axis=0, concat_axis=0, tiled=True)  13.2 us
    pallas_call x4, Pallas kernels, call(): pl.pallas_call(kernel, out_shape=out_shape, in_specs=[PLACE] + [WHOLE] *...  6.17 us
    ppermute x1, starting transfers between devices, body(): turned = lax.ppermute(d_out, AXES, TRANSPOSE)  5.91 us
    ppermute x1, waiting for transfers between devices, body(): turned = lax.ppermute(d_out, AXES, TRANSPOSE)  4.25 us
    ppermute x1, waiting for transfers between devices, body(): beside = lax.ppermute(turned, AXES, NEXT_CHIP)  3.66 us
  transfers between devices with their start and end apart: 16, of which 12 were waited for; matrix products, arithmetic and copies ran while one was open for 2% of the time, Pallas kernels for 4%

profile of v3, /device:TPU:3, one launch (start us, length us, event | category | flops | bytes accessed | tf_op | source)
XLA Modules:
  0.0 138.5 jit_solution(13393848752078179026)
XLA Ops:
  0.6 5.9 %collective-permute-start = (bf16[128,256]{1,0:T(8,128)(2,1)}, bf16[128,256]{1,0:T(8,128)(2,1)S(1)}, u32[]{:S(2)}, u32[]{:S(2)}) collective-permute-start(bf16[128,256]{1,0:T(8,128)(2,1)} %param.7), channel_id=1, source_target_pairs={{0,16},{1,17},{2,18},{3,19},{4,48},{5,49},{6,50},{7,51},{8,80},{9,... | collective-permute-start | bytes 196616 | tf_op jit(solution)/shard_map/ppermute | solution.py:180
  7.5 4.2 %collective-permute-done = bf16[128,256]{1,0:T(8,128)(2,1)S(1)} collective-permute-done((bf16[128,256]{1,0:T(8,128)(2,1)}, bf16[128,256]{1,0:T(8,128)(2,1)S(1)}, u32[]{:S(2)}, u32[]{:S(2)}) %collective-permute-start) | collective-permute-done | bytes 65568 | tf_op jit(solution)/shard_map/ppermute | solution.py:180
  11.8 3.7 %collective-permute-done.1 = bf16[128,256]{1,0:T(8,128)(2,1)S(1)} collective-permute-done((bf16[128,256]{1,0:T(8,128)(2,1)S(1)}, bf16[128,256]{1,0:T(8,128)(2,1)S(1)}, u32[]{:S(2)}, u32[]{:S(2)}) %collective-permute-start.1) | collective-permute-done | bytes 65568 | tf_op jit(solution)/shard_map/ppermute | solution.py:186
  17.0 5.5 %all-to-all-start = ((bf16[16,2,128,256]{3,2,1,0:T(8,128)(2,1)}), bf16[16,2,128,256]{3,2,1,0:T(8,128)(2,1)S(1)}, u32[]{:S(2)}, u32[]{:S(2)}) async-start(bf16[16,2,128,256]{3,2,1,0:T(8,128)(2,1)} %broadcast_in_dim.2), calls=%async_computation | async-start | bytes 4194304 | tf_op jit(solution)/shard_map/all_to_all | solution.py:171
  24.7 5.1 %collective-permute-start.3 = (bf16[2,448,128]{2,1,0:T(8,128)(2,1)S(1)}, bf16[2,448,128]{2,1,0:T(8,128)(2,1)}, u32[]{:S(2)}, u32[]{:S(2)}) collective-permute-start(bf16[2,448,128]{2,1,0:T(8,128)(2,1)S(1)} %pad_maximum_fusion.2), channel_id=1, source_target_pairs={{0,128},{1,129},{2,130},{3,131},{4,132},{5,133},{6,134},{7,135},{8... | collective-permute-start | bytes 688136 | tf_op jit(solution)/shard_map/ppermute | solution.py:175
  29.8 2.5 %collective-permute-start.4 = (bf16[2,448,128]{2,1,0:T(8,128)(2,1)S(1)}, bf16[2,448,128]{2,1,0:T(8,128)(2,1)}, u32[]{:S(2)}, u32[]{:S(2)}) collective-permute-start(bf16[2,448,128]{2,1,0:T(8,128)(2,1)S(1)} %pad_maximum_fusion.2), channel_id=1, source_target_pairs={{0,192},{1,193},{2,194},{3,195},{4,196},{5,197},{6,198},{7,199},{8... | collective-permute-start | bytes 688136 | tf_op jit(solution)/shard_map/ppermute | solution.py:175
  32.4 2.7 %collective-permute-done.2 = bf16[2,448,128]{2,1,0:T(8,128)(2,1)S(1)} collective-permute-done((bf16[2,448,128]{2,1,0:T(8,128)(2,1)S(1)}, bf16[2,448,128]{2,1,0:T(8,128)(2,1)S(1)}, u32[]{:S(2)}, u32[]{:S(2)}) %collective-permute-start.2) | collective-permute-done | bytes 229408 | tf_op jit(solution)/shard_map/ppermute | solution.py:175
  35.1 9.5 %collective-permute-done.3 = bf16[2,448,128]{2,1,0:T(8,128)(2,1)} collective-permute-done((bf16[2,448,128]{2,1,0:T(8,128)(2,1)S(1)}, bf16[2,448,128]{2,1,0:T(8,128)(2,1)}, u32[]{:S(2)}, u32[]{:S(2)}) %collective-permute-start.3) | collective-permute-done | bytes 229408 | tf_op jit(solution)/shard_map/ppermute | solution.py:175
  44.6 5.9 %collective-permute-done.4 = bf16[2,448,128]{2,1,0:T(8,128)(2,1)} collective-permute-done((bf16[2,448,128]{2,1,0:T(8,128)(2,1)S(1)}, bf16[2,448,128]{2,1,0:T(8,128)(2,1)}, u32[]{:S(2)}, u32[]{:S(2)}) %collective-permute-start.4) | collective-permute-done | bytes 229408 | tf_op jit(solution)/shard_map/ppermute | solution.py:175
  50.6 2.7 %shard_map.94 = (f32[4,224,256]{2,1,0:T(8,128)S(1)}, f32[4,224,256]{2,1,0:T(8,128)S(1)}) custom-call(s32[2]{0:T(128)S(1)} %pad_add_fusion.place, bf16[4,4,2,128,256]{4,3,2,1,0:T(8,128)(2,1)S(1)} %bitcast.30, bf16[448,1024]{1,0:T(8,128)(2,1)S(1)} %bitcast.36), custom_call_target="tpu_custom_call" | custom-call | tf_op jit(solution)/shard_map/pallas_call | solution.py:71
  56.6 5.2 %collective-permute-start.8 = (bf16[224,256]{1,0:T(8,128)(2,1)S(1)}, bf16[224,256]{1,0:T(8,128)(2,1)S(1)}, u32[]{:S(2)}, u32[]{:S(2)}) collective-permute-start(bf16[224,256]{1,0:T(8,128)(2,1)S(1)} %get-tuple-element.28), channel_id=1, source_target_pairs={{0,192},{1,193},{2,194},{3,195},{4,196},{5,197},{6,198},{7,199},{8... | collective-permute-start | bytes 344072 | tf_op jit(solution)/shard_map/ppermute | solution.py:175
  62.8 2.3 %collective-permute-start.6 = (bf16[224,256]{1,0:T(8,128)(2,1)S(1)}, bf16[224,256]{1,0:T(8,128)(2,1)S(1)}, u32[]{:S(2)}, u32[]{:S(2)}) collective-permute-start(bf16[224,256]{1,0:T(8,128)(2,1)S(1)} %get-tuple-element.26), channel_id=1, source_target_pairs={{0,64},{1,65},{2,66},{3,67},{4,68},{5,69},{6,70},{7,71},{8,72},{9,... | collective-permute-start | bytes 344072 | tf_op jit(solution)/shard_map/ppermute | solution.py:175
  65.1 9.0 %collective-permute-done.7 = bf16[224,256]{1,0:T(8,128)(2,1)S(1)} collective-permute-done((bf16[224,256]{1,0:T(8,128)(2,1)S(1)}, bf16[224,256]{1,0:T(8,128)(2,1)S(1)}, u32[]{:S(2)}, u32[]{:S(2)}) %collective-permute-start.7) | collective-permute-done | bytes 114720 | tf_op jit(solution)/shard_map/ppermute | solution.py:175
  74.1 3.0 %collective-permute-start.11 = (bf16[224,256]{1,0:T(8,128)(2,1)S(1)}, bf16[224,256]{1,0:T(8,128)(2,1)S(1)}, u32[]{:S(2)}, u32[]{:S(2)}) collective-permute-start(bf16[224,256]{1,0:T(8,128)(2,1)S(1)} %add_convert_fusion), channel_id=1, source_target_pairs={{0,192},{1,193},{2,194},{3,195},{4,196},{5,197},{6,198},{7,199},{8... | collective-permute-start | bytes 344072 | tf_op jit(solution)/shard_map/ppermute | solution.py:175
  77.1 2.4 %collective-permute-start.10 = (bf16[224,256]{1,0:T(8,128)(2,1)S(1)}, bf16[224,256]{1,0:T(8,128)(2,1)S(1)}, u32[]{:S(2)}, u32[]{:S(2)}) collective-permute-start(bf16[224,256]{1,0:T(8,128)(2,1)S(1)} %add_convert_fusion), channel_id=1, source_target_pairs={{0,128},{1,129},{2,130},{3,131},{4,132},{5,133},{6,134},{7,135},{8... | collective-permute-start | bytes 344072 | tf_op jit(solution)/shard_map/ppermute | solution.py:175
  79.5 2.3 %collective-permute-start.9 = (bf16[224,256]{1,0:T(8,128)(2,1)S(1)}, bf16[224,256]{1,0:T(8,128)(2,1)S(1)}, u32[]{:S(2)}, u32[]{:S(2)}) collective-permute-start(bf16[224,256]{1,0:T(8,128)(2,1)S(1)} %add_convert_fusion), channel_id=1, source_target_pairs={{0,64},{1,65},{2,66},{3,67},{4,68},{5,69},{6,70},{7,71},{8,72},{9,... | collective-permute-start | bytes 344072 | tf_op jit(solution)/shard_map/ppermute | solution.py:175
  84.2 3.3 %collective-permute-done.10 = bf16[224,256]{1,0:T(8,128)(2,1)S(1)} collective-permute-done((bf16[224,256]{1,0:T(8,128)(2,1)S(1)}, bf16[224,256]{1,0:T(8,128)(2,1)S(1)}, u32[]{:S(2)}, u32[]{:S(2)}) %collective-permute-start.10) | collective-permute-done | bytes 114720 | tf_op jit(solution)/shard_map/ppermute | solution.py:175
  90.0 2.6 %collective-permute-start.13 = (bf16[4,256,512]{2,1,0:T(8,128)(2,1)S(1)}, bf16[4,256,512]{2,1,0:T(8,128)(2,1)S(1)}, u32[]{:S(2)}, u32[]{:S(2)}) collective-permute-start(bf16[4,256,512]{2,1,0:T(8,128)(2,1)S(1)} %shard_map.97.mine), channel_id=1, source_target_pairs={{0,32},{1,33},{2,34},{3,35},{4,36},{5,37},{6,38},{7,39},{8,40},{9,... | collective-permute-start | bytes 3145736 | tf_op jit(solution)/shard_map/ppermute | solution.py:227
  92.6 2.3 %collective-permute-done.13.other = bf16[4,256,512]{2,1,0:T(8,128)(2,1)S(1)} collective-permute-done((bf16[4,256,512]{2,1,0:T(8,128)(2,1)S(1)}, bf16[4,256,512]{2,1,0:T(8,128)(2,1)S(1)}, u32[]{:S(2)}, u32[]{:S(2)}) %collective-permute-start.13) | collective-permute-done | bytes 1048608 | tf_op jit(solution)/shard_map/ppermute | solution.py:227
  94.9 2.9 %shard_map.98 = bf16[4,2,128,1024]{3,2,1,0:T(8,128)(2,1)S(1)} custom-call(s32[2]{0:T(128)S(1)} %pad_add_fusion.place, bf16[4,256,512]{2,1,0:T(8,128)(2,1)S(1)} %shard_map.97.mine, bf16[4,256,512]{2,1,0:T(8,128)(2,1)S(1)} %collective-permute-done.13.other, bf16[448,1024]{1,0:T(8,128)(2,1)S(1)} %bitcast.34, bf16[448,1024]{1,0:T(8,128)(2,1)S(1)} %bitcast.35), custom_call_target="tpu_custom_call" | custom-call | tf_op jit(solution)/shard_map/pallas_call | solution.py:44
  99.1 7.7 %all-to-all-start.1 = ((bf16[32,32,1024]{2,1,0:T(8,128)(2,1)}), bf16[32,32,1024]{2,1,0:T(8,128)(2,1)}, u32[]{:S(2)}, u32[]{:S(2)}) async-start(bf16[32,32,1024]{2,1,0:T(8,128)(2,1)} %bitcast.32), calls=%async_computation.1 | async-start | bytes 4194304 | tf_op jit(solution)/shard_map/all_to_all | solution.py:171
  108.3 3.2 %shard_map.100 = (bf16[448,1024]{1,0:T(8,128)(2,1)}, f32[448,1024]{1,0:T(8,128)}) custom-call(bf16[4,4,2,128,256]{4,3,2,1,0:T(8,128)(2,1)S(1)} %bitcast.31, bf16[1,4,448,256]{3,2,1,0:T(8,128)(2,1)S(1)} %get-tuple-element.34.refs_1_, f32[448,1024]{1,0:T(8,128)S(1)} %bitcast.33), custom_call_target="tpu_custom_call" | custom-call | tf_op jit(solution)/shard_map/pallas_call | solution.py:244
  111.5 24.6 %all-to-all-done.1.slices = bf16[32,32,1024]{2,1,0:T(8,128)(2,1)} async-done(((bf16[32,32,1024]{2,1,0:T(8,128)(2,1)}), bf16[32,32,1024]{2,1,0:T(8,128)(2,1)}, u32[]{:S(2)}, u32[]{:S(2)}) %all-to-all-start.1) | async-done | bytes 2097184 | tf_op jit(solution)/shard_map/all_to_all | solution.py:171
  136.1 2.2 %shard_map.99 = bf16[32,1024]{1,0:T(8,128)(2,1)} custom-call(bf16[32,32,1024]{2,1,0:T(8,128)(2,1)} %all-to-all-done.1.slices), custom_call_target="tpu_custom_call" | custom-call | tf_op jit(solution)/shard_map/pallas_call | solution.py:231
  (33 shorter events, 16.9 us)
Async XLA Ops:
  0.6 11.1 %collective-permute-start = (bf16[128,256]{1,0:T(8,128)(2,1)}, bf16[128,256]{1,0:T(8,128)(2,1)S(1)}, u32[]{:S(2)}, u32[]{:S(2)}) collective-permute-start(bf16[128,256]{1,0:T(8,128)(2,1)} %param.7), channel_id=1, source_target_pairs={{0,16},{1,17},{2,18},{3,19},{4,48},{5,49},{6,50},{7,51},{8,80},{9,... | collective-permute-start | bytes 196616 | tf_op jit(solution)/shard_map/ppermute | solution.py:180
  11.8 3.7 %collective-permute-start.1 = (bf16[128,256]{1,0:T(8,128)(2,1)S(1)}, bf16[128,256]{1,0:T(8,128)(2,1)S(1)}, u32[]{:S(2)}, u32[]{:S(2)}) collective-permute-start(bf16[128,256]{1,0:T(8,128)(2,1)S(1)} %collective-permute-done), channel_id=1, source_target_pairs={{0,4},{1,5},{2,6},{3,7},{4,0},{5,1},{6,2},{7,3},{8,12},{9,13},{10,... | collective-permute-start | bytes 196616 | tf_op jit(solution)/shard_map/ppermute | solution.py:186
  17.0 33.5 %copy-start.4 = (bf16[1024,448]{0,1:T(8,128)(2,1)S(1)}, bf16[1024,448]{0,1:T(8,128)(2,1)}, u32[]{:S(2)}) copy-start(bf16[1024,448]{0,1:T(8,128)(2,1)} %param.12) | copy-start | bytes 2752516
  17.0 33.5 %all-to-all-start = ((bf16[16,2,128,256]{3,2,1,0:T(8,128)(2,1)}), bf16[16,2,128,256]{3,2,1,0:T(8,128)(2,1)S(1)}, u32[]{:S(2)}, u32[]{:S(2)}) async-start(bf16[16,2,128,256]{3,2,1,0:T(8,128)(2,1)} %broadcast_in_dim.2), calls=%async_computation | async-start | bytes 4194304 | tf_op jit(solution)/shard_map/all_to_all | solution.py:171
  22.6 12.6 %collective-permute-start.2 = (bf16[2,448,128]{2,1,0:T(8,128)(2,1)S(1)}, bf16[2,448,128]{2,1,0:T(8,128)(2,1)S(1)}, u32[]{:S(2)}, u32[]{:S(2)}) collective-permute-start(bf16[2,448,128]{2,1,0:T(8,128)(2,1)S(1)} %pad_maximum_fusion.2), channel_id=1, source_target_pairs={{0,64},{1,65},{2,66},{3,67},{4,68},{5,69},{6,70},{7,71},{8,72},{9,... | collective-permute-start | bytes 688136 | tf_op jit(solution)/shard_map/ppermute | solution.py:175
  24.7 19.9 %collective-permute-start.3 = (bf16[2,448,128]{2,1,0:T(8,128)(2,1)S(1)}, bf16[2,448,128]{2,1,0:T(8,128)(2,1)}, u32[]{:S(2)}, u32[]{:S(2)}) collective-permute-start(bf16[2,448,128]{2,1,0:T(8,128)(2,1)S(1)} %pad_maximum_fusion.2), channel_id=1, source_target_pairs={{0,128},{1,129},{2,130},{3,131},{4,132},{5,133},{6,134},{7,135},{8... | collective-permute-start | bytes 688136 | tf_op jit(solution)/shard_map/ppermute | solution.py:175
  29.8 20.8 %collective-permute-start.4 = (bf16[2,448,128]{2,1,0:T(8,128)(2,1)S(1)}, bf16[2,448,128]{2,1,0:T(8,128)(2,1)}, u32[]{:S(2)}, u32[]{:S(2)}) collective-permute-start(bf16[2,448,128]{2,1,0:T(8,128)(2,1)S(1)} %pad_maximum_fusion.2), channel_id=1, source_target_pairs={{0,192},{1,193},{2,194},{3,195},{4,196},{5,197},{6,198},{7,199},{8... | collective-permute-start | bytes 688136 | tf_op jit(solution)/shard_map/ppermute | solution.py:175
  53.3 2.7 %collective-permute-start.5 = (f32[4,224,256]{2,1,0:T(8,128)S(1)}, f32[4,224,256]{2,1,0:T(8,128)S(1)}, u32[]{:S(2)}, u32[]{:S(2)}) collective-permute-start(f32[4,224,256]{2,1,0:T(8,128)S(1)} %get-tuple-element.24), channel_id=1, source_target_pairs={{0,32},{1,33},{2,34},{3,35},{4,36},{5,37},{6,38},{7,39},{8,40},{9,... | collective-permute-start | bytes 2752520 | tf_op jit(solution)/shard_map/ppermute | solution.py:211
  55.0 26.7 %collective-permute-start.12 = (bf16[4,2,448,128]{3,2,1,0:T(8,128)(2,1)S(1)}, bf16[4,2,448,128]{3,2,1,0:T(8,128)(2,1)S(1)}, u32[]{:S(2)}, u32[]{:S(2)}) collective-permute-start(bf16[4,2,448,128]{3,2,1,0:T(8,128)(2,1)S(1)} %pad_maximum_fusion.mine), channel_id=1, source_target_pairs={{0,32},{1,33},{2,34},{3,35},{4,36},{5,37},{6,38},{7,39},{8,40},{9,... | collective-permute-start | bytes 2752520 | tf_op jit(solution)/shard_map/ppermute | solution.py:197
  56.6 8.5 %collective-permute-start.8 = (bf16[224,256]{1,0:T(8,128)(2,1)S(1)}, bf16[224,256]{1,0:T(8,128)(2,1)S(1)}, u32[]{:S(2)}, u32[]{:S(2)}) collective-permute-start(bf16[224,256]{1,0:T(8,128)(2,1)S(1)} %get-tuple-element.28), channel_id=1, source_target_pairs={{0,192},{1,193},{2,194},{3,195},{4,196},{5,197},{6,198},{7,199},{8... | collective-permute-start | bytes 344072 | tf_op jit(solution)/shard_map/ppermute | solution.py:175
  61.8 12.2 %collective-permute-start.7 = (bf16[224,256]{1,0:T(8,128)(2,1)S(1)}, bf16[224,256]{1,0:T(8,128)(2,1)S(1)}, u32[]{:S(2)}, u32[]{:S(2)}) collective-permute-start(bf16[224,256]{1,0:T(8,128)(2,1)S(1)} %get-tuple-element.27), channel_id=1, source_target_pairs={{0,128},{1,129},{2,130},{3,131},{4,132},{5,133},{6,134},{7,135},{8... | collective-permute-start | bytes 344072 | tf_op jit(solution)/shard_map/ppermute | solution.py:175
  62.8 11.2 %collective-permute-start.6 = (bf16[224,256]{1,0:T(8,128)(2,1)S(1)}, bf16[224,256]{1,0:T(8,128)(2,1)S(1)}, u32[]{:S(2)}, u32[]{:S(2)}) collective-permute-start(bf16[224,256]{1,0:T(8,128)(2,1)S(1)} %get-tuple-element.26), channel_id=1, source_target_pairs={{0,64},{1,65},{2,66},{3,67},{4,68},{5,69},{6,70},{7,71},{8,72},{9,... | collective-permute-start | bytes 344072 | tf_op jit(solution)/shard_map/ppermute | solution.py:175
  74.1 10.2 %collective-permute-start.11 = (bf16[224,256]{1,0:T(8,128)(2,1)S(1)}, bf16[224,256]{1,0:T(8,128)(2,1)S(1)}, u32[]{:S(2)}, u32[]{:S(2)}) collective-permute-start(bf16[224,256]{1,0:T(8,128)(2,1)S(1)} %add_convert_fusion), channel_id=1, source_target_pairs={{0,192},{1,193},{2,194},{3,195},{4,196},{5,197},{6,198},{7,199},{8... | collective-permute-start | bytes 344072 | tf_op jit(solution)/shard_map/ppermute | solution.py:175
  77.1 10.4 %collective-permute-start.10 = (bf16[224,256]{1,0:T(8,128)(2,1)S(1)}, bf16[224,256]{1,0:T(8,128)(2,1)S(1)}, u32[]{:S(2)}, u32[]{:S(2)}) collective-permute-start(bf16[224,256]{1,0:T(8,128)(2,1)S(1)} %add_convert_fusion), channel_id=1, source_target_pairs={{0,128},{1,129},{2,130},{3,131},{4,132},{5,133},{6,134},{7,135},{8... | collective-permute-start | bytes 344072 | tf_op jit(solution)/shard_map/ppermute | solution.py:175
  79.5 9.6 %collective-permute-start.9 = (bf16[224,256]{1,0:T(8,128)(2,1)S(1)}, bf16[224,256]{1,0:T(8,128)(2,1)S(1)}, u32[]{:S(2)}, u32[]{:S(2)}) collective-permute-start(bf16[224,256]{1,0:T(8,128)(2,1)S(1)} %add_convert_fusion), channel_id=1, source_target_pairs={{0,64},{1,65},{2,66},{3,67},{4,68},{5,69},{6,70},{7,71},{8,72},{9,... | collective-permute-start | bytes 344072 | tf_op jit(solution)/shard_map/ppermute | solution.py:175
  89.1 5.8 %copy-start.2 = (bf16[1024,448]{0,1:T(8,128)(2,1)S(1)}, bf16[1024,448]{0,1:T(8,128)(2,1)}, u32[]{:S(2)}) copy-start(bf16[1024,448]{0,1:T(8,128)(2,1)} %param.10) | copy-start | bytes 2752516
  89.1 5.8 %copy-start.3 = (bf16[1024,448]{0,1:T(8,128)(2,1)S(1)}, bf16[1024,448]{0,1:T(8,128)(2,1)}, u32[]{:S(2)}) copy-start(bf16[1024,448]{0,1:T(8,128)(2,1)} %param.11) | copy-start | bytes 2752516
  90.0 4.9 %collective-permute-start.13 = (bf16[4,256,512]{2,1,0:T(8,128)(2,1)S(1)}, bf16[4,256,512]{2,1,0:T(8,128)(2,1)S(1)}, u32[]{:S(2)}, u32[]{:S(2)}) collective-permute-start(bf16[4,256,512]{2,1,0:T(8,128)(2,1)S(1)} %shard_map.97.mine), channel_id=1, source_target_pairs={{0,32},{1,33},{2,34},{3,35},{4,36},{5,37},{6,38},{7,39},{8,40},{9,... | collective-permute-start | bytes 3145736 | tf_op jit(solution)/shard_map/ppermute | solution.py:227
  97.8 1.3 copy-start
  99.1 37.0 %all-to-all-start.1 = ((bf16[32,32,1024]{2,1,0:T(8,128)(2,1)}), bf16[32,32,1024]{2,1,0:T(8,128)(2,1)}, u32[]{:S(2)}, u32[]{:S(2)}) async-start(bf16[32,32,1024]{2,1,0:T(8,128)(2,1)} %bitcast.32), calls=%async_computation.1 | async-start | bytes 4194304 | tf_op jit(solution)/shard_map/all_to_all | solution.py:171
  106.8 1.5 %copy-start.1 = (f32[1024,448]{0,1:T(8,128)S(1)}, f32[1024,448]{0,1:T(8,128)}, u32[]{:S(2)}) copy-start(f32[1024,448]{0,1:T(8,128)} %param.13) | copy-start | bytes 5505028

commit v4 on v1

v4 whole, which is shorter than its diff:
```python
import jax
import jax.numpy as jnp
import numpy as np
from jax import lax
from jax.experimental import pallas as pl
from jax.experimental.pallas import tpu as pltpu
from jax.sharding import Mesh, PartitionSpec as P

AXES = ("zh", "co", "x", "zl", "y")
SIZES = (4, 2, 4, 2, 4)
DP = ("zh", "co")
TENSOR = ("x", "zl", "y")
F32, BF16 = jnp.float32, jnp.bfloat16
PLACE = pl.BlockSpec(memory_space=pltpu.SMEM)
WHOLE = pl.BlockSpec(memory_space=pltpu.VMEM)
LIMIT = 16 * 1024 * 1024


def pairs(move):
    found = []
    for source in range(256):
        place = [int(v) for v in np.unravel_index(source, SIZES)]
        found.append((source, int(np.ravel_multi_index(move(*place), SIZES))))
    return found


TRANSPOSE = pairs(lambda zh, co, x, zl, y: (x, co, (zh + 2) % 4, zl, y))
OTHER_CORE = pairs(lambda zh, co, x, zl, y: (zh, 1 - co, x, zl, y))
NEXT_CHIP = pairs(lambda zh, co, x, zl, y: (zh, co, x, 1 - zl, y))
ALONG = [pairs(lambda zh, co, x, zl, y, k=k: ((zh + k) % 4, co, x, zl, y)) for k in (1, 2, 3)]


def shape(*dims, kind=F32):
    return jax.ShapeDtypeStruct(dims, kind)


def call(kernel, out_shape, operands):
    return pl.pallas_call(
        kernel,
        out_shape=out_shape,
        in_specs=[PLACE] + [WHOLE] * (len(operands) - 1),
        out_specs=jax.tree.map(lambda _: WHOLE, out_shape),
        compiler_params=pltpu.CompilerParams(vmem_limit_bytes=LIMIT),
    )(*operands)


def product_kernel(place, slots, own_weight, other_weight, own, one, two, three, held, sems):
    core = place[1]
    copies = [
        pltpu.make_async_copy(
            slots.at[jnp.bitwise_xor(lax.rem(place[0] + k, 4), 2)], held.at[k], sems.at[k]
        )
        for k in range(4)
    ]
    for copy in copies:
        copy.start()
    turn = (((1,), (1,)), ((), ()))
    for k, outs in ((0, (own, one)), (2, (two, three))):
        copies[k].wait()
        copies[k + 1].wait()
        total = None
        for weight, which in ((own_weight, core), (other_weight, 1 - core)):
            for y in range(4):
                term = lax.dot_general(
                    weight[:, y * 256 : (y + 1) * 256],
                    held[k : k + 2, y, which].reshape(256, 256),
                    turn,
                    preferred_element_type=F32,
                )
                total = term if total is None else total + term
        for i, out in enumerate(outs):
            out[...] = total[:, i * 128 : (i + 1) * 128].astype(out.dtype)


def first_product(place, slots, own_weight, other_weight):
    return pl.pallas_call(
        product_kernel,
        out_shape=(shape(448, 128),) + (shape(448, 128, kind=BF16),) * 3,
        in_specs=[PLACE, pl.BlockSpec(memory_space=pl.ANY), WHOLE, WHOLE],
        out_specs=[WHOLE] * 4,
        scratch_shapes=[pltpu.VMEM((4, 4, 2, 128, 256), BF16), pltpu.SemaphoreType.DMA((4,))],
        compiler_params=pltpu.CompilerParams(vmem_limit_bytes=LIMIT),
    )(place, slots, own_weight, other_weight)


def factor_kernel(place, zero, one, two, three, hidden, by_gate, by_up):
    for k, held in enumerate((zero, one, two, three)):
        group = lax.rem(place[0] + 4 - k, 4)
        gate, up = held[0].astype(F32), held[1].astype(F32)
        sigma = jax.nn.sigmoid(gate)
        swish = gate * sigma
        hidden[group] = (swish * up).astype(BF16)
        by_up[group] = swish
        by_gate[group] = up * sigma * (1.0 + gate * (1.0 - sigma))


def back_kernel(place, zero, one, two, three, by_gate, by_up, out):
    for k, held in enumerate((zero, one, two, three)):
        group = lax.rem(place[0] + 4 - k, 4)
        block = held[...].astype(F32)
        both = jnp.concatenate([block * by_gate[group], block * by_up[group]], axis=0)
        out[group] = both.astype(BF16).T


def input_kernel(place, mine, other, gate_weight, up_weight, out):
    core = place[1]
    for n in range(4):
        columns = slice(n * 256, (n + 1) * 256)
        right = jnp.concatenate([gate_weight[:, columns], up_weight[:, columns]], axis=0)
        for held, which in ((mine, core), (other, 1 - core)):
            total = jnp.dot(held[...].reshape(512, 896), right, preferred_element_type=F32)
            for zh in range(4):
                out[zh, which, :, columns] = total[zh * 128 : (zh + 1) * 128].astype(BF16)


def momentum_kernel(place, slots, far, mine, other, momentum, direction, new_momentum):
    core = place[1]
    lefts = [mine[zh] for zh in range(4)] + [other[zh] for zh in range(4)]
    rights = [slots[zh ^ 2, 0, core] for zh in range(4)] + [far[zh ^ 2, 0] for zh in range(4)]
    total = jnp.dot(
        jnp.concatenate(lefts, axis=1), jnp.concatenate(rights, axis=0), preferred_element_type=F32
    )
    mean = total * 0.125
    direction[...] = (0.9 * momentum[...] + 0.1 * mean).astype(BF16)
    new_momentum[...] = 0.99 * momentum[...] + 0.01 * mean


def sum_kernel(slices, out, held, sems):
    copies = [
        pltpu.make_async_copy(slices.at[pl.ds(4 * i, 4)], held.at[pl.ds(4 * i, 4)], sems.at[i])
        for i in range(8)
    ]
    for copy in copies:
        copy.start()
    total = None
    for i, copy in enumerate(copies):
        copy.wait()
        for j in range(4 * i, 4 * i + 4):
            term = held[j].astype(F32)
            total = term if total is None else total + term
    out[...] = total.astype(BF16)


def exchange(slots, axes):
    return lax.all_to_all(slots, axes, split_axis=0, concat_axis=0, tiled=True)


def moved(block, route):
    return lax.ppermute(block, AXES, route)


def around(block):
    return [moved(block, route) for route in ALONG]


def body(d_out, gate_act, up_act, gate_weight, up_weight, down_weight, momentum):
    core = lax.axis_index("co")
    place = jnp.stack([lax.axis_index("zh"), core]).astype(jnp.int32)
    turned = moved(d_out, TRANSPOSE)
    acts = jnp.stack([gate_act.T, up_act.T])
    down_weight = down_weight.T
    down_other = moved(down_weight, OTHER_CORE)
    acts, turned, down_other = lax.optimization_barrier((acts, turned, down_other))
    beside = moved(turned, NEXT_CHIP)
    first = lax.axis_index("zl") == 0
    pair = jnp.stack([jnp.where(first, turned, beside), jnp.where(first, beside, turned)])
    slots = exchange(jnp.broadcast_to(pair[None], (16, 2, 128, 256)), ("x", "y"))
    slots = slots.reshape(4, 4, 2, 128, 256)
    groups = [acts] + around(acts)
    slots, *groups = lax.optimization_barrier((slots, *groups))

    own, *away = first_product(place, slots, down_weight, down_other)
    total = own
    for piece, route in zip(away, ALONG):
        total = total + moved(piece, route).astype(F32)
    total = total.astype(BF16)

    hidden, by_gate, by_up = call(
        factor_kernel,
        (shape(4, 448, 128, kind=BF16), shape(4, 448, 128), shape(4, 448, 128)),
        (place, *groups),
    )

    mine = call(
        back_kernel,
        shape(4, 128, 896, kind=BF16),
        (place, total, *around(total), by_gate, by_up),
    )
    other = moved(mine, OTHER_CORE)
    partial = call(
        input_kernel,
        shape(4, 2, 128, 1024, kind=BF16),
        (place, mine, other, gate_weight.T, up_weight.T),
    )
    slices = exchange(partial.reshape(32, 32, 1024), TENSOR)
    d_in = pl.pallas_call(
        sum_kernel,
        out_shape=shape(32, 1024, kind=BF16),
        in_specs=[pl.BlockSpec(memory_space=pl.ANY)],
        scratch_shapes=[pltpu.VMEM((32, 32, 1024), BF16), pltpu.SemaphoreType.DMA((8,))],
        compiler_params=pltpu.CompilerParams(vmem_limit_bytes=LIMIT),
    )(slices)

    hidden, slots, mine = lax.optimization_barrier((hidden, slots, mine))
    other = moved(hidden, OTHER_CORE)
    far = moved(lax.dynamic_index_in_dim(slots, 1 - core, 2, keepdims=False), OTHER_CORE)
    held = pl.BlockSpec((4, 448, 128), lambda y: (0, 0, 0))
    near = pl.BlockSpec((4, 1, 2, 128, 256), lambda y: (0, y, 0, 0, 0))
    some = pl.BlockSpec((4, 1, 128, 256), lambda y: (0, y, 0, 0))
    part = pl.BlockSpec((448, 256), lambda y: (0, y))
    direction, new_momentum = pl.pallas_call(
        momentum_kernel,
        grid=(4,),
        out_shape=(shape(448, 1024, kind=BF16), shape(448, 1024)),
        in_specs=[PLACE, near, some, held, held, part],
        out_specs=[part] * 2,
        compiler_params=pltpu.CompilerParams(vmem_limit_bytes=LIMIT),
    )(place, slots, far, hidden, other, momentum.T)
    return d_in, direction.T, new_momentum.T


def solution(mesh):
    fine = Mesh(mesh.devices.reshape(SIZES), AXES)
    both = P(DP, TENSOR)
    return jax.shard_map(
        body,
        mesh=fine,
        in_specs=(both,) * 7,
        out_specs=(P(TENSOR, DP), both, both),
        check_vma=False,
    )
```

time: 190 us -> 136 us (0.72)
  blocking collectives: 120 us -> 0 us
  waiting for transfers between devices: 25.7 us -> 62 us
  starting transfers between devices: 23.8 us -> 52.7 us
  matrix products: 14.6 us -> 0 us
  Pallas kernels: 0 us -> 14.4 us
    all_gather x3 -> x0, blocking collectives: 82.3 us -> none  [the longest x1 40.5 us: body(): lax.all_gather(gate_act, DP, axis=0, tiled=True).astype(jnp.float32)]
    ppermute x1 -> x15, waiting for transfers between devices: 2.38 us -> 40.5 us  [moved(): return lax.ppermute(block, AXES, route)]
    all_to_all x1 -> x0, blocking collectives: 37.4 us -> none  [body(): lax.all_to_all(spread, TENSOR, split_axis=0, concat_axis=0, tiled=True)]
    ppermute x1 -> x15, starting transfers between devices: 6.92 us -> 37.5 us  [moved(): return lax.ppermute(block, AXES, route)]
    dot_general x4 -> x0, matrix products: 14.6 us -> none  [the longest x1 5.85 us: body(): lax.dot_general(exchanged, hidden, (((0,), (0,)), ((), ())), preferred_el...]
    pallas_call x0 -> x6, Pallas kernels: none -> 14.4 us  [the longest x3 5.42 us: call(): pl.pallas_call(kernel, out_shape=out_shape, in_specs=[PLACE] + [WHOLE] *...]
    transpose x1 -> x0, local copies, waits for them, and re-layouts: 2.56 us -> none  [body(): slots.reshape(8, 4, 128, 256).transpose(0, 2, 1, 3).reshape(1024, 1024)]
    unnamed x10 -> x14, local copies, waits for them, and re-layouts: 0.03 us -> 2.51 us
  transfers between devices with their start and end apart: 3 -> 17, of which waited for: 2 -> 12; matrix products, arithmetic and copies ran while one was open for 3% -> 1% of each run, Pallas kernels for 0% -> 4%
where the time goes in v4:
time: 136 us; the launch traced here: 135 us
  waiting for transfers between devices  62 us (46%)
  starting transfers between devices  52.7 us (39%)
  Pallas kernels  14.4 us (11%)
  local copies, waits for them, and re-layouts  4.18 us (3%)
    ppermute x15, waiting for transfers between devices, moved(): return lax.ppermute(block, AXES, route)  40.5 us
    ppermute x15, starting transfers between devices, moved(): return lax.ppermute(block, AXES, route)  37.5 us
    all_to_all x2, waiting for transfers between devices, exchange(): return lax.all_to_all(slots, axes, split_axis=0, concat_axis=0, tiled=True)  21.5 us
    all_to_all x2, starting transfers between devices, exchange(): return lax.all_to_all(slots, axes, split_axis=0, concat_axis=0, tiled=True)  15.3 us
    pallas_call x3, Pallas kernels, call(): pl.pallas_call(kernel, out_shape=out_shape, in_specs=[PLACE] + [WHOLE] *...  5.42 us
    pallas_call x1, Pallas kernels, body(): pl.pallas_call(momentum_kernel, grid=(4,), out_shape=(shape(448, 1024, ki...  3.74 us
    pallas_call x1, Pallas kernels, first_product(): pl.pallas_call(product_kernel, out_shape=(shape(448, 128),) + (shape(448,...  2.99 us
  transfers between devices with their start and end apart: 17, of which 12 were waited for; matrix products, arithmetic and copies ran while one was open for 1% of the time, Pallas kernels for 4%

profile of v4, /device:TPU:3, one launch (start us, length us, event | category | flops | bytes accessed | tf_op | source)
XLA Modules:
  0.0 135.4 jit_solution(17904458915378687945)
XLA Ops:
  1.4 3.9 %collective-permute-start = (bf16[128,256]{1,0:T(8,128)(2,1)}, bf16[128,256]{1,0:T(8,128)(2,1)S(1)}, u32[]{:S(2)}, u32[]{:S(2)}) collective-permute-start(bf16[128,256]{1,0:T(8,128)(2,1)} %param.7), channel_id=1, source_target_pairs={{0,16},{1,17},{2,18},{3,19},{4,20},{5,21},{6,22},{7,23},{8,80},{9,... | collective-permute-start | bytes 196616 | tf_op jit(solution)/shard_map/ppermute | solution.py:149
  6.3 3.7 %collective-permute-done = bf16[128,256]{1,0:T(8,128)(2,1)S(1)} collective-permute-done((bf16[128,256]{1,0:T(8,128)(2,1)}, bf16[128,256]{1,0:T(8,128)(2,1)S(1)}, u32[]{:S(2)}, u32[]{:S(2)}) %collective-permute-start) | collective-permute-done | bytes 65568 | tf_op jit(solution)/shard_map/ppermute | solution.py:149
  10.0 3.5 %collective-permute-start.2 = (bf16[128,256]{1,0:T(8,128)(2,1)S(1)}, bf16[128,256]{1,0:T(8,128)(2,1)S(1)}, u32[]{:S(2)}, u32[]{:S(2)}) collective-permute-start(bf16[128,256]{1,0:T(8,128)(2,1)S(1)} %collective-permute-done), channel_id=1, source_target_pairs={{0,4},{1,5},{2,6},{3,7},{4,0},{5,1},{6,2},{7,3},{8,12},{9,13},{10,... | collective-permute-start | bytes 196616 | tf_op jit(solution)/shard_map/ppermute | solution.py:149
  16.8 5.5 %all-to-all-start = ((bf16[16,2,128,256]{3,2,1,0:T(8,128)(2,1)}), bf16[16,2,128,256]{3,2,1,0:T(8,128)(2,1)S(1)}, u32[]{:S(2)}, u32[]{:S(2)}) async-start(bf16[16,2,128,256]{3,2,1,0:T(8,128)(2,1)} %broadcast_in_dim.2), calls=%async_computation | async-start | bytes 4194304 | tf_op jit(solution)/shard_map/all_to_all | solution.py:145
  22.3 6.6 %collective-permute-start.5 = (bf16[2,448,128]{2,1,0:T(8,128)(2,1)S(1)}, bf16[2,448,128]{2,1,0:T(8,128)(2,1)S(1)}, u32[]{:S(2)}, u32[]{:S(2)}) collective-permute-start(bf16[2,448,128]{2,1,0:T(8,128)(2,1)S(1)} %pad_maximum_fusion.zero), channel_id=1, source_target_pairs={{0,192},{1,193},{2,194},{3,195},{4,196},{5,197},{6,198},{7,199},{8... | collective-permute-start | bytes 688136 | tf_op jit(solution)/shard_map/ppermute | solution.py:149
  28.9 2.3 %collective-permute-start.3 = (bf16[2,448,128]{2,1,0:T(8,128)(2,1)S(1)}, bf16[2,448,128]{2,1,0:T(8,128)(2,1)}, u32[]{:S(2)}, u32[]{:S(2)}) collective-permute-start(bf16[2,448,128]{2,1,0:T(8,128)(2,1)S(1)} %pad_maximum_fusion.zero), channel_id=1, source_target_pairs={{0,64},{1,65},{2,66},{3,67},{4,68},{5,69},{6,70},{7,71},{8,72},{9,... | collective-permute-start | bytes 688136 | tf_op jit(solution)/shard_map/ppermute | solution.py:149
  33.1 10.5 %collective-permute-done.4.two = bf16[2,448,128]{2,1,0:T(8,128)(2,1)} collective-permute-done((bf16[2,448,128]{2,1,0:T(8,128)(2,1)S(1)}, bf16[2,448,128]{2,1,0:T(8,128)(2,1)}, u32[]{:S(2)}, u32[]{:S(2)}) %collective-permute-start.4) | collective-permute-done | bytes 229408 | tf_op jit(solution)/shard_map/ppermute | solution.py:149
  43.6 3.2 %collective-permute-done.3.one = bf16[2,448,128]{2,1,0:T(8,128)(2,1)} collective-permute-done((bf16[2,448,128]{2,1,0:T(8,128)(2,1)S(1)}, bf16[2,448,128]{2,1,0:T(8,128)(2,1)}, u32[]{:S(2)}, u32[]{:S(2)}) %collective-permute-start.3) | collective-permute-done | bytes 229408 | tf_op jit(solution)/shard_map/ppermute | solution.py:149
  48.1 3.0 %shard_map.94 = (f32[448,128]{1,0:T(8,128)S(1)}, bf16[448,128]{1,0:T(8,128)(2,1)S(1)}, bf16[448,128]{1,0:T(8,128)(2,1)S(1)}, bf16[448,128]{1,0:T(8,128)(2,1)S(1)}) custom-call(s32[2]{0:T(128)S(1)} %pad_add_fusion.place, bf16[4,4,2,128,256]{4,3,2,1,0:T(8,128)(2,1)S(1)} %bitcast.22, bf16[448,1024]{1,0:T(8,128)(2,1)S(1)} %bitcast.28, ...), custom_call_target="tpu_custom_call" | custom-call | tf_op jit(solution)/shard_map/pallas_call | solution.py:76
  51.1 3.3 %collective-permute-start.6 = (bf16[448,128]{1,0:T(8,128)(2,1)S(1)}, bf16[448,128]{1,0:T(8,128)(2,1)S(1)}, u32[]{:S(2)}, u32[]{:S(2)}) collective-permute-start(bf16[448,128]{1,0:T(8,128)(2,1)S(1)} %get-tuple-element.27), channel_id=1, source_target_pairs={{0,64},{1,65},{2,66},{3,67},{4,68},{5,69},{6,70},{7,71},{8,72},{9,... | collective-permute-start | bytes 344072 | tf_op jit(solution)/shard_map/ppermute | solution.py:149
  54.3 5.2 %collective-permute-start.7 = (bf16[448,128]{1,0:T(8,128)(2,1)S(1)}, bf16[448,128]{1,0:T(8,128)(2,1)S(1)}, u32[]{:S(2)}, u32[]{:S(2)}) collective-permute-start(bf16[448,128]{1,0:T(8,128)(2,1)S(1)} %get-tuple-element.28), channel_id=1, source_target_pairs={{0,128},{1,129},{2,130},{3,131},{4,132},{5,133},{6,134},{7,135},{8... | collective-permute-start | bytes 344072 | tf_op jit(solution)/shard_map/ppermute | solution.py:149
  60.9 2.5 %collective-permute-done.7 = bf16[448,128]{1,0:T(8,128)(2,1)S(1)} collective-permute-done((bf16[448,128]{1,0:T(8,128)(2,1)S(1)}, bf16[448,128]{1,0:T(8,128)(2,1)S(1)}, u32[]{:S(2)}, u32[]{:S(2)}) %collective-permute-start.7) | collective-permute-done | bytes 114720 | tf_op jit(solution)/shard_map/ppermute | solution.py:149
  63.4 5.5 %collective-permute-done.8 = bf16[448,128]{1,0:T(8,128)(2,1)S(1)} collective-permute-done((bf16[448,128]{1,0:T(8,128)(2,1)S(1)}, bf16[448,128]{1,0:T(8,128)(2,1)S(1)}, u32[]{:S(2)}, u32[]{:S(2)}) %collective-permute-start.8) | collective-permute-done | bytes 114720 | tf_op jit(solution)/shard_map/ppermute | solution.py:149
  69.1 3.6 %collective-permute-start.10 = (bf16[448,128]{1,0:T(8,128)(2,1)S(1)}, bf16[448,128]{1,0:T(8,128)(2,1)S(1)}, u32[]{:S(2)}, u32[]{:S(2)}) collective-permute-start(bf16[448,128]{1,0:T(8,128)(2,1)S(1)} %add_convert_fusion.zero), channel_id=1, source_target_pairs={{0,128},{1,129},{2,130},{3,131},{4,132},{5,133},{6,134},{7,135},{8... | collective-permute-start | bytes 344072 | tf_op jit(solution)/shard_map/ppermute | solution.py:149
  74.2 3.8 %collective-permute-done.10.two = bf16[448,128]{1,0:T(8,128)(2,1)S(1)} collective-permute-done((bf16[448,128]{1,0:T(8,128)(2,1)S(1)}, bf16[448,128]{1,0:T(8,128)(2,1)S(1)}, u32[]{:S(2)}, u32[]{:S(2)}) %collective-permute-start.10) | collective-permute-done | bytes 114720 | tf_op jit(solution)/shard_map/ppermute | solution.py:149
  78.0 2.8 %collective-permute-done.9.one = bf16[448,128]{1,0:T(8,128)(2,1)S(1)} collective-permute-done((bf16[448,128]{1,0:T(8,128)(2,1)S(1)}, bf16[448,128]{1,0:T(8,128)(2,1)S(1)}, u32[]{:S(2)}, u32[]{:S(2)}) %collective-permute-start.9) | collective-permute-done | bytes 114720 | tf_op jit(solution)/shard_map/ppermute | solution.py:149
  81.6 5.8 %collective-permute-start.12 = (bf16[4,128,896]{2,1,0:T(8,128)(2,1)S(1)}, bf16[4,128,896]{2,1,0:T(8,128)(2,1)S(1)}, u32[]{:S(2)}, u32[]{:S(2)}) collective-permute-start(bf16[4,128,896]{2,1,0:T(8,128)(2,1)S(1)} %shard_map.96.mine), channel_id=1, source_target_pairs={{0,32},{1,33},{2,34},{3,35},{4,36},{5,37},{6,38},{7,39},{8,40},{9,... | collective-permute-start | bytes 2752520 | tf_op jit(solution)/shard_map/ppermute | solution.py:149
  87.4 2.1 %collective-permute-done.12.other = bf16[4,128,896]{2,1,0:T(8,128)(2,1)S(1)} collective-permute-done((bf16[4,128,896]{2,1,0:T(8,128)(2,1)S(1)}, bf16[4,128,896]{2,1,0:T(8,128)(2,1)S(1)}, u32[]{:S(2)}, u32[]{:S(2)}) %collective-permute-start.12) | collective-permute-done | bytes 917536 | tf_op jit(solution)/shard_map/ppermute | solution.py:149
  89.5 3.1 %shard_map.97 = bf16[4,2,128,1024]{3,2,1,0:T(8,128)(2,1)S(1)} custom-call(s32[2]{0:T(128)S(1)} %pad_add_fusion.place, bf16[4,128,896]{2,1,0:T(8,128)(2,1)S(1)} %shard_map.96.mine, bf16[4,128,896]{2,1,0:T(8,128)(2,1)S(1)} %collective-permute-done.12.other, bf16[448,1024]{1,0:T(8,128)(2,1)S(1)} %bitcast.29, bf16[448,1024]{1,0:T(8,128)(2,1)S(1)} %bitcast.30), custom_call_target="tpu_custom_call" | custom-call | tf_op jit(solution)/shard_map/pallas_call | solution.py:38
  93.9 9.8 %all-to-all-start.1 = ((bf16[32,32,1024]{2,1,0:T(8,128)(2,1)}), bf16[32,32,1024]{2,1,0:T(8,128)(2,1)}, u32[]{:S(2)}, u32[]{:S(2)}) async-start(bf16[32,32,1024]{2,1,0:T(8,128)(2,1)} %bitcast.25), calls=%async_computation.1 | async-start | bytes 4194304 | tf_op jit(solution)/shard_map/all_to_all | solution.py:145
  104.9 2.8 %collective-permute-done.14.other = bf16[4,448,128]{2,1,0:T(8,128)(2,1)S(1)} collective-permute-done((bf16[4,448,128]{2,1,0:T(8,128)(2,1)S(1)}, bf16[4,448,128]{2,1,0:T(8,128)(2,1)S(1)}, u32[]{:S(2)}, u32[]{:S(2)}) %collective-permute-start.14) | collective-permute-done | bytes 458784 | tf_op jit(solution)/shard_map/ppermute | solution.py:149
  107.8 3.7 %shard_map.99 = (bf16[448,1024]{1,0:T(8,128)(2,1)}, f32[448,1024]{1,0:T(8,128)}) custom-call(s32[2]{0:T(128)S(1)} %pad_add_fusion.place, bf16[4,4,2,128,256]{4,3,2,1,0:T(8,128)(2,1)S(1)} %bitcast.24, bf16[4,4,128,256]{3,2,1,0:T(8,128)(2,1)S(1)} %collective-permute-done.13.far, bf16[4,448,128]{2,1,0:T(8,128)(2,1)S(1)} %get-tuple-element.38.mine, ...), custom_call_target="tpu_custom_call" | custom-call | tf_op jit(solution)/shard_map/pallas_call | solution.py:211
  111.5 21.5 %all-to-all-done.1.slices = bf16[32,32,1024]{2,1,0:T(8,128)(2,1)} async-done(((bf16[32,32,1024]{2,1,0:T(8,128)(2,1)}), bf16[32,32,1024]{2,1,0:T(8,128)(2,1)}, u32[]{:S(2)}, u32[]{:S(2)}) %all-to-all-start.1) | async-done | bytes 2097184 | tf_op jit(solution)/shard_map/all_to_all | solution.py:145
  133.0 2.2 %shard_map.98 = bf16[32,1024]{1,0:T(8,128)(2,1)} custom-call(bf16[32,32,1024]{2,1,0:T(8,128)(2,1)} %all-to-all-done.1.slices), custom_call_target="tpu_custom_call" | custom-call | tf_op jit(solution)/shard_map/pallas_call | solution.py:196
  (37 shorter events, 14.5 us)
Async XLA Ops:
  0.6 9.4 %collective-permute-start.1 = (bf16[448,1024]{1,0:T(8,128)(2,1)}, bf16[448,1024]{1,0:T(8,128)(2,1)S(1)}, u32[]{:S(2)}, u32[]{:S(2)}) collective-permute-start(bf16[448,1024]{1,0:T(8,128)(2,1)} %bitcast.27), channel_id=1, source_target_pairs={{0,32},{1,33},{2,34},{3,35},{4,36},{5,37},{6,38},{7,39},{8,40},{9,... | collective-permute-start | bytes 2752520 | tf_op jit(solution)/shard_map/ppermute | solution.py:149
  1.4 8.6 %collective-permute-start = (bf16[128,256]{1,0:T(8,128)(2,1)}, bf16[128,256]{1,0:T(8,128)(2,1)S(1)}, u32[]{:S(2)}, u32[]{:S(2)}) collective-permute-start(bf16[128,256]{1,0:T(8,128)(2,1)} %param.7), channel_id=1, source_target_pairs={{0,16},{1,17},{2,18},{3,19},{4,20},{5,21},{6,22},{7,23},{8,80},{9,... | collective-permute-start | bytes 196616 | tf_op jit(solution)/shard_map/ppermute | solution.py:149
  10.0 6.8 %copy-start.5 = (bf16[448,1024]{1,0:T(8,128)(2,1)}, bf16[448,1024]{1,0:T(8,128)(2,1)S(1)}, u32[]{:S(2)}) copy-start(bf16[448,1024]{1,0:T(8,128)(2,1)S(1)} %collective-permute-done.1.other_weight) | copy-start | bytes 2752516
  10.0 5.1 %collective-permute-start.2 = (bf16[128,256]{1,0:T(8,128)(2,1)S(1)}, bf16[128,256]{1,0:T(8,128)(2,1)S(1)}, u32[]{:S(2)}, u32[]{:S(2)}) collective-permute-start(bf16[128,256]{1,0:T(8,128)(2,1)S(1)} %collective-permute-done), channel_id=1, source_target_pairs={{0,4},{1,5},{2,6},{3,7},{4,0},{5,1},{6,2},{7,3},{8,12},{9,13},{10,... | collective-permute-start | bytes 196616 | tf_op jit(solution)/shard_map/ppermute | solution.py:149
  16.8 30.1 %copy-start.2 = (bf16[1024,448]{0,1:T(8,128)(2,1)S(1)}, bf16[1024,448]{0,1:T(8,128)(2,1)}, u32[]{:S(2)}) copy-start(bf16[1024,448]{0,1:T(8,128)(2,1)} %param.12) | copy-start | bytes 2752516
  16.8 30.1 %all-to-all-start = ((bf16[16,2,128,256]{3,2,1,0:T(8,128)(2,1)}), bf16[16,2,128,256]{3,2,1,0:T(8,128)(2,1)S(1)}, u32[]{:S(2)}, u32[]{:S(2)}) async-start(bf16[16,2,128,256]{3,2,1,0:T(8,128)(2,1)} %broadcast_in_dim.2), calls=%async_computation | async-start | bytes 4194304 | tf_op jit(solution)/shard_map/all_to_all | solution.py:145
  22.3 10.8 %collective-permute-start.5 = (bf16[2,448,128]{2,1,0:T(8,128)(2,1)S(1)}, bf16[2,448,128]{2,1,0:T(8,128)(2,1)S(1)}, u32[]{:S(2)}, u32[]{:S(2)}) collective-permute-start(bf16[2,448,128]{2,1,0:T(8,128)(2,1)S(1)} %pad_maximum_fusion.zero), channel_id=1, source_target_pairs={{0,192},{1,193},{2,194},{3,195},{4,196},{5,197},{6,198},{7,199},{8... | collective-permute-start | bytes 688136 | tf_op jit(solution)/shard_map/ppermute | solution.py:149
  28.9 14.7 %collective-permute-start.4 = (bf16[2,448,128]{2,1,0:T(8,128)(2,1)S(1)}, bf16[2,448,128]{2,1,0:T(8,128)(2,1)}, u32[]{:S(2)}, u32[]{:S(2)}) collective-permute-start(bf16[2,448,128]{2,1,0:T(8,128)(2,1)S(1)} %pad_maximum_fusion.zero), channel_id=1, source_target_pairs={{0,128},{1,129},{2,130},{3,131},{4,132},{5,133},{6,134},{7,135},{8... | collective-permute-start | bytes 688136 | tf_op jit(solution)/shard_map/ppermute | solution.py:149
  28.9 18.0 %collective-permute-start.3 = (bf16[2,448,128]{2,1,0:T(8,128)(2,1)S(1)}, bf16[2,448,128]{2,1,0:T(8,128)(2,1)}, u32[]{:S(2)}, u32[]{:S(2)}) collective-permute-start(bf16[2,448,128]{2,1,0:T(8,128)(2,1)S(1)} %pad_maximum_fusion.zero), channel_id=1, source_target_pairs={{0,64},{1,65},{2,66},{3,67},{4,68},{5,69},{6,70},{7,71},{8,72},{9,... | collective-permute-start | bytes 688136 | tf_op jit(solution)/shard_map/ppermute | solution.py:149
  46.9 1.2 copy-start.6
  51.1 9.8 %collective-permute-start.6 = (bf16[448,128]{1,0:T(8,128)(2,1)S(1)}, bf16[448,128]{1,0:T(8,128)(2,1)S(1)}, u32[]{:S(2)}, u32[]{:S(2)}) collective-permute-start(bf16[448,128]{1,0:T(8,128)(2,1)S(1)} %get-tuple-element.27), channel_id=1, source_target_pairs={{0,64},{1,65},{2,66},{3,67},{4,68},{5,69},{6,70},{7,71},{8,72},{9,... | collective-permute-start | bytes 344072 | tf_op jit(solution)/shard_map/ppermute | solution.py:149
  54.3 9.1 %collective-permute-start.7 = (bf16[448,128]{1,0:T(8,128)(2,1)S(1)}, bf16[448,128]{1,0:T(8,128)(2,1)S(1)}, u32[]{:S(2)}, u32[]{:S(2)}) collective-permute-start(bf16[448,128]{1,0:T(8,128)(2,1)S(1)} %get-tuple-element.28), channel_id=1, source_target_pairs={{0,128},{1,129},{2,130},{3,131},{4,132},{5,133},{6,134},{7,135},{8... | collective-permute-start | bytes 344072 | tf_op jit(solution)/shard_map/ppermute | solution.py:149
  59.5 9.4 %collective-permute-start.8 = (bf16[448,128]{1,0:T(8,128)(2,1)S(1)}, bf16[448,128]{1,0:T(8,128)(2,1)S(1)}, u32[]{:S(2)}, u32[]{:S(2)}) collective-permute-start(bf16[448,128]{1,0:T(8,128)(2,1)S(1)} %get-tuple-element.29), channel_id=1, source_target_pairs={{0,192},{1,193},{2,194},{3,195},{4,196},{5,197},{6,198},{7,199},{8... | collective-permute-start | bytes 344072 | tf_op jit(solution)/shard_map/ppermute | solution.py:149
  69.0 20.6 %copy-start.3 = (bf16[1024,448]{0,1:T(8,128)(2,1)S(1)}, bf16[1024,448]{0,1:T(8,128)(2,1)}, u32[]{:S(2)}) copy-start(bf16[1024,448]{0,1:T(8,128)(2,1)} %param.10) | copy-start | bytes 2752516
  69.0 20.6 %copy-start.4 = (bf16[1024,448]{0,1:T(8,128)(2,1)S(1)}, bf16[1024,448]{0,1:T(8,128)(2,1)}, u32[]{:S(2)}) copy-start(bf16[1024,448]{0,1:T(8,128)(2,1)} %param.11) | copy-start | bytes 2752516
  69.0 5.2 %collective-permute-start.11 = (bf16[448,128]{1,0:T(8,128)(2,1)S(1)}, bf16[448,128]{1,0:T(8,128)(2,1)S(1)}, u32[]{:S(2)}, u32[]{:S(2)}) collective-permute-start(bf16[448,128]{1,0:T(8,128)(2,1)S(1)} %add_convert_fusion.zero), channel_id=1, source_target_pairs={{0,192},{1,193},{2,194},{3,195},{4,196},{5,197},{6,198},{7,199},{8... | collective-permute-start | bytes 344072 | tf_op jit(solution)/shard_map/ppermute | solution.py:149
  69.1 9.0 %collective-permute-start.10 = (bf16[448,128]{1,0:T(8,128)(2,1)S(1)}, bf16[448,128]{1,0:T(8,128)(2,1)S(1)}, u32[]{:S(2)}, u32[]{:S(2)}) collective-permute-start(bf16[448,128]{1,0:T(8,128)(2,1)S(1)} %add_convert_fusion.zero), channel_id=1, source_target_pairs={{0,128},{1,129},{2,130},{3,131},{4,132},{5,133},{6,134},{7,135},{8... | collective-permute-start | bytes 344072 | tf_op jit(solution)/shard_map/ppermute | solution.py:149
  72.7 8.1 %collective-permute-start.9 = (bf16[448,128]{1,0:T(8,128)(2,1)S(1)}, bf16[448,128]{1,0:T(8,128)(2,1)S(1)}, u32[]{:S(2)}, u32[]{:S(2)}) collective-permute-start(bf16[448,128]{1,0:T(8,128)(2,1)S(1)} %add_convert_fusion.zero), channel_id=1, source_target_pairs={{0,64},{1,65},{2,66},{3,67},{4,68},{5,69},{6,70},{7,71},{8,72},{9,... | collective-permute-start | bytes 344072 | tf_op jit(solution)/shard_map/ppermute | solution.py:149
  81.6 7.9 %collective-permute-start.12 = (bf16[4,128,896]{2,1,0:T(8,128)(2,1)S(1)}, bf16[4,128,896]{2,1,0:T(8,128)(2,1)S(1)}, u32[]{:S(2)}, u32[]{:S(2)}) collective-permute-start(bf16[4,128,896]{2,1,0:T(8,128)(2,1)S(1)} %shard_map.96.mine), channel_id=1, source_target_pairs={{0,32},{1,33},{2,34},{3,35},{4,36},{5,37},{6,38},{7,39},{8,40},{9,... | collective-permute-start | bytes 2752520 | tf_op jit(solution)/shard_map/ppermute | solution.py:149
  92.6 1.3 copy-start
  93.9 39.1 %all-to-all-start.1 = ((bf16[32,32,1024]{2,1,0:T(8,128)(2,1)}), bf16[32,32,1024]{2,1,0:T(8,128)(2,1)}, u32[]{:S(2)}, u32[]{:S(2)}) async-start(bf16[32,32,1024]{2,1,0:T(8,128)(2,1)} %bitcast.25), calls=%async_computation.1 | async-start | bytes 4194304 | tf_op jit(solution)/shard_map/all_to_all | solution.py:145
  103.7 4.1 %copy-start.1 = (f32[1024,448]{0,1:T(8,128)S(1)}, f32[1024,448]{0,1:T(8,128)}, u32[]{:S(2)}) copy-start(f32[1024,448]{0,1:T(8,128)} %param.13) | copy-start | bytes 5505028
  103.8 4.0 %collective-permute-start.13 = (bf16[4,4,128,256]{3,2,1,0:T(8,128)(2,1)S(1)}, bf16[4,4,128,256]{3,2,1,0:T(8,128)(2,1)S(1)}, u32[]{:S(2)}, u32[]{:S(2)}) collective-permute-start(bf16[4,4,128,256]{3,2,1,0:T(8,128)(2,1)S(1)} %dynamic-slice_bitcast_fusion), channel_id=1, source_target_pairs={{0,32},{1,33},{2,34},{3,35},{4,36},{5,37},{6,38},{7,39},{8,40},{9,... | collective-permute-start | bytes 3145736 | tf_op jit(solution)/shard_map/ppermute | solution.py:149
  104.8 2.9 %collective-permute-start.14 = (bf16[4,448,128]{2,1,0:T(8,128)(2,1)S(1)}, bf16[4,448,128]{2,1,0:T(8,128)(2,1)S(1)}, u32[]{:S(2)}, u32[]{:S(2)}) collective-permute-start(bf16[4,448,128]{2,1,0:T(8,128)(2,1)S(1)} %get-tuple-element.38.mine), channel_id=1, source_target_pairs={{0,32},{1,33},{2,34},{3,35},{4,36},{5,37},{6,38},{7,39},{8,40},{9,... | collective-permute-start | bytes 1376264 | tf_op jit(solution)/shard_map/ppermute | solution.py:149

commit v5 on v4

--- a/solution.py
+++ b/solution.py
@@ -1,3 +1,5 @@
+import functools
+
 import jax
 import jax.numpy as jnp
 import numpy as np
@@ -102,15 +104,31 @@
         out[group] = both.astype(BF16).T
 
 
-def input_kernel(place, mine, other, gate_weight, up_weight, out):
-    core = place[1]
+def input_kernel(own, place, held, gate_weight, up_weight, *refs):
+    out, part, sem = refs[-3:]
+    which = place[1] if own else 1 - place[1]
+    left = held[...].reshape(512, 896)
     for n in range(4):
         columns = slice(n * 256, (n + 1) * 256)
         right = jnp.concatenate([gate_weight[:, columns], up_weight[:, columns]], axis=0)
-        for held, which in ((mine, core), (other, 1 - core)):
-            total = jnp.dot(held[...].reshape(512, 896), right, preferred_element_type=F32)
-            for zh in range(4):
-                out[zh, which, :, columns] = total[zh * 128 : (zh + 1) * 128].astype(BF16)
+        total = jnp.dot(left, right, preferred_element_type=F32)
+        part[:, :, columns] = total.astype(BF16).reshape(4, 128, 256)
+    copy = pltpu.make_async_copy(part, out.at[:, which], sem)
+    copy.start()
+    copy.wait()
+
+
+def second_product(own, place, held, gate_weight, up_weight, *filled):
+    far = pl.BlockSpec(memory_space=pl.ANY)
+    return pl.pallas_call(
+        functools.partial(input_kernel, own),
+        out_shape=shape(4, 2, 128, 1024, kind=BF16),
+        in_specs=[PLACE] + [WHOLE] * 3 + [far] * len(filled),
+        out_specs=far,
+        scratch_shapes=[pltpu.VMEM((4, 128, 1024), BF16), pltpu.SemaphoreType.DMA],
+        input_output_aliases={4: 0} if filled else {},
+        compiler_params=pltpu.CompilerParams(vmem_limit_bytes=LIMIT),
+    )(place, held, gate_weight, up_weight, *filled)
 
 
 def momentum_kernel(place, slots, far, mine, other, momentum, direction, new_momentum):
@@ -187,11 +205,9 @@
         (place, total, *around(total), by_gate, by_up),
     )
     other = moved(mine, OTHER_CORE)
-    partial = call(
-        input_kernel,
-        shape(4, 2, 128, 1024, kind=BF16),
-        (place, mine, other, gate_weight.T, up_weight.T),
-    )
+    weights = gate_weight.T, up_weight.T
+    partial = second_product(True, place, mine, *weights)
+    partial = second_product(False, place, other, *weights, partial)
     slices = exchange(partial.reshape(32, 32, 1024), TENSOR)
     d_in = pl.pallas_call(
         sum_kernel,

time: 136 us -> 133 us (0.978)
  starting transfers between devices: 52.7 us -> 50.6 us
  waiting for transfers between devices: 62 us -> 60.3 us
    pallas_call x0 -> x2, Pallas kernels: none -> 3.76 us  [second_product(): pl.pallas_call(functools.partial(input_kernel, own), out_shape=shape(4, 2...]
    pallas_call x3 -> x2, Pallas kernels: 5.42 us -> 2.35 us  [call(): pl.pallas_call(kernel, out_shape=out_shape, in_specs=[PLACE] + [WHOLE] *...]
    ppermute x15, waiting for transfers between devices: 40.5 us -> 38.8 us  [moved(): return lax.ppermute(block, AXES, route)]
    all_to_all x2, starting transfers between devices: 15.3 us -> 13.7 us  [exchange(): return lax.all_to_all(slots, axes, split_axis=0, concat_axis=0, tiled=True)]
  transfers between devices with their start and end apart: 17 -> 17, of which waited for: 12 -> 13; matrix products, arithmetic and copies ran while one was open for 1% -> 1% of each run, Pallas kernels for 4% -> 5%
where the time goes in v5:
time: 133 us; the launch traced here: 132 us
  waiting for transfers between devices  60.3 us (45%)
  starting transfers between devices  50.6 us (38%)
  Pallas kernels  15.1 us (11%)
  local copies, waits for them, and re-layouts  4.17 us (3%)
    ppermute x15, waiting for transfers between devices, moved(): return lax.ppermute(block, AXES, route)  38.8 us
    ppermute x15, starting transfers between devices, moved(): return lax.ppermute(block, AXES, route)  36.9 us
    all_to_all x2, waiting for transfers between devices, exchange(): return lax.all_to_all(slots, axes, split_axis=0, concat_axis=0, tiled=True)  21.5 us
    all_to_all x2, starting transfers between devices, exchange(): return lax.all_to_all(slots, axes, split_axis=0, concat_axis=0, tiled=True)  13.7 us
    pallas_call x2, Pallas kernels, second_product(): pl.pallas_call(functools.partial(input_kernel, own), out_shape=shape(4, 2...  3.76 us
    pallas_call x1, Pallas kernels, body(): pl.pallas_call(momentum_kernel, grid=(4,), out_shape=(shape(448, 1024, ki...  3.74 us
    pallas_call x1, Pallas kernels, first_product(): pl.pallas_call(product_kernel, out_shape=(shape(448, 128),) + (shape(448,...  2.99 us
  transfers between devices with their start and end apart: 17, of which 13 were waited for; matrix products, arithmetic and copies ran while one was open for 1% of the time, Pallas kernels for 5%

profile of v5, /device:TPU:3, one launch (start us, length us, event | category | flops | bytes accessed | tf_op | source)
XLA Modules:
  0.0 132.2 jit_solution(6678963605814087248)
XLA Ops:
  1.4 3.9 %collective-permute-start = (bf16[128,256]{1,0:T(8,128)(2,1)}, bf16[128,256]{1,0:T(8,128)(2,1)S(1)}, u32[]{:S(2)}, u32[]{:S(2)}) collective-permute-start(bf16[128,256]{1,0:T(8,128)(2,1)} %param.7), channel_id=1, source_target_pairs={{0,16},{1,17},{2,18},{3,19},{4,20},{5,21},{6,22},{7,23},{8,80},{9,... | collective-permute-start | bytes 196616 | tf_op jit(solution)/shard_map/ppermute | solution.py:167
  6.3 3.7 %collective-permute-done = bf16[128,256]{1,0:T(8,128)(2,1)S(1)} collective-permute-done((bf16[128,256]{1,0:T(8,128)(2,1)}, bf16[128,256]{1,0:T(8,128)(2,1)S(1)}, u32[]{:S(2)}, u32[]{:S(2)}) %collective-permute-start) | collective-permute-done | bytes 65568 | tf_op jit(solution)/shard_map/ppermute | solution.py:167
  10.0 3.5 %collective-permute-start.2 = (bf16[128,256]{1,0:T(8,128)(2,1)S(1)}, bf16[128,256]{1,0:T(8,128)(2,1)S(1)}, u32[]{:S(2)}, u32[]{:S(2)}) collective-permute-start(bf16[128,256]{1,0:T(8,128)(2,1)S(1)} %collective-permute-done), channel_id=1, source_target_pairs={{0,4},{1,5},{2,6},{3,7},{4,0},{5,1},{6,2},{7,3},{8,12},{9,13},{10,... | collective-permute-start | bytes 196616 | tf_op jit(solution)/shard_map/ppermute | solution.py:167
  13.5 1.7 %collective-permute-done.2 = bf16[128,256]{1,0:T(8,128)(2,1)S(1)} collective-permute-done((bf16[128,256]{1,0:T(8,128)(2,1)S(1)}, bf16[128,256]{1,0:T(8,128)(2,1)S(1)}, u32[]{:S(2)}, u32[]{:S(2)}) %collective-permute-start.2) | collective-permute-done | bytes 65568 | tf_op jit(solution)/shard_map/ppermute | solution.py:167
  16.8 5.5 %all-to-all-start = ((bf16[16,2,128,256]{3,2,1,0:T(8,128)(2,1)}), bf16[16,2,128,256]{3,2,1,0:T(8,128)(2,1)S(1)}, u32[]{:S(2)}, u32[]{:S(2)}) async-start(bf16[16,2,128,256]{3,2,1,0:T(8,128)(2,1)} %broadcast_in_dim.2), calls=%async_computation | async-start | bytes 4194304 | tf_op jit(solution)/shard_map/all_to_all | solution.py:163
  22.3 2.5 %collective-permute-start.3 = (bf16[2,448,128]{2,1,0:T(8,128)(2,1)S(1)}, bf16[2,448,128]{2,1,0:T(8,128)(2,1)S(1)}, u32[]{:S(2)}, u32[]{:S(2)}) collective-permute-start(bf16[2,448,128]{2,1,0:T(8,128)(2,1)S(1)} %pad_maximum_fusion.zero), channel_id=1, source_target_pairs={{0,64},{1,65},{2,66},{3,67},{4,68},{5,69},{6,70},{7,71},{8,72},{9,... | collective-permute-start | bytes 688136 | tf_op jit(solution)/shard_map/ppermute | solution.py:167
  24.8 6.2 %collective-permute-start.4 = (bf16[2,448,128]{2,1,0:T(8,128)(2,1)S(1)}, bf16[2,448,128]{2,1,0:T(8,128)(2,1)}, u32[]{:S(2)}, u32[]{:S(2)}) collective-permute-start(bf16[2,448,128]{2,1,0:T(8,128)(2,1)S(1)} %pad_maximum_fusion.zero), channel_id=1, source_target_pairs={{0,128},{1,129},{2,130},{3,131},{4,132},{5,133},{6,134},{7,135},{8... | collective-permute-start | bytes 688136 | tf_op jit(solution)/shard_map/ppermute | solution.py:167
  32.5 3.8 %collective-permute-done.3.one = bf16[2,448,128]{2,1,0:T(8,128)(2,1)S(1)} collective-permute-done((bf16[2,448,128]{2,1,0:T(8,128)(2,1)S(1)}, bf16[2,448,128]{2,1,0:T(8,128)(2,1)S(1)}, u32[]{:S(2)}, u32[]{:S(2)}) %collective-permute-start.3) | collective-permute-done | bytes 229408 | tf_op jit(solution)/shard_map/ppermute | solution.py:167
  36.2 9.4 %collective-permute-done.4.two = bf16[2,448,128]{2,1,0:T(8,128)(2,1)} collective-permute-done((bf16[2,448,128]{2,1,0:T(8,128)(2,1)S(1)}, bf16[2,448,128]{2,1,0:T(8,128)(2,1)}, u32[]{:S(2)}, u32[]{:S(2)}) %collective-permute-start.4) | collective-permute-done | bytes 229408 | tf_op jit(solution)/shard_map/ppermute | solution.py:167
  45.7 5.0 %collective-permute-done.5.three = bf16[2,448,128]{2,1,0:T(8,128)(2,1)} collective-permute-done((bf16[2,448,128]{2,1,0:T(8,128)(2,1)S(1)}, bf16[2,448,128]{2,1,0:T(8,128)(2,1)}, u32[]{:S(2)}, u32[]{:S(2)}) %collective-permute-start.5) | collective-permute-done | bytes 229408 | tf_op jit(solution)/shard_map/ppermute | solution.py:167
  51.8 3.0 %shard_map.94 = (f32[448,128]{1,0:T(8,128)S(1)}, bf16[448,128]{1,0:T(8,128)(2,1)S(1)}, bf16[448,128]{1,0:T(8,128)(2,1)S(1)}, bf16[448,128]{1,0:T(8,128)(2,1)S(1)}) custom-call(s32[2]{0:T(128)S(1)} %pad_add_fusion.place, bf16[4,4,2,128,256]{4,3,2,1,0:T(8,128)(2,1)S(1)} %bitcast.22, bf16[448,1024]{1,0:T(8,128)(2,1)S(1)} %bitcast.32, ...), custom_call_target="tpu_custom_call" | custom-call | tf_op jit(solution)/shard_map/pallas_call | solution.py:78
  56.1 4.3 %collective-permute-start.7 = (bf16[448,128]{1,0:T(8,128)(2,1)S(1)}, bf16[448,128]{1,0:T(8,128)(2,1)S(1)}, u32[]{:S(2)}, u32[]{:S(2)}) collective-permute-start(bf16[448,128]{1,0:T(8,128)(2,1)S(1)} %get-tuple-element.28), channel_id=1, source_target_pairs={{0,128},{1,129},{2,130},{3,131},{4,132},{5,133},{6,134},{7,135},{8... | collective-permute-start | bytes 344072 | tf_op jit(solution)/shard_map/ppermute | solution.py:167
  61.7 5.0 %collective-permute-done.7 = bf16[448,128]{1,0:T(8,128)(2,1)S(1)} collective-permute-done((bf16[448,128]{1,0:T(8,128)(2,1)S(1)}, bf16[448,128]{1,0:T(8,128)(2,1)S(1)}, u32[]{:S(2)}, u32[]{:S(2)}) %collective-permute-start.7) | collective-permute-done | bytes 114720 | tf_op jit(solution)/shard_map/ppermute | solution.py:167
  68.2 4.8 %collective-permute-start.10 = (bf16[448,128]{1,0:T(8,128)(2,1)S(1)}, bf16[448,128]{1,0:T(8,128)(2,1)S(1)}, u32[]{:S(2)}, u32[]{:S(2)}) collective-permute-start(bf16[448,128]{1,0:T(8,128)(2,1)S(1)} %add_convert_fusion.zero), channel_id=1, source_target_pairs={{0,128},{1,129},{2,130},{3,131},{4,132},{5,133},{6,134},{7,135},{8... | collective-permute-start | bytes 344072 | tf_op jit(solution)/shard_map/ppermute | solution.py:167
  73.5 1.8 %collective-permute-start.9 = (bf16[448,128]{1,0:T(8,128)(2,1)S(1)}, bf16[448,128]{1,0:T(8,128)(2,1)S(1)}, u32[]{:S(2)}, u32[]{:S(2)}) collective-permute-start(bf16[448,128]{1,0:T(8,128)(2,1)S(1)} %add_convert_fusion.zero), channel_id=1, source_target_pairs={{0,64},{1,65},{2,66},{3,67},{4,68},{5,69},{6,70},{7,71},{8,72},{9,... | collective-permute-start | bytes 344072 | tf_op jit(solution)/shard_map/ppermute | solution.py:167
  78.0 3.9 %collective-permute-done.9.one = bf16[448,128]{1,0:T(8,128)(2,1)S(1)} collective-permute-done((bf16[448,128]{1,0:T(8,128)(2,1)S(1)}, bf16[448,128]{1,0:T(8,128)(2,1)S(1)}, u32[]{:S(2)}, u32[]{:S(2)}) %collective-permute-start.9) | collective-permute-done | bytes 114720 | tf_op jit(solution)/shard_map/ppermute | solution.py:167
  82.7 4.3 %collective-permute-start.12 = (bf16[4,128,896]{2,1,0:T(8,128)(2,1)S(1)}, bf16[4,128,896]{2,1,0:T(8,128)(2,1)S(1)}, u32[]{:S(2)}, u32[]{:S(2)}) collective-permute-start(bf16[4,128,896]{2,1,0:T(8,128)(2,1)S(1)} %shard_map.96.held), channel_id=1, source_target_pairs={{0,32},{1,33},{2,34},{3,35},{4,36},{5,37},{6,38},{7,39},{8,40},{9,... | collective-permute-start | bytes 2752520 | tf_op jit(solution)/shard_map/ppermute | solution.py:167
  87.0 1.9 %shard_map.97.refs_0_ = bf16[4,2,128,1024]{3,2,1,0:T(8,128)(2,1)S(1)} custom-call(s32[2]{0:T(128)S(1)} %pad_add_fusion.place, bf16[4,128,896]{2,1,0:T(8,128)(2,1)S(1)} %shard_map.96.held, bf16[448,1024]{1,0:T(8,128)(2,1)S(1)} %bitcast.26, bf16[448,1024]{1,0:T(8,128)(2,1)S(1)} %bitcast.28), custom_call_target="tpu_custom_call" | custom-call | tf_op jit(solution)/shard_map/pallas_call | solution.py:123
  89.1 1.9 %shard_map.98 = bf16[4,2,128,1024]{3,2,1,0:T(8,128)(2,1)S(1)} custom-call(s32[2]{0:T(128)S(1)} %pad_add_fusion.place, bf16[4,128,896]{2,1,0:T(8,128)(2,1)S(1)} %collective-permute-done.12.held, bf16[448,1024]{1,0:T(8,128)(2,1)S(1)} %bitcast.27, bf16[448,1024]{1,0:T(8,128)(2,1)S(1)} %bitcast.29, ...), custom_call_target="tpu_custom_call", output_to_operand_aliasing={{}: (4, {})} | custom-call | tf_op jit(solution)/shard_map/pallas_call | solution.py:123
  92.3 8.2 %all-to-all-start.1 = ((bf16[32,32,1024]{2,1,0:T(8,128)(2,1)}), bf16[32,32,1024]{2,1,0:T(8,128)(2,1)}, u32[]{:S(2)}, u32[]{:S(2)}) async-start(bf16[32,32,1024]{2,1,0:T(8,128)(2,1)} %bitcast.25), calls=%async_computation.1 | async-start | bytes 4194304 | tf_op jit(solution)/shard_map/all_to_all | solution.py:163
  101.7 2.8 %collective-permute-done.14.other = bf16[4,448,128]{2,1,0:T(8,128)(2,1)S(1)} collective-permute-done((bf16[4,448,128]{2,1,0:T(8,128)(2,1)S(1)}, bf16[4,448,128]{2,1,0:T(8,128)(2,1)S(1)}, u32[]{:S(2)}, u32[]{:S(2)}) %collective-permute-start.14) | collective-permute-done | bytes 458784 | tf_op jit(solution)/shard_map/ppermute | solution.py:167
  104.6 3.7 %shard_map.100 = (bf16[448,1024]{1,0:T(8,128)(2,1)}, f32[448,1024]{1,0:T(8,128)}) custom-call(s32[2]{0:T(128)S(1)} %pad_add_fusion.place, bf16[4,4,2,128,256]{4,3,2,1,0:T(8,128)(2,1)S(1)} %bitcast.24, bf16[4,4,128,256]{3,2,1,0:T(8,128)(2,1)S(1)} %collective-permute-done.13.far, bf16[4,448,128]{2,1,0:T(8,128)(2,1)S(1)} %get-tuple-element.38.mine, ...), custom_call_target="tpu_custom_call" | custom-call | tf_op jit(solution)/shard_map/pallas_call | solution.py:227
  108.3 21.5 %all-to-all-done.1.slices = bf16[32,32,1024]{2,1,0:T(8,128)(2,1)} async-done(((bf16[32,32,1024]{2,1,0:T(8,128)(2,1)}), bf16[32,32,1024]{2,1,0:T(8,128)(2,1)}, u32[]{:S(2)}, u32[]{:S(2)}) %all-to-all-start.1) | async-done | bytes 2097184 | tf_op jit(solution)/shard_map/all_to_all | solution.py:163
  129.8 2.2 %shard_map.99 = bf16[32,1024]{1,0:T(8,128)(2,1)} custom-call(bf16[32,32,1024]{2,1,0:T(8,128)(2,1)} %all-to-all-done.1.slices), custom_call_target="tpu_custom_call" | custom-call | tf_op jit(solution)/shard_map/pallas_call | solution.py:212
  (38 shorter events, 16.7 us)
Async XLA Ops:
  0.6 9.4 %collective-permute-start.1 = (bf16[448,1024]{1,0:T(8,128)(2,1)}, bf16[448,1024]{1,0:T(8,128)(2,1)S(1)}, u32[]{:S(2)}, u32[]{:S(2)}) collective-permute-start(bf16[448,1024]{1,0:T(8,128)(2,1)} %bitcast.31), channel_id=1, source_target_pairs={{0,32},{1,33},{2,34},{3,35},{4,36},{5,37},{6,38},{7,39},{8,40},{9,... | collective-permute-start | bytes 2752520 | tf_op jit(solution)/shard_map/ppermute | solution.py:167
  1.4 8.6 %collective-permute-start = (bf16[128,256]{1,0:T(8,128)(2,1)}, bf16[128,256]{1,0:T(8,128)(2,1)S(1)}, u32[]{:S(2)}, u32[]{:S(2)}) collective-permute-start(bf16[128,256]{1,0:T(8,128)(2,1)} %param.7), channel_id=1, source_target_pairs={{0,16},{1,17},{2,18},{3,19},{4,20},{5,21},{6,22},{7,23},{8,80},{9,... | collective-permute-start | bytes 196616 | tf_op jit(solution)/shard_map/ppermute | solution.py:167
  10.0 6.8 %copy-start.5 = (bf16[448,1024]{1,0:T(8,128)(2,1)}, bf16[448,1024]{1,0:T(8,128)(2,1)S(1)}, u32[]{:S(2)}) copy-start(bf16[448,1024]{1,0:T(8,128)(2,1)S(1)} %collective-permute-done.1.other_weight) | copy-start | bytes 2752516
  10.0 5.1 %collective-permute-start.2 = (bf16[128,256]{1,0:T(8,128)(2,1)S(1)}, bf16[128,256]{1,0:T(8,128)(2,1)S(1)}, u32[]{:S(2)}, u32[]{:S(2)}) collective-permute-start(bf16[128,256]{1,0:T(8,128)(2,1)S(1)} %collective-permute-done), channel_id=1, source_target_pairs={{0,4},{1,5},{2,6},{3,7},{4,0},{5,1},{6,2},{7,3},{8,12},{9,13},{10,... | collective-permute-start | bytes 196616 | tf_op jit(solution)/shard_map/ppermute | solution.py:167
  16.8 33.9 %copy-start.4 = (bf16[1024,448]{0,1:T(8,128)(2,1)S(1)}, bf16[1024,448]{0,1:T(8,128)(2,1)}, u32[]{:S(2)}) copy-start(bf16[1024,448]{0,1:T(8,128)(2,1)} %param.12) | copy-start | bytes 2752516
  16.8 33.8 %all-to-all-start = ((bf16[16,2,128,256]{3,2,1,0:T(8,128)(2,1)}), bf16[16,2,128,256]{3,2,1,0:T(8,128)(2,1)S(1)}, u32[]{:S(2)}, u32[]{:S(2)}) async-start(bf16[16,2,128,256]{3,2,1,0:T(8,128)(2,1)} %broadcast_in_dim.2), calls=%async_computation | async-start | bytes 4194304 | tf_op jit(solution)/shard_map/all_to_all | solution.py:163
  22.3 13.9 %collective-permute-start.3 = (bf16[2,448,128]{2,1,0:T(8,128)(2,1)S(1)}, bf16[2,448,128]{2,1,0:T(8,128)(2,1)S(1)}, u32[]{:S(2)}, u32[]{:S(2)}) collective-permute-start(bf16[2,448,128]{2,1,0:T(8,128)(2,1)S(1)} %pad_maximum_fusion.zero), channel_id=1, source_target_pairs={{0,64},{1,65},{2,66},{3,67},{4,68},{5,69},{6,70},{7,71},{8,72},{9,... | collective-permute-start | bytes 688136 | tf_op jit(solution)/shard_map/ppermute | solution.py:167
  24.8 20.9 %collective-permute-start.4 = (bf16[2,448,128]{2,1,0:T(8,128)(2,1)S(1)}, bf16[2,448,128]{2,1,0:T(8,128)(2,1)}, u32[]{:S(2)}, u32[]{:S(2)}) collective-permute-start(bf16[2,448,128]{2,1,0:T(8,128)(2,1)S(1)} %pad_maximum_fusion.zero), channel_id=1, source_target_pairs={{0,128},{1,129},{2,130},{3,131},{4,132},{5,133},{6,134},{7,135},{8... | collective-permute-start | bytes 688136 | tf_op jit(solution)/shard_map/ppermute | solution.py:167
  31.0 19.7 %collective-permute-start.5 = (bf16[2,448,128]{2,1,0:T(8,128)(2,1)S(1)}, bf16[2,448,128]{2,1,0:T(8,128)(2,1)}, u32[]{:S(2)}, u32[]{:S(2)}) collective-permute-start(bf16[2,448,128]{2,1,0:T(8,128)(2,1)S(1)} %pad_maximum_fusion.zero), channel_id=1, source_target_pairs={{0,192},{1,193},{2,194},{3,195},{4,196},{5,197},{6,198},{7,199},{8... | collective-permute-start | bytes 688136 | tf_op jit(solution)/shard_map/ppermute | solution.py:167
  50.7 1.2 copy-start.6
  54.8 6.9 %collective-permute-start.6 = (bf16[448,128]{1,0:T(8,128)(2,1)S(1)}, bf16[448,128]{1,0:T(8,128)(2,1)S(1)}, u32[]{:S(2)}, u32[]{:S(2)}) collective-permute-start(bf16[448,128]{1,0:T(8,128)(2,1)S(1)} %get-tuple-element.27), channel_id=1, source_target_pairs={{0,64},{1,65},{2,66},{3,67},{4,68},{5,69},{6,70},{7,71},{8,72},{9,... | collective-permute-start | bytes 344072 | tf_op jit(solution)/shard_map/ppermute | solution.py:167
  56.1 10.7 %collective-permute-start.7 = (bf16[448,128]{1,0:T(8,128)(2,1)S(1)}, bf16[448,128]{1,0:T(8,128)(2,1)S(1)}, u32[]{:S(2)}, u32[]{:S(2)}) collective-permute-start(bf16[448,128]{1,0:T(8,128)(2,1)S(1)} %get-tuple-element.28), channel_id=1, source_target_pairs={{0,128},{1,129},{2,130},{3,131},{4,132},{5,133},{6,134},{7,135},{8... | collective-permute-start | bytes 344072 | tf_op jit(solution)/shard_map/ppermute | solution.py:167
  60.4 7.7 %collective-permute-start.8 = (bf16[448,128]{1,0:T(8,128)(2,1)S(1)}, bf16[448,128]{1,0:T(8,128)(2,1)S(1)}, u32[]{:S(2)}, u32[]{:S(2)}) collective-permute-start(bf16[448,128]{1,0:T(8,128)(2,1)S(1)} %get-tuple-element.29), channel_id=1, source_target_pairs={{0,192},{1,193},{2,194},{3,195},{4,196},{5,197},{6,198},{7,199},{8... | collective-permute-start | bytes 344072 | tf_op jit(solution)/shard_map/ppermute | solution.py:167
  68.2 18.9 %copy-start.1 = (bf16[1024,448]{0,1:T(8,128)(2,1)S(1)}, bf16[1024,448]{0,1:T(8,128)(2,1)}, u32[]{:S(2)}) copy-start(bf16[1024,448]{0,1:T(8,128)(2,1)} %param.10) | copy-start | bytes 2752516
  68.2 18.9 %copy-start.2 = (bf16[1024,448]{0,1:T(8,128)(2,1)S(1)}, bf16[1024,448]{0,1:T(8,128)(2,1)}, u32[]{:S(2)}) copy-start(bf16[1024,448]{0,1:T(8,128)(2,1)} %param.11) | copy-start | bytes 2752516
  68.2 8.7 %collective-permute-start.10 = (bf16[448,128]{1,0:T(8,128)(2,1)S(1)}, bf16[448,128]{1,0:T(8,128)(2,1)S(1)}, u32[]{:S(2)}, u32[]{:S(2)}) collective-permute-start(bf16[448,128]{1,0:T(8,128)(2,1)S(1)} %add_convert_fusion.zero), channel_id=1, source_target_pairs={{0,128},{1,129},{2,130},{3,131},{4,132},{5,133},{6,134},{7,135},{8... | collective-permute-start | bytes 344072 | tf_op jit(solution)/shard_map/ppermute | solution.py:167
  73.0 5.0 %collective-permute-start.11 = (bf16[448,128]{1,0:T(8,128)(2,1)S(1)}, bf16[448,128]{1,0:T(8,128)(2,1)S(1)}, u32[]{:S(2)}, u32[]{:S(2)}) collective-permute-start(bf16[448,128]{1,0:T(8,128)(2,1)S(1)} %add_convert_fusion.zero), channel_id=1, source_target_pairs={{0,192},{1,193},{2,194},{3,195},{4,196},{5,197},{6,198},{7,199},{8... | collective-permute-start | bytes 344072 | tf_op jit(solution)/shard_map/ppermute | solution.py:167
  73.5 8.4 %collective-permute-start.9 = (bf16[448,128]{1,0:T(8,128)(2,1)S(1)}, bf16[448,128]{1,0:T(8,128)(2,1)S(1)}, u32[]{:S(2)}, u32[]{:S(2)}) collective-permute-start(bf16[448,128]{1,0:T(8,128)(2,1)S(1)} %add_convert_fusion.zero), channel_id=1, source_target_pairs={{0,64},{1,65},{2,66},{3,67},{4,68},{5,69},{6,70},{7,71},{8,72},{9,... | collective-permute-start | bytes 344072 | tf_op jit(solution)/shard_map/ppermute | solution.py:167
  82.7 6.4 %collective-permute-start.12 = (bf16[4,128,896]{2,1,0:T(8,128)(2,1)S(1)}, bf16[4,128,896]{2,1,0:T(8,128)(2,1)S(1)}, u32[]{:S(2)}, u32[]{:S(2)}) collective-permute-start(bf16[4,128,896]{2,1,0:T(8,128)(2,1)S(1)} %shard_map.96.held), channel_id=1, source_target_pairs={{0,32},{1,33},{2,34},{3,35},{4,36},{5,37},{6,38},{7,39},{8,40},{9,... | collective-permute-start | bytes 2752520 | tf_op jit(solution)/shard_map/ppermute | solution.py:167
  91.0 1.3 copy-start
  92.3 37.5 %all-to-all-start.1 = ((bf16[32,32,1024]{2,1,0:T(8,128)(2,1)}), bf16[32,32,1024]{2,1,0:T(8,128)(2,1)}, u32[]{:S(2)}, u32[]{:S(2)}) async-start(bf16[32,32,1024]{2,1,0:T(8,128)(2,1)} %bitcast.25), calls=%async_computation.1 | async-start | bytes 4194304 | tf_op jit(solution)/shard_map/all_to_all | solution.py:163
  100.5 4.1 %copy-start.3 = (f32[1024,448]{0,1:T(8,128)S(1)}, f32[1024,448]{0,1:T(8,128)}, u32[]{:S(2)}) copy-start(f32[1024,448]{0,1:T(8,128)} %param.13) | copy-start | bytes 5505028
  100.6 4.0 %collective-permute-start.13 = (bf16[4,4,128,256]{3,2,1,0:T(8,128)(2,1)S(1)}, bf16[4,4,128,256]{3,2,1,0:T(8,128)(2,1)S(1)}, u32[]{:S(2)}, u32[]{:S(2)}) collective-permute-start(bf16[4,4,128,256]{3,2,1,0:T(8,128)(2,1)S(1)} %dynamic-slice_bitcast_fusion), channel_id=1, source_target_pairs={{0,32},{1,33},{2,34},{3,35},{4,36},{5,37},{6,38},{7,39},{8,40},{9,... | collective-permute-start | bytes 3145736 | tf_op jit(solution)/shard_map/ppermute | solution.py:167
  101.6 2.9 %collective-permute-start.14 = (bf16[4,448,128]{2,1,0:T(8,128)(2,1)S(1)}, bf16[4,448,128]{2,1,0:T(8,128)(2,1)S(1)}, u32[]{:S(2)}, u32[]{:S(2)}) collective-permute-start(bf16[4,448,128]{2,1,0:T(8,128)(2,1)S(1)} %get-tuple-element.38.mine), channel_id=1, source_target_pairs={{0,32},{1,33},{2,34},{3,35},{4,36},{5,37},{6,38},{7,39},{8,40},{9,... | collective-permute-start | bytes 1376264 | tf_op jit(solution)/shard_map/ppermute | solution.py:167

commit v6 on v5

--- a/solution.py
+++ b/solution.py
@@ -105,17 +105,19 @@
 
 
 def input_kernel(own, place, held, gate_weight, up_weight, *refs):
-    out, part, sem = refs[-3:]
+    out, part, sems = refs[-3:]
+    copies = []
     which = place[1] if own else 1 - place[1]
     left = held[...].reshape(512, 896)
     for n in range(4):
         columns = slice(n * 256, (n + 1) * 256)
         right = jnp.concatenate([gate_weight[:, columns], up_weight[:, columns]], axis=0)
         total = jnp.dot(left, right, preferred_element_type=F32)
-        part[:, :, columns] = total.astype(BF16).reshape(4, 128, 256)
-    copy = pltpu.make_async_copy(part, out.at[:, which], sem)
-    copy.start()
-    copy.wait()
+        part[n] = total.astype(BF16).reshape(4, 128, 256)
+        copies.append(pltpu.make_async_copy(part.at[n], out.at[:, which, :, columns], sems.at[n]))
+        copies[-1].start()
+    for copy in copies:
+        copy.wait()
 
 
 def second_product(own, place, held, gate_weight, up_weight, *filled):
@@ -125,7 +127,7 @@
         out_shape=shape(4, 2, 128, 1024, kind=BF16),
         in_specs=[PLACE] + [WHOLE] * 3 + [far] * len(filled),
         out_specs=far,
-        scratch_shapes=[pltpu.VMEM((4, 128, 1024), BF16), pltpu.SemaphoreType.DMA],
+        scratch_shapes=[pltpu.VMEM((4, 4, 128, 256), BF16), pltpu.SemaphoreType.DMA((4,))],
         input_output_aliases={4: 0} if filled else {},
         compiler_params=pltpu.CompilerParams(vmem_limit_bytes=LIMIT),
     )(place, held, gate_weight, up_weight, *filled)

time: 133 us -> 136 us (1.023)
  Pallas kernels: 15.1 us -> 18.3 us
    pallas_call x2, Pallas kernels: 3.76 us -> 6.99 us  [second_product(): pl.pallas_call(functools.partial(input_kernel, own), out_shape=shape(4, 2...]
  transfers between devices with their start and end apart: 17 -> 17, of which waited for: 13 -> 12; matrix products, arithmetic and copies ran while one was open for 1% -> 1% of each run, Pallas kernels for 5% -> 6%
where the time goes in v6:
time: 136 us; the launch traced here: 135 us
  waiting for transfers between devices  60.3 us (44%)
  starting transfers between devices  50.2 us (37%)
  Pallas kernels  18.3 us (13%)
  local copies, waits for them, and re-layouts  4.17 us (3%)
    ppermute x15, waiting for transfers between devices, moved(): return lax.ppermute(block, AXES, route)  38.6 us
    ppermute x15, starting transfers between devices, moved(): return lax.ppermute(block, AXES, route)  36.5 us
    all_to_all x2, waiting for transfers between devices, exchange(): return lax.all_to_all(slots, axes, split_axis=0, concat_axis=0, tiled=True)  21.7 us
    all_to_all x2, starting transfers between devices, exchange(): return lax.all_to_all(slots, axes, split_axis=0, concat_axis=0, tiled=True)  13.7 us
    pallas_call x2, Pallas kernels, second_product(): pl.pallas_call(functools.partial(input_kernel, own), out_shape=shape(4, 2...  6.99 us
    pallas_call x1, Pallas kernels, body(): pl.pallas_call(momentum_kernel, grid=(4,), out_shape=(shape(448, 1024, ki...  3.74 us
    pallas_call x1, Pallas kernels, first_product(): pl.pallas_call(product_kernel, out_shape=(shape(448, 128),) + (shape(448,...  2.99 us
  transfers between devices with their start and end apart: 17, of which 12 were waited for; matrix products, arithmetic and copies ran while one was open for 1% of the time, Pallas kernels for 6%

profile of v6, /device:TPU:3, one launch (start us, length us, event | category | flops | bytes accessed | tf_op | source)
XLA Modules:
  0.0 135.1 jit_solution(10325452439839585491)
XLA Ops:
  1.4 3.9 %collective-permute-start = (bf16[128,256]{1,0:T(8,128)(2,1)}, bf16[128,256]{1,0:T(8,128)(2,1)S(1)}, u32[]{:S(2)}, u32[]{:S(2)}) collective-permute-start(bf16[128,256]{1,0:T(8,128)(2,1)} %param.7), channel_id=1, source_target_pairs={{0,16},{1,17},{2,18},{3,19},{4,20},{5,21},{6,22},{7,23},{8,80},{9,... | collective-permute-start | bytes 196616 | tf_op jit(solution)/shard_map/ppermute | solution.py:169
  6.3 3.7 %collective-permute-done = bf16[128,256]{1,0:T(8,128)(2,1)S(1)} collective-permute-done((bf16[128,256]{1,0:T(8,128)(2,1)}, bf16[128,256]{1,0:T(8,128)(2,1)S(1)}, u32[]{:S(2)}, u32[]{:S(2)}) %collective-permute-start) | collective-permute-done | bytes 65568 | tf_op jit(solution)/shard_map/ppermute | solution.py:169
  10.0 3.5 %collective-permute-start.2 = (bf16[128,256]{1,0:T(8,128)(2,1)S(1)}, bf16[128,256]{1,0:T(8,128)(2,1)S(1)}, u32[]{:S(2)}, u32[]{:S(2)}) collective-permute-start(bf16[128,256]{1,0:T(8,128)(2,1)S(1)} %collective-permute-done), channel_id=1, source_target_pairs={{0,4},{1,5},{2,6},{3,7},{4,0},{5,1},{6,2},{7,3},{8,12},{9,13},{10,... | collective-permute-start | bytes 196616 | tf_op jit(solution)/shard_map/ppermute | solution.py:169
  13.5 1.7 %collective-permute-done.2 = bf16[128,256]{1,0:T(8,128)(2,1)S(1)} collective-permute-done((bf16[128,256]{1,0:T(8,128)(2,1)S(1)}, bf16[128,256]{1,0:T(8,128)(2,1)S(1)}, u32[]{:S(2)}, u32[]{:S(2)}) %collective-permute-start.2) | collective-permute-done | bytes 65568 | tf_op jit(solution)/shard_map/ppermute | solution.py:169
  16.8 5.5 %all-to-all-start = ((bf16[16,2,128,256]{3,2,1,0:T(8,128)(2,1)}), bf16[16,2,128,256]{3,2,1,0:T(8,128)(2,1)S(1)}, u32[]{:S(2)}, u32[]{:S(2)}) async-start(bf16[16,2,128,256]{3,2,1,0:T(8,128)(2,1)} %broadcast_in_dim.2), calls=%async_computation | async-start | bytes 4194304 | tf_op jit(solution)/shard_map/all_to_all | solution.py:165
  22.3 2.5 %collective-permute-start.3 = (bf16[2,448,128]{2,1,0:T(8,128)(2,1)S(1)}, bf16[2,448,128]{2,1,0:T(8,128)(2,1)S(1)}, u32[]{:S(2)}, u32[]{:S(2)}) collective-permute-start(bf16[2,448,128]{2,1,0:T(8,128)(2,1)S(1)} %pad_maximum_fusion.zero), channel_id=1, source_target_pairs={{0,64},{1,65},{2,66},{3,67},{4,68},{5,69},{6,70},{7,71},{8,72},{9,... | collective-permute-start | bytes 688136 | tf_op jit(solution)/shard_map/ppermute | solution.py:169
  24.8 6.2 %collective-permute-start.4 = (bf16[2,448,128]{2,1,0:T(8,128)(2,1)S(1)}, bf16[2,448,128]{2,1,0:T(8,128)(2,1)}, u32[]{:S(2)}, u32[]{:S(2)}) collective-permute-start(bf16[2,448,128]{2,1,0:T(8,128)(2,1)S(1)} %pad_maximum_fusion.zero), channel_id=1, source_target_pairs={{0,128},{1,129},{2,130},{3,131},{4,132},{5,133},{6,134},{7,135},{8... | collective-permute-start | bytes 688136 | tf_op jit(solution)/shard_map/ppermute | solution.py:169
  32.5 3.8 %collective-permute-done.3.one = bf16[2,448,128]{2,1,0:T(8,128)(2,1)S(1)} collective-permute-done((bf16[2,448,128]{2,1,0:T(8,128)(2,1)S(1)}, bf16[2,448,128]{2,1,0:T(8,128)(2,1)S(1)}, u32[]{:S(2)}, u32[]{:S(2)}) %collective-permute-start.3) | collective-permute-done | bytes 229408 | tf_op jit(solution)/shard_map/ppermute | solution.py:169
  36.2 9.4 %collective-permute-done.4.two = bf16[2,448,128]{2,1,0:T(8,128)(2,1)} collective-permute-done((bf16[2,448,128]{2,1,0:T(8,128)(2,1)S(1)}, bf16[2,448,128]{2,1,0:T(8,128)(2,1)}, u32[]{:S(2)}, u32[]{:S(2)}) %collective-permute-start.4) | collective-permute-done | bytes 229408 | tf_op jit(solution)/shard_map/ppermute | solution.py:169
  45.7 5.0 %collective-permute-done.5.three = bf16[2,448,128]{2,1,0:T(8,128)(2,1)} collective-permute-done((bf16[2,448,128]{2,1,0:T(8,128)(2,1)S(1)}, bf16[2,448,128]{2,1,0:T(8,128)(2,1)}, u32[]{:S(2)}, u32[]{:S(2)}) %collective-permute-start.5) | collective-permute-done | bytes 229408 | tf_op jit(solution)/shard_map/ppermute | solution.py:169
  51.8 3.0 %shard_map.94 = (f32[448,128]{1,0:T(8,128)S(1)}, bf16[448,128]{1,0:T(8,128)(2,1)S(1)}, bf16[448,128]{1,0:T(8,128)(2,1)S(1)}, bf16[448,128]{1,0:T(8,128)(2,1)S(1)}) custom-call(s32[2]{0:T(128)S(1)} %pad_add_fusion.place, bf16[4,4,2,128,256]{4,3,2,1,0:T(8,128)(2,1)S(1)} %bitcast.22, bf16[448,1024]{1,0:T(8,128)(2,1)S(1)} %bitcast.32, ...), custom_call_target="tpu_custom_call" | custom-call | tf_op jit(solution)/shard_map/pallas_call | solution.py:78
  56.1 4.3 %collective-permute-start.7 = (bf16[448,128]{1,0:T(8,128)(2,1)S(1)}, bf16[448,128]{1,0:T(8,128)(2,1)S(1)}, u32[]{:S(2)}, u32[]{:S(2)}) collective-permute-start(bf16[448,128]{1,0:T(8,128)(2,1)S(1)} %get-tuple-element.28), channel_id=1, source_target_pairs={{0,128},{1,129},{2,130},{3,131},{4,132},{5,133},{6,134},{7,135},{8... | collective-permute-start | bytes 344072 | tf_op jit(solution)/shard_map/ppermute | solution.py:169
  61.7 5.0 %collective-permute-done.7 = bf16[448,128]{1,0:T(8,128)(2,1)S(1)} collective-permute-done((bf16[448,128]{1,0:T(8,128)(2,1)S(1)}, bf16[448,128]{1,0:T(8,128)(2,1)S(1)}, u32[]{:S(2)}, u32[]{:S(2)}) %collective-permute-start.7) | collective-permute-done | bytes 114720 | tf_op jit(solution)/shard_map/ppermute | solution.py:169
  68.2 4.8 %collective-permute-start.10 = (bf16[448,128]{1,0:T(8,128)(2,1)S(1)}, bf16[448,128]{1,0:T(8,128)(2,1)S(1)}, u32[]{:S(2)}, u32[]{:S(2)}) collective-permute-start(bf16[448,128]{1,0:T(8,128)(2,1)S(1)} %add_convert_fusion.zero), channel_id=1, source_target_pairs={{0,128},{1,129},{2,130},{3,131},{4,132},{5,133},{6,134},{7,135},{8... | collective-permute-start | bytes 344072 | tf_op jit(solution)/shard_map/ppermute | solution.py:169
  73.5 1.8 %collective-permute-start.9 = (bf16[448,128]{1,0:T(8,128)(2,1)S(1)}, bf16[448,128]{1,0:T(8,128)(2,1)S(1)}, u32[]{:S(2)}, u32[]{:S(2)}) collective-permute-start(bf16[448,128]{1,0:T(8,128)(2,1)S(1)} %add_convert_fusion.zero), channel_id=1, source_target_pairs={{0,64},{1,65},{2,66},{3,67},{4,68},{5,69},{6,70},{7,71},{8,72},{9,... | collective-permute-start | bytes 344072 | tf_op jit(solution)/shard_map/ppermute | solution.py:169
  78.0 3.9 %collective-permute-done.9.one = bf16[448,128]{1,0:T(8,128)(2,1)S(1)} collective-permute-done((bf16[448,128]{1,0:T(8,128)(2,1)S(1)}, bf16[448,128]{1,0:T(8,128)(2,1)S(1)}, u32[]{:S(2)}, u32[]{:S(2)}) %collective-permute-start.9) | collective-permute-done | bytes 114720 | tf_op jit(solution)/shard_map/ppermute | solution.py:169
  82.7 4.3 %collective-permute-start.12 = (bf16[4,128,896]{2,1,0:T(8,128)(2,1)S(1)}, bf16[4,128,896]{2,1,0:T(8,128)(2,1)S(1)}, u32[]{:S(2)}, u32[]{:S(2)}) collective-permute-start(bf16[4,128,896]{2,1,0:T(8,128)(2,1)S(1)} %shard_map.96.held), channel_id=1, source_target_pairs={{0,32},{1,33},{2,34},{3,35},{4,36},{5,37},{6,38},{7,39},{8,40},{9,... | collective-permute-start | bytes 2752520 | tf_op jit(solution)/shard_map/ppermute | solution.py:169
  87.0 3.5 %shard_map.97.refs_0_ = bf16[4,2,128,1024]{3,2,1,0:T(8,128)(2,1)S(1)} custom-call(s32[2]{0:T(128)S(1)} %pad_add_fusion.place, bf16[4,128,896]{2,1,0:T(8,128)(2,1)S(1)} %shard_map.96.held, bf16[448,1024]{1,0:T(8,128)(2,1)S(1)} %bitcast.26, bf16[448,1024]{1,0:T(8,128)(2,1)S(1)} %bitcast.28), custom_call_target="tpu_custom_call" | custom-call | tf_op jit(solution)/shard_map/pallas_call | solution.py:125
  90.5 3.5 %shard_map.98 = bf16[4,2,128,1024]{3,2,1,0:T(8,128)(2,1)S(1)} custom-call(s32[2]{0:T(128)S(1)} %pad_add_fusion.place, bf16[4,128,896]{2,1,0:T(8,128)(2,1)S(1)} %collective-permute-done.12.held, bf16[448,1024]{1,0:T(8,128)(2,1)S(1)} %bitcast.27, bf16[448,1024]{1,0:T(8,128)(2,1)S(1)} %bitcast.29, ...), custom_call_target="tpu_custom_call", output_to_operand_aliasing={{}: (4, {})} | custom-call | tf_op jit(solution)/shard_map/pallas_call | solution.py:125
  95.3 8.2 %all-to-all-start.1 = ((bf16[32,32,1024]{2,1,0:T(8,128)(2,1)}), bf16[32,32,1024]{2,1,0:T(8,128)(2,1)}, u32[]{:S(2)}, u32[]{:S(2)}) async-start(bf16[32,32,1024]{2,1,0:T(8,128)(2,1)} %bitcast.25), calls=%async_computation.1 | async-start | bytes 4194304 | tf_op jit(solution)/shard_map/all_to_all | solution.py:165
  104.4 2.8 %collective-permute-done.14.other = bf16[4,448,128]{2,1,0:T(8,128)(2,1)S(1)} collective-permute-done((bf16[4,448,128]{2,1,0:T(8,128)(2,1)S(1)}, bf16[4,448,128]{2,1,0:T(8,128)(2,1)S(1)}, u32[]{:S(2)}, u32[]{:S(2)}) %collective-permute-start.14) | collective-permute-done | bytes 458784 | tf_op jit(solution)/shard_map/ppermute | solution.py:169
  107.3 3.7 %shard_map.100 = (bf16[448,1024]{1,0:T(8,128)(2,1)}, f32[448,1024]{1,0:T(8,128)}) custom-call(s32[2]{0:T(128)S(1)} %pad_add_fusion.place, bf16[4,4,2,128,256]{4,3,2,1,0:T(8,128)(2,1)S(1)} %bitcast.24, bf16[4,4,128,256]{3,2,1,0:T(8,128)(2,1)S(1)} %collective-permute-done.13.far, bf16[4,448,128]{2,1,0:T(8,128)(2,1)S(1)} %get-tuple-element.38.mine, ...), custom_call_target="tpu_custom_call" | custom-call | tf_op jit(solution)/shard_map/pallas_call | solution.py:229
  111.0 21.7 %all-to-all-done.1.slices = bf16[32,32,1024]{2,1,0:T(8,128)(2,1)} async-done(((bf16[32,32,1024]{2,1,0:T(8,128)(2,1)}), bf16[32,32,1024]{2,1,0:T(8,128)(2,1)}, u32[]{:S(2)}, u32[]{:S(2)}) %all-to-all-start.1) | async-done | bytes 2097184 | tf_op jit(solution)/shard_map/all_to_all | solution.py:165
  132.7 2.2 %shard_map.99 = bf16[32,1024]{1,0:T(8,128)(2,1)} custom-call(bf16[32,32,1024]{2,1,0:T(8,128)(2,1)} %all-to-all-done.1.slices), custom_call_target="tpu_custom_call" | custom-call | tf_op jit(solution)/shard_map/pallas_call | solution.py:214
  (38 shorter events, 16.2 us)
Async XLA Ops:
  0.6 9.4 %collective-permute-start.1 = (bf16[448,1024]{1,0:T(8,128)(2,1)}, bf16[448,1024]{1,0:T(8,128)(2,1)S(1)}, u32[]{:S(2)}, u32[]{:S(2)}) collective-permute-start(bf16[448,1024]{1,0:T(8,128)(2,1)} %bitcast.31), channel_id=1, source_target_pairs={{0,32},{1,33},{2,34},{3,35},{4,36},{5,37},{6,38},{7,39},{8,40},{9,... | collective-permute-start | bytes 2752520 | tf_op jit(solution)/shard_map/ppermute | solution.py:169
  1.4 8.6 %collective-permute-start = (bf16[128,256]{1,0:T(8,128)(2,1)}, bf16[128,256]{1,0:T(8,128)(2,1)S(1)}, u32[]{:S(2)}, u32[]{:S(2)}) collective-permute-start(bf16[128,256]{1,0:T(8,128)(2,1)} %param.7), channel_id=1, source_target_pairs={{0,16},{1,17},{2,18},{3,19},{4,20},{5,21},{6,22},{7,23},{8,80},{9,... | collective-permute-start | bytes 196616 | tf_op jit(solution)/shard_map/ppermute | solution.py:169
  10.0 6.8 %copy-start.5 = (bf16[448,1024]{1,0:T(8,128)(2,1)}, bf16[448,1024]{1,0:T(8,128)(2,1)S(1)}, u32[]{:S(2)}) copy-start(bf16[448,1024]{1,0:T(8,128)(2,1)S(1)} %collective-permute-done.1.other_weight) | copy-start | bytes 2752516
  10.0 5.1 %collective-permute-start.2 = (bf16[128,256]{1,0:T(8,128)(2,1)S(1)}, bf16[128,256]{1,0:T(8,128)(2,1)S(1)}, u32[]{:S(2)}, u32[]{:S(2)}) collective-permute-start(bf16[128,256]{1,0:T(8,128)(2,1)S(1)} %collective-permute-done), channel_id=1, source_target_pairs={{0,4},{1,5},{2,6},{3,7},{4,0},{5,1},{6,2},{7,3},{8,12},{9,13},{10,... | collective-permute-start | bytes 196616 | tf_op jit(solution)/shard_map/ppermute | solution.py:169
  16.8 33.9 %copy-start.4 = (bf16[1024,448]{0,1:T(8,128)(2,1)S(1)}, bf16[1024,448]{0,1:T(8,128)(2,1)}, u32[]{:S(2)}) copy-start(bf16[1024,448]{0,1:T(8,128)(2,1)} %param.12) | copy-start | bytes 2752516
  16.8 33.8 %all-to-all-start = ((bf16[16,2,128,256]{3,2,1,0:T(8,128)(2,1)}), bf16[16,2,128,256]{3,2,1,0:T(8,128)(2,1)S(1)}, u32[]{:S(2)}, u32[]{:S(2)}) async-start(bf16[16,2,128,256]{3,2,1,0:T(8,128)(2,1)} %broadcast_in_dim.2), calls=%async_computation | async-start | bytes 4194304 | tf_op jit(solution)/shard_map/all_to_all | solution.py:165
  22.3 13.9 %collective-permute-start.3 = (bf16[2,448,128]{2,1,0:T(8,128)(2,1)S(1)}, bf16[2,448,128]{2,1,0:T(8,128)(2,1)S(1)}, u32[]{:S(2)}, u32[]{:S(2)}) collective-permute-start(bf16[2,448,128]{2,1,0:T(8,128)(2,1)S(1)} %pad_maximum_fusion.zero), channel_id=1, source_target_pairs={{0,64},{1,65},{2,66},{3,67},{4,68},{5,69},{6,70},{7,71},{8,72},{9,... | collective-permute-start | bytes 688136 | tf_op jit(solution)/shard_map/ppermute | solution.py:169
  24.8 20.9 %collective-permute-start.4 = (bf16[2,448,128]{2,1,0:T(8,128)(2,1)S(1)}, bf16[2,448,128]{2,1,0:T(8,128)(2,1)}, u32[]{:S(2)}, u32[]{:S(2)}) collective-permute-start(bf16[2,448,128]{2,1,0:T(8,128)(2,1)S(1)} %pad_maximum_fusion.zero), channel_id=1, source_target_pairs={{0,128},{1,129},{2,130},{3,131},{4,132},{5,133},{6,134},{7,135},{8... | collective-permute-start | bytes 688136 | tf_op jit(solution)/shard_map/ppermute | solution.py:169
  31.0 19.7 %collective-permute-start.5 = (bf16[2,448,128]{2,1,0:T(8,128)(2,1)S(1)}, bf16[2,448,128]{2,1,0:T(8,128)(2,1)}, u32[]{:S(2)}, u32[]{:S(2)}) collective-permute-start(bf16[2,448,128]{2,1,0:T(8,128)(2,1)S(1)} %pad_maximum_fusion.zero), channel_id=1, source_target_pairs={{0,192},{1,193},{2,194},{3,195},{4,196},{5,197},{6,198},{7,199},{8... | collective-permute-start | bytes 688136 | tf_op jit(solution)/shard_map/ppermute | solution.py:169
  50.7 1.2 copy-start.6
  54.8 6.9 %collective-permute-start.6 = (bf16[448,128]{1,0:T(8,128)(2,1)S(1)}, bf16[448,128]{1,0:T(8,128)(2,1)S(1)}, u32[]{:S(2)}, u32[]{:S(2)}) collective-permute-start(bf16[448,128]{1,0:T(8,128)(2,1)S(1)} %get-tuple-element.27), channel_id=1, source_target_pairs={{0,64},{1,65},{2,66},{3,67},{4,68},{5,69},{6,70},{7,71},{8,72},{9,... | collective-permute-start | bytes 344072 | tf_op jit(solution)/shard_map/ppermute | solution.py:169
  56.1 10.7 %collective-permute-start.7 = (bf16[448,128]{1,0:T(8,128)(2,1)S(1)}, bf16[448,128]{1,0:T(8,128)(2,1)S(1)}, u32[]{:S(2)}, u32[]{:S(2)}) collective-permute-start(bf16[448,128]{1,0:T(8,128)(2,1)S(1)} %get-tuple-element.28), channel_id=1, source_target_pairs={{0,128},{1,129},{2,130},{3,131},{4,132},{5,133},{6,134},{7,135},{8... | collective-permute-start | bytes 344072 | tf_op jit(solution)/shard_map/ppermute | solution.py:169
  60.4 7.7 %collective-permute-start.8 = (bf16[448,128]{1,0:T(8,128)(2,1)S(1)}, bf16[448,128]{1,0:T(8,128)(2,1)S(1)}, u32[]{:S(2)}, u32[]{:S(2)}) collective-permute-start(bf16[448,128]{1,0:T(8,128)(2,1)S(1)} %get-tuple-element.29), channel_id=1, source_target_pairs={{0,192},{1,193},{2,194},{3,195},{4,196},{5,197},{6,198},{7,199},{8... | collective-permute-start | bytes 344072 | tf_op jit(solution)/shard_map/ppermute | solution.py:169
  68.2 18.9 %copy-start.1 = (bf16[1024,448]{0,1:T(8,128)(2,1)S(1)}, bf16[1024,448]{0,1:T(8,128)(2,1)}, u32[]{:S(2)}) copy-start(bf16[1024,448]{0,1:T(8,128)(2,1)} %param.10) | copy-start | bytes 2752516
  68.2 18.9 %copy-start.2 = (bf16[1024,448]{0,1:T(8,128)(2,1)S(1)}, bf16[1024,448]{0,1:T(8,128)(2,1)}, u32[]{:S(2)}) copy-start(bf16[1024,448]{0,1:T(8,128)(2,1)} %param.11) | copy-start | bytes 2752516
  68.2 8.7 %collective-permute-start.10 = (bf16[448,128]{1,0:T(8,128)(2,1)S(1)}, bf16[448,128]{1,0:T(8,128)(2,1)S(1)}, u32[]{:S(2)}, u32[]{:S(2)}) collective-permute-start(bf16[448,128]{1,0:T(8,128)(2,1)S(1)} %add_convert_fusion.zero), channel_id=1, source_target_pairs={{0,128},{1,129},{2,130},{3,131},{4,132},{5,133},{6,134},{7,135},{8... | collective-permute-start | bytes 344072 | tf_op jit(solution)/shard_map/ppermute | solution.py:169
  73.0 5.0 %collective-permute-start.11 = (bf16[448,128]{1,0:T(8,128)(2,1)S(1)}, bf16[448,128]{1,0:T(8,128)(2,1)S(1)}, u32[]{:S(2)}, u32[]{:S(2)}) collective-permute-start(bf16[448,128]{1,0:T(8,128)(2,1)S(1)} %add_convert_fusion.zero), channel_id=1, source_target_pairs={{0,192},{1,193},{2,194},{3,195},{4,196},{5,197},{6,198},{7,199},{8... | collective-permute-start | bytes 344072 | tf_op jit(solution)/shard_map/ppermute | solution.py:169
  73.5 8.4 %collective-permute-start.9 = (bf16[448,128]{1,0:T(8,128)(2,1)S(1)}, bf16[448,128]{1,0:T(8,128)(2,1)S(1)}, u32[]{:S(2)}, u32[]{:S(2)}) collective-permute-start(bf16[448,128]{1,0:T(8,128)(2,1)S(1)} %add_convert_fusion.zero), channel_id=1, source_target_pairs={{0,64},{1,65},{2,66},{3,67},{4,68},{5,69},{6,70},{7,71},{8,72},{9,... | collective-permute-start | bytes 344072 | tf_op jit(solution)/shard_map/ppermute | solution.py:169
  82.7 7.8 %collective-permute-start.12 = (bf16[4,128,896]{2,1,0:T(8,128)(2,1)S(1)}, bf16[4,128,896]{2,1,0:T(8,128)(2,1)S(1)}, u32[]{:S(2)}, u32[]{:S(2)}) collective-permute-start(bf16[4,128,896]{2,1,0:T(8,128)(2,1)S(1)} %shard_map.96.held), channel_id=1, source_target_pairs={{0,32},{1,33},{2,34},{3,35},{4,36},{5,37},{6,38},{7,39},{8,40},{9,... | collective-permute-start | bytes 2752520 | tf_op jit(solution)/shard_map/ppermute | solution.py:169
  94.0 1.3 copy-start
  95.3 37.3 %all-to-all-start.1 = ((bf16[32,32,1024]{2,1,0:T(8,128)(2,1)}), bf16[32,32,1024]{2,1,0:T(8,128)(2,1)}, u32[]{:S(2)}, u32[]{:S(2)}) async-start(bf16[32,32,1024]{2,1,0:T(8,128)(2,1)} %bitcast.25), calls=%async_computation.1 | async-start | bytes 4194304 | tf_op jit(solution)/shard_map/all_to_all | solution.py:165
  103.5 3.7 %copy-start.3 = (f32[1024,448]{0,1:T(8,128)S(1)}, f32[1024,448]{0,1:T(8,128)}, u32[]{:S(2)}) copy-start(f32[1024,448]{0,1:T(8,128)} %param.13) | copy-start | bytes 5505028
  103.6 3.6 %collective-permute-start.13 = (bf16[4,4,128,256]{3,2,1,0:T(8,128)(2,1)S(1)}, bf16[4,4,128,256]{3,2,1,0:T(8,128)(2,1)S(1)}, u32[]{:S(2)}, u32[]{:S(2)}) collective-permute-start(bf16[4,4,128,256]{3,2,1,0:T(8,128)(2,1)S(1)} %dynamic-slice_bitcast_fusion), channel_id=1, source_target_pairs={{0,32},{1,33},{2,34},{3,35},{4,36},{5,37},{6,38},{7,39},{8,40},{9,... | collective-permute-start | bytes 3145736 | tf_op jit(solution)/shard_map/ppermute | solution.py:169
  104.3 2.9 %collective-permute-start.14 = (bf16[4,448,128]{2,1,0:T(8,128)(2,1)S(1)}, bf16[4,448,128]{2,1,0:T(8,128)(2,1)S(1)}, u32[]{:S(2)}, u32[]{:S(2)}) collective-permute-start(bf16[4,448,128]{2,1,0:T(8,128)(2,1)S(1)} %get-tuple-element.38.mine), channel_id=1, source_target_pairs={{0,32},{1,33},{2,34},{3,35},{4,36},{5,37},{6,38},{7,39},{8,40},{9,... | collective-permute-start | bytes 1376264 | tf_op jit(solution)/shard_map/ppermute | solution.py:169
